TPU v7x, 512 devices: a whole 4x8x8 slice. The times are simulated.
512 devices in a mesh: rows: 128 (over z_hi, x, y), rep: 4 (over z_lo, core).
Axes of the slice: x: 4, y: 8, z: 8 (z_hi: 4, z_lo: 2; z = z_hi * 2 + z_lo), core: 2. Of those that a mesh axis runs over, the one named last changes fastest.
Arguments:
- features: bfloat16 [16384, 128], P('rows', 'rep'), may hold values from -6 to 6
- weight: bfloat16 [128, 128], replicated, may hold values from -0.5 to 0.5
- tiles: bfloat16 [128, 16, 128, 128], P('rows'), may hold values from -0.1875 to 0.1875
- tile_rows: int32 [128, 16], P('rows'), may hold values from 0 to 127
- tile_live: int32 [128, 16], P('rows'), may hold values from 0 to 1, as said below
- pos_partner: int32 [16384, 8], P('rows'), may hold values from 0 to 16383
- neg_partner: int32 [16384, 8], P('rows'), may hold values from 0 to 16383
Outputs:
- embedding: bfloat16 [16384, 128], P('rows', 'rep')
- grad_weight: float32 [128, 128], P('rep')
- grad_features: bfloat16 [16384, 128], P('rows', 'rep')
Inputs may be any that keep to these rules, and one draw needn't show every extreme that they name: `tile_live`: the share of live slots differs between column blocks.
All inputs are finite; a program needn't handle non-finite values.
Results may differ from a plain program's by a relative error of at most 0.008.
Values may be sent and summed in bfloat16 or wider, within the bound.
No kernel may reach another device: no remote copies, remote signals or barrier semaphores. Data moves between devices by JAX's collectives and lax.ppermute only.
A program may use at most 64 MiB of HBM per device.

v0:
```python
import math

import jax
import jax.numpy as jnp
from jax import lax
from jax.sharding import PartitionSpec as P

F = 128


def on_device(features, weight, tiles, tile_rows, tile_live, pos_partner, neg_partner):
    block_size = tiles.shape[2]
    part_width = features.shape[1]
    block_count = lax.axis_size("rows")
    node_count = block_count * block_size
    col_start = lax.axis_index("rep") * part_width
    tile_set = tiles[0]
    rows_set = tile_rows[0]
    live_flags = tile_live[0].astype(jnp.float32)
    high = lax.Precision.HIGHEST
    weight_cols = lax.dynamic_slice_in_dim(weight, col_start, part_width, 1)
    weight_rows = lax.dynamic_slice_in_dim(weight, col_start, part_width, 0)
    products = jnp.einsum("kij,jf->kif", tile_set, features, preferred_element_type=jnp.float32)
    weighted = products * live_flags[:, None, None]
    partial_value = (
        jnp.zeros((block_count, block_size, part_width), jnp.float32).at[rows_set].add(weighted)
    )
    summed = lax.psum_scatter(
        partial_value.reshape(block_count, block_size * part_width),
        "rows",
        scatter_dimension=0,
        tiled=True,
    )
    agg_own = summed.reshape(block_size, part_width).astype(jnp.bfloat16)
    agg_full = lax.all_gather(agg_own, "rep", axis=1, tiled=True)
    embedding = jnp.dot(agg_full, weight_cols, preferred_element_type=jnp.float32).astype(
        jnp.bfloat16
    )
    slab_rows = lax.all_gather(embedding, "rows", axis=0, tiled=True)
    pos_rows = slab_rows[pos_partner]
    neg_rows = slab_rows[neg_partner]
    pos_part = jnp.einsum("nf,nkf->nk", embedding, pos_rows, preferred_element_type=jnp.float32)
    neg_part = jnp.einsum("nf,nkf->nk", embedding, neg_rows, preferred_element_type=jnp.float32)
    pos_logit, neg_logit = lax.psum((pos_part, neg_part), "rep")
    pair_count = pos_partner.shape[1]
    pos_coeffs = (jax.nn.sigmoid(pos_logit / math.sqrt(F)) - 1.0) / pair_count
    neg_coeffs = jax.nn.sigmoid(neg_logit / math.sqrt(F)) / pair_count
    direct = jnp.einsum("nk,nkf->nf", pos_coeffs, pos_rows.astype(jnp.float32), precision=high)
    direct = direct + jnp.einsum(
        "nk,nkf->nf", neg_coeffs, neg_rows.astype(jnp.float32), precision=high
    )
    wide_embed = embedding.astype(jnp.float32)
    contrib = jnp.zeros((node_count, part_width), jnp.float32)
    for coeffs, partners in ((pos_coeffs, pos_partner), (neg_coeffs, neg_partner)):
        pair_terms = (coeffs[:, :, None] * wide_embed[:, None, :]).reshape(-1, part_width)
        contrib = contrib.at[partners.reshape(-1)].add(pair_terms)
    incoming = lax.psum_scatter(contrib, "rows", scatter_dimension=0, tiled=True)
    grad_own = (direct + incoming).astype(jnp.bfloat16)
    grad_full_own = lax.all_gather(grad_own, "rep", axis=1, tiled=True)
    grad_agg_own = jnp.dot(grad_full_own, weight_rows.T, preferred_element_type=jnp.float32).astype(
        jnp.bfloat16
    )
    grad_agg_slab = lax.all_gather(grad_agg_own, "rows", axis=0, tiled=True)
    weight_terms = jnp.dot(agg_own.T, grad_full_own, preferred_element_type=jnp.float32)
    grad_weight = lax.psum(weight_terms, "rows") / math.sqrt(node_count)
    grad_blocks = grad_agg_slab.reshape(block_count, block_size, part_width)
    selected = grad_blocks[rows_set] * tile_live[0].astype(jnp.bfloat16)[:, None, None]
    feature_sum = jnp.einsum("kij,kif->jf", tile_set, selected, preferred_element_type=jnp.float32)
    return (embedding, grad_weight, feature_sum.astype(jnp.bfloat16))


def solution(mesh):
    return jax.shard_map(
        on_device,
        mesh=mesh,
        in_specs=(
            P("rows", "rep"),
            P(),
            P("rows", None, None, None),
            P("rows", None),
            P("rows", None),
            P("rows", None),
            P("rows", None),
        ),
        out_specs=(P("rows", "rep"), P("rep", None), P("rows", "rep")),
        check_vma=False,
    )
```

profile of v0, /device:TPU:64, one launch (start us, length us, event | category | flops | bytes accessed | tf_op | source)
XLA Modules:
  0.0 2471.2 jit_solution(18135945696206819045)
XLA Ops:
  7.2 0.0 copy-start
  7.2 0.0 copy-start.1
  7.2 0.0 copy-start.2
  7.2 0.0 copy-start.3
  7.2 0.0 all-gather.3.cloned.1.call-start
  7.3 0.7 fusion.21
  8.0 0.7 convert_bitcast_fusion
  8.7 0.0 copy-done
  8.7 1.0 convolution_multiply_fusion
  9.7 0.3 broadcast_in_dim.8
  9.9 1.2 scatter_fusion
  11.2 2.3 copy.42
  13.5 775.6 %all-reduce.3 = bf16[128,4096]{0,1:T(8,128)(2,1)S(1)} all-reduce(f32[128,4096]{0,1:T(8,128)} %bitcast.66), channel_id=2, replica_groups=mesh['rows'=128,'rep'=4] {'rows'}, use_global_device_ids=true, to_apply=%region_1.0.clone | all-reduce | flops 524288 | bytes 3145728
  789.1 1.3 dynamic-slice
  790.3 1.4 fusion.4
  791.7 0.1 convert_element_type.49
  791.8 0.1 copy.43
  791.9 5.2 all_gather.12
  797.1 0.0 copy-done.1
  797.1 0.9 convolution_convert_fusion.1
  797.9 0.0 all-gather.3.cloned.1.call-update
  797.9 0.0 reduce-scatter.3.cloned.1.call-start
  798.0 0.8 copy.71
  798.8 0.0 copy-done.2
  798.8 0.1 copy.51
  798.9 0.1 copy.46
  799.0 0.1 reshape.141
  799.1 0.0 copy-done.3
  799.1 0.1 copy.48
  799.2 0.1 copy.44
  799.3 0.1 reshape.133
  799.4 0.1 reshape.128
  799.5 0.1 reshape.129
  799.7 96.7 %all-gather.3.cloned.1.call-done = bf16[16384,32]{0,1:T(8,128)(2,1)} async-done(((bf16[128,32]{0,1:T(8,128)(2,1)}), bf16[16384,32]{0,1:T(8,128)(2,1)}) %all-gather.3.cloned.1.call-update) | async-done | bytes 1048592 | tf_op jit(solution)/shard_map/all_gather | solution.py:39
  896.4 4.6 copy.45
  900.9 5.6 gather_fusion.1
  906.6 5.6 gather_fusion
  912.2 0.4 multiply_reduce_fusion
  912.6 0.1 copy.59
  912.6 7.5 all-reduce.1
  920.2 0.1 copy.52
  920.3 0.1 mul.59
  920.4 0.1 copy.49
  920.5 0.1 mul.54
  920.6 10.3 scatter_custom_fusion.1
  930.9 12.5 scatter_custom_fusion.2
  943.4 0.0 reduce-scatter.3.cloned.1.call-update
  943.4 0.0 all-gather.5.cloned.1.call-start
  943.5 0.1 copy.67
  943.6 0.1 copy.60
  943.7 0.6 fusion.8
  944.3 0.6 fusion.10
  944.8 769.9 %reduce-scatter.3.cloned.1.call-done = f32[128,32]{1,0:T(8,128)} async-done(((f32[16384,32]{1,0:T(8,128)}), f32[128,32]{1,0:T(8,128)}) %reduce-scatter.3.cloned.1.call-update) | async-done | bytes 16400 | tf_op jit(solution)/shard_map/reduce_scatter | solution.py:57
  1714.7 0.9 add_convert_fusion
  1715.5 0.1 copy.53
  1715.6 5.2 all_gather.14
  1720.8 0.7 convolution_convert_fusion
  1721.5 0.0 all-gather.5.cloned.1.call-update
  1721.6 0.2 fusion.26
  1721.7 739.5 %psum.23 = f32[32,128]{1,0:T(8,128)S(1)} all-reduce(f32[32,128]{1,0:T(8,128)S(1)} %fusion.26), channel_id=1, replica_groups=mesh['rows'=128,'rep'=4] {'rows'}, use_global_device_ids=true, to_apply=%region_7.0 | all-reduce | flops 4096 | bytes 32768 | tf_op jit(solution)/shard_map/psum | solution.py:65
  2461.2 0.6 broadcast_multiply_fusion
  2461.8 1.4 copy_bitcast_fusion
  2463.2 0.6 gather_fusion.2
  2463.8 0.9 fusion.3
  (10 shorter events, 0.1 us)
Async XLA Ops:
  7.2 1.5 copy-start
  7.2 789.9 %copy-start.1 = (bf16[128,128]{1,0:T(8,128)(2,1)S(1)}, bf16[128,128]{1,0:T(8,128)(2,1)}, u32[]{:S(2)}) copy-start(bf16[128,128]{1,0:T(8,128)(2,1)} %param.8) | copy-start | bytes 98308
  7.2 791.6 %copy-start.2 = (s32[128,8]{0,1:T(8,128)S(1)}, s32[128,8]{0,1:T(8,128)}, u32[]{:S(2)}) copy-start(s32[128,8]{0,1:T(8,128)} %param.13) | copy-start | bytes 12292
  7.2 791.9 %copy-start.3 = (s32[128,8]{0,1:T(8,128)S(1)}, s32[128,8]{0,1:T(8,128)}, u32[]{:S(2)}) copy-start(s32[128,8]{0,1:T(8,128)} %param.12) | copy-start | bytes 12292
  7.2 889.2 %all-gather.3.cloned.1.call-start = ((), (), s32[]{:S(2)}) async-start(), calls=%async_computation.1 | async-start | bytes 1056768 | tf_op jit(solution)/shard_map/all_gather | solution.py:39
  797.9 916.7 %reduce-scatter.3.cloned.1.call-start = ((), (), s32[]{:S(2)}) async-start(), calls=%async_computation.2 | async-start | bytes 8454144 | tf_op jit(solution)/shard_map/reduce_scatter | solution.py:57
  943.4 1518.4 %all-gather.5.cloned.1.call-start = ((), (), s32[]{:S(2)}) async-start(), calls=%async_computation.3 | async-start | bytes 1056768 | tf_op jit(solution)/shard_map/all_gather | solution.py:63
Sparse Core Ops, SparseCore 0:
  798.1 98.2 all-gather.2
  943.6 771.0 reduce-scatter.2
  1721.7 98.9 all-gather.4
where the time goes:
time: 2470 us
  blocking collectives  1530 us (62%)
  waiting for transfers between devices  867 us (35%)
  other arithmetic  27.3 us (1%)
  local copies, waits for them, and re-layouts  25.5 us (1%)
    unnamed x1, blocking collectives  776 us
    reduce_scatter x1, waiting for transfers between devices, on_device(): lax.psum_scatter(contrib, 'rows', scatter_dimension=0, tiled=True)  770 us
    psum x1, blocking collectives, on_device(): grad_weight = lax.psum(weight_terms, 'rows') / math.sqrt(node_count)  739 us
    all_gather x1, waiting for transfers between devices, on_device(): slab_rows = lax.all_gather(embedding, 'rows', axis=0, tiled=True)  96.7 us
  transfers between devices with their start and end apart: 3, of which 2 were waited for; matrix products, arithmetic and copies ran while one was open for 0% of the time, Pallas kernels for 0%

commit v1 on v0

v1 whole, which is shorter than its diff:
```python
import functools
import math

import jax
import jax.numpy as jnp
from jax import lax
from jax.experimental import pallas as pl
from jax.experimental.pallas import tpu as pltpu
from jax.sharding import Mesh, PartitionSpec as P

BF = jnp.bfloat16
F32 = jnp.float32
B = 128
F = 128
W32 = 32
ROWS = ("zh", "x", "y")
REP = ("zl", "core")
PARAMS = pltpu.CompilerParams(vmem_limit_bytes=40 * 1024 * 1024)
VMEM = pl.BlockSpec(memory_space=pltpu.VMEM)
SMEM = pl.BlockSpec(memory_space=pltpu.SMEM)


def tn(a, b):
    return lax.dot_general(a, b, (((0,), (0,)), ((), ())), preferred_element_type=F32)


def nt(a, b):
    return lax.dot_general(a, b, (((1,), (1,)), ((), ())), preferred_element_type=F32)


def nn(a, b):
    return lax.dot_general(a, b, (((1,), (0,)), ((), ())), preferred_element_type=F32)


def call(body, in_specs, out_shape, scratch=(), flops=1000000, nbytes=1000000):
    multi = isinstance(out_shape, (tuple, list))
    return pl.pallas_call(
        body,
        out_shape=out_shape,
        in_specs=in_specs,
        out_specs=[VMEM] * len(out_shape) if multi else VMEM,
        scratch_shapes=list(scratch),
        compiler_params=PARAMS,
        cost_estimate=pl.CostEstimate(flops=flops, bytes_accessed=nbytes, transcendentals=0),
    )


def products_kernel(xy, rows_ref, live_ref, feat_ref, tiles_ref, out_ref, acc):
    acc[...] = jnp.zeros_like(acc)
    slots = tiles_ref.shape[1]
    for s in range(slots):
        prod = nt(feat_ref[...], tiles_ref[0, s]) * live_ref[0, s].astype(F32)
        row = rows_ref[0, s]
        acc[lax.rem(row, xy), lax.div(row, xy)] += prod
    out_ref[...] = acc[...].astype(BF)


def direct_kernel(xy, place_ref, pos_ref, neg_ref, cpos_ref, ctot_ref, ids):
    pk = pos_ref.shape[1]
    for k in range(pk):
        ids[k] = jnp.broadcast_to(pos_ref[:, k : k + 1], (B, B))
        ids[pk + k] = jnp.broadcast_to(neg_ref[:, k : k + 1], (B, B))
    lane = lax.broadcasted_iota(jnp.int32, (B, B), 1)
    base = place_ref[0] * xy * B

    def step(mb, carry):
        want = lane + (base + mb * B)
        cpos = jnp.zeros((B, B), F32)
        cneg = jnp.zeros((B, B), F32)
        for k in range(pk):
            cpos = jnp.where(ids[k] == want, cpos + 1.0, cpos)
            cneg = jnp.where(ids[pk + k] == want, cneg + 1.0, cneg)
        cpos_ref[mb] = cpos.astype(BF)
        ctot_ref[mb] = (cpos + cneg).astype(BF)
        return carry

    lax.fori_loop(0, xy, step, 0)


def partial_kernel(recv_ref, pos_ref, neg_ref, out_ref):
    out_ref[0:B, :] = jnp.sum(recv_ref[...].astype(F32), axis=0).astype(BF)
    pk = pos_ref.shape[0]
    table = jnp.concatenate([pos_ref[...], neg_ref[...]], axis=0)
    block = lax.shift_right_logical(table, 7)
    out_ref[B : B + 2 * pk, :] = block.astype(F32).astype(BF)
    out_ref[B + 2 * pk :, :] = (table - block * B).astype(F32).astype(BF)


def embed_kernel(q, place_ref, got_ref, w_ref, eown_ref, embt_ref, aggt_ref, send_ref, agg_s, et_s):
    part, plane = place_ref[0], place_ref[1]

    def block_agg(b):
        first = pl.multiple_of(b * W32, W32)
        for p in range(q):
            total = got_ref[p, pl.ds(first, W32), :].astype(F32)
            for z in range(1, q):
                total = total + got_ref[z * q + p, pl.ds(first, W32), :].astype(F32)
            agg_s[p * W32 : (p + 1) * W32, :] = total.astype(BF)

    mine = pl.ds(pl.multiple_of(part * W32, W32), W32)
    block_agg(part)
    send = tn(agg_s[...], w_ref[...]).astype(BF)
    table = got_ref[part * q, B:, :]
    for d in range(send_ref.shape[0]):
        send_ref[d, 0:B, :] = send
        send_ref[d, B:, :] = table
    block_agg(plane)
    et = tn(w_ref[...], agg_s[...])
    et_s[...] = et.astype(BF)
    eown_ref[...] = et.T.astype(BF)
    embt_ref[...] = et_s[mine, :]
    aggt_ref[...] = agg_s[mine, :]


def decoder_kernel(group, place_ref, got_ref, eown_ref, cpos_ref, ctot_ref, out_ref):
    blocks = got_ref.shape[0]
    slots = (got_ref.shape[1] - B) // 2
    pk = slots // 2
    own = place_ref[2].astype(F32)
    sub = lax.broadcasted_iota(jnp.int32, (B, B), 0).astype(F32)
    eown = eown_ref[...]
    scale = 1.0 / math.sqrt(F)

    def step(i, acc):
        terms = []
        first = i * group
        em = got_ref[pl.ds(first, group), 0:B, :].reshape(group * B, F)
        logits = nt(eown, em)
        for j in range(group):
            mb = first + j
            tab = got_ref[mb, B:, :].astype(F32)
            place = jnp.where(tab[:slots] == own, tab[slots:], -1.0)
            cpos = cpos_ref[mb].astype(F32)
            ctot = ctot_ref[mb].astype(F32)
            ipos = jnp.zeros((B, B), F32)
            ineg = jnp.zeros((B, B), F32)
            for k in range(pk):
                ipos = jnp.where(sub == place[k : k + 1], ipos + 1.0, ipos)
                ineg = jnp.where(sub == place[pk + k : pk + k + 1], ineg + 1.0, ineg)
            sig = jax.nn.sigmoid(logits[:, j * B : (j + 1) * B] * scale)
            coef = (ctot + ipos + ineg) * sig - (cpos + ipos)
            terms.append(coef)
        coefs = jnp.concatenate(terms, axis=1)
        high = coefs.astype(BF)
        low = (coefs - high.astype(F32)).astype(BF)
        return acc + nn(high, em) + nn(low, em)

    acc = lax.fori_loop(0, blocks // group, step, jnp.zeros((B, F), F32))
    out_ref[...] = acc * (1.0 / pk)


def grads_kernel(q, place_ref, got_ref, w_ref, aggt_ref, out_ref):
    total = got_ref[0:B, :]
    for p in range(1, q):
        total = total + got_ref[p * B : (p + 1) * B, :]
    grad = total.astype(BF)
    wrows = w_ref[pl.ds(pl.multiple_of(place_ref[0] * W32, W32), W32), :]
    grad_agg = nt(wrows, grad).astype(BF)
    terms = nn(aggt_ref[...], grad)
    high = terms.astype(BF)
    low = (terms - high.astype(F32)).astype(BF)
    for d in range(out_ref.shape[0]):
        out_ref[d, 0:W32, :] = grad_agg
        out_ref[d, W32 : 2 * W32, :] = high
        out_ref[d, 2 * W32 :, :] = low


def merge_kernel(got_ref, out_ref):
    ny = got_ref.shape[0]
    terms = jnp.sum(
        got_ref[:, W32 : 2 * W32, :].astype(F32) + got_ref[:, 2 * W32 :, :].astype(F32), axis=0
    )
    high = terms.astype(BF)
    low = (terms - high.astype(F32)).astype(BF)
    blocks = got_ref[:, 0:W32, :].reshape(ny * W32, B)
    for d in range(out_ref.shape[0]):
        out_ref[d, 0 : ny * W32, :] = blocks
        out_ref[d, ny * W32 : (ny + 1) * W32, :] = high
        out_ref[d, (ny + 1) * W32 :, :] = low


def features_kernel(ny, node_count, rows_ref, live_ref, got_ref, tiles_ref, gft_ref, gw_ref):
    slots = tiles_ref.shape[1]
    total = jnp.zeros((W32, B), F32)
    for s in range(slots):
        row = rows_ref[0, s]
        first = pl.multiple_of(lax.rem(row, ny) * W32, W32)
        block = got_ref[lax.div(row, ny), pl.ds(first, W32), :]
        block = (block.astype(F32) * live_ref[0, s].astype(F32)).astype(BF)
        total = total + nn(block, tiles_ref[0, s])
    gft_ref[...] = total.astype(BF)
    first = ny * W32
    terms = got_ref[:, first : first + W32, :].astype(F32) + got_ref[:, first + W32 :, :].astype(F32)
    gw_ref[...] = jnp.sum(terms, axis=0) * (1.0 / math.sqrt(node_count))


def on_device(features, weight, tiles, tile_rows, tile_live, pos_partner, neg_partner):
    q = lax.axis_size("zh")
    nx, ny = lax.axis_size("x"), lax.axis_size("y")
    xy = nx * ny
    node_count = q * xy * B
    plane, part = lax.axis_index("zh"), lax.axis_index(REP)
    own_block = lax.axis_index(ROWS)
    place = jnp.stack([part, plane, own_block]).astype(jnp.int32)
    shape = jax.ShapeDtypeStruct
    pos_t, neg_t = pos_partner.T, neg_partner.T
    slots = 2 * pos_partner.shape[1]

    sent = call(
        functools.partial(products_kernel, xy),
        [SMEM, SMEM, VMEM, VMEM],
        shape((xy, q, W32, B), BF),
        [pltpu.VMEM((xy, q, W32, B), F32)],
    )(tile_rows, tile_live, features.T, tiles)
    recv = lax.all_to_all(sent.reshape(xy, q * W32, B), ("x", "y"), 0, 0, tiled=True)

    cpos, ctot = call(
        functools.partial(direct_kernel, xy),
        [SMEM, VMEM, VMEM],
        (shape((xy, B, B), BF), shape((xy, B, B), BF)),
        [pltpu.VMEM((slots, B, B), jnp.int32)],
        flops=100000000,
    )(place, pos_partner, neg_partner)

    partial_value = call(partial_kernel, [VMEM, VMEM, VMEM], shape((q * W32 + 2 * slots, B), BF))(
        recv, pos_t, neg_t
    )
    height = partial_value.shape[0]
    gathered = lax.all_gather(partial_value, ("zh",) + REP, axis=0)

    eown, emb_t, agg_t, slab_part = call(
        functools.partial(embed_kernel, q),
        [SMEM, VMEM, VMEM],
        (shape((B, F), BF), shape((W32, B), BF), shape((W32, B), BF), shape((xy, height, B), BF)),
        [pltpu.VMEM((F, B), BF), pltpu.VMEM((F, B), BF)],
    )(place, gathered, weight)
    slab = lax.all_to_all(slab_part, ("x", "y"), 0, 0, tiled=True)

    group = math.gcd(xy, 4)
    grad_part = call(
        functools.partial(decoder_kernel, group),
        [SMEM, VMEM, VMEM, VMEM, VMEM],
        shape((B, F), F32),
    )(place, slab, eown, cpos, ctot)
    grad_parts = lax.all_gather(grad_part, REP, axis=0, tiled=True)

    line_part = call(
        functools.partial(grads_kernel, q),
        [SMEM, VMEM, VMEM, VMEM],
        shape((ny, 3 * W32, B), BF),
    )(place, grad_parts, weight, agg_t)
    line = lax.all_to_all(line_part, "y", 0, 0, tiled=True)
    rest_part = call(merge_kernel, [VMEM], shape((q * nx, (ny + 2) * W32, B), BF))(line)
    rest = lax.all_to_all(rest_part, ("zh", "x"), 0, 0, tiled=True)

    gf_t, grad_weight = call(
        functools.partial(features_kernel, ny, node_count),
        [SMEM, SMEM, VMEM, VMEM],
        (shape((W32, B), BF), shape((W32, F), F32)),
    )(tile_rows, tile_live, rest, tiles)
    return (emb_t.T, grad_weight, gf_t.T)


def sharded(mesh):
    return jax.shard_map(
        on_device,
        mesh=mesh,
        in_specs=(
            P(ROWS, REP),
            P(),
            P(ROWS, None, None, None),
            P(ROWS, None),
            P(ROWS, None),
            P(ROWS, None),
            P(ROWS, None),
        ),
        out_specs=(P(ROWS, REP), P(REP, None), P(ROWS, REP)),
        check_vma=False,
    )


def solution(mesh):
    rows = mesh.shape["rows"]
    parts = mesh.devices.reshape(4, 4, rows // 16, 2, 2)
    return sharded(Mesh(parts, ("zh", "x", "y", "zl", "core")))
```

time: 2470 us -> 178 us (0.07)
  the two profiles are of different devices: /device:TPU:64 before, /device:TPU:1 now
where the time goes in v1:
time: 178 us; the launch traced here: 177 us
  blocking collectives  88.8 us (50%)
  waiting for transfers between devices  50.3 us (28%)
  Pallas kernels  17.3 us (10%)
  starting transfers between devices  15.4 us (9%)
  local copies, waits for them, and re-layouts  4.73 us (3%)
    all_to_all x1, blocking collectives, on_device(): rest = lax.all_to_all(rest_part, ('zh', 'x'), 0, 0, tiled=True)  37.1 us
    all_gather x1, blocking collectives, on_device(): gathered = lax.all_gather(partial_value, ('zh',) + REP, axis=0)  29.8 us
    all_to_all x1, waiting for transfers between devices, on_device(): slab = lax.all_to_all(slab_part, ('x', 'y'), 0, 0, tiled=True)  25.7 us
    all_to_all x1, waiting for transfers between devices, on_device(): lax.all_to_all(sent.reshape(xy, q * W32, B), ('x', 'y'), 0, 0, tiled=True)  24.5 us
    all_to_all x1, blocking collectives, on_device(): line = lax.all_to_all(line_part, 'y', 0, 0, tiled=True)  13.2 us
    all_to_all x1, starting transfers between devices, on_device(): lax.all_to_all(sent.reshape(xy, q * W32, B), ('x', 'y'), 0, 0, tiled=True)  10.6 us
    all_gather x1, blocking collectives, on_device(): grad_parts = lax.all_gather(grad_part, REP, axis=0, tiled=True)  8.78 us
    pallas_call x1, Pallas kernels, on_device(): call(functools.partial(decoder_kernel, group), [SMEM, VMEM, VMEM, VMEM, V...  6.47 us
  transfers between devices with their start and end apart: 2, of which 2 were waited for; matrix products, arithmetic and copies ran while one was open for 1% of the time, Pallas kernels for 2%

profile of v1, /device:TPU:1, one launch (start us, length us, event | category | flops | bytes accessed | tf_op | source)
XLA Modules:
  0.0 177.3 jit_solution(8477402856999333523)
XLA Ops:
  0.6 0.0 copy-start
  0.6 1.0 copy-done
  1.7 0.0 copy-start.6
  1.7 0.7 copy-done.6
  2.4 0.0 copy-start.7
  2.4 0.7 copy-done.7
  3.0 0.0 copy-start.9
  3.0 0.7 copy-done.9
  3.7 2.0 %shard_map.94 = bf16[32,4,32,128]{3,2,1,0:T(8,128)(2,1)} custom-call(s32[1,16]{1,0:T(1,128)S(1)} %copy-done.7, s32[1,16]{1,0:T(1,128)S(1)} %copy-done.9, bf16[32,128]{1,0:T(8,128)(2,1)S(1)} %bitcast.13, bf16[1,16,128,128]{3,2,1,0:T(8,128)(2,1)S(1)} %copy-done), custom_call_target="tpu_custom_call" | custom-call | flops 1000000 | bytes 1000000 | tf_op jit(solution)/shard_map/pallas_call | solution.py:209
  5.7 0.0 copy-start.4
  5.7 0.0 copy-start.5
  5.7 10.6 %all-to-all-start = ((bf16[32,128,128]{2,1,0:T(8,128)(2,1)}), bf16[32,128,128]{2,1,0:T(8,128)(2,1)S(1)}, u32[]{:S(2)}, u32[]{:S(2)}) async-start(bf16[32,128,128]{2,1,0:T(8,128)(2,1)} %bitcast.4), calls=%async_computation | async-start | bytes 2097152 | tf_op jit(solution)/shard_map/all_to_all | solution.py:215
  16.4 0.0 copy-start.2
  16.4 0.1 pad_add_fusion.place_ref
  16.4 24.5 %all-to-all-done.recv_ref = bf16[32,128,128]{2,1,0:T(8,128)(2,1)S(1)} async-done(((bf16[32,128,128]{2,1,0:T(8,128)(2,1)}), bf16[32,128,128]{2,1,0:T(8,128)(2,1)S(1)}, u32[]{:S(2)}, u32[]{:S(2)}) %all-to-all-start) | async-done | bytes 1048608 | tf_op jit(solution)/shard_map/all_to_all | solution.py:215
  41.0 0.0 copy-done.4
  41.0 0.0 copy-done.5
  41.0 0.1 shard_map.95
  41.1 29.8 %all-gather = bf16[2560,128]{1,0:T(8,128)(2,1)S(1)} all-gather(bf16[160,128]{1,0:T(8,128)(2,1)S(1)} %shard_map.95), channel_id=2, replica_groups=mesh['zh'=4,'x'=4,'y'=8,'zl'=2,'core'=2] {'zh','zl','core'}, dimensions={0}, use_global_device_ids=true | all-gather | bytes 696320 | tf_op jit(solution)/shard_map/all_gather | solution.py:229
  70.9 0.0 copy-done.2
  70.9 1.9 %shard_map.96 = (bf16[128,128]{1,0:T(8,128)(2,1)S(1)}, bf16[32,128]{1,0:T(8,128)(2,1)}, bf16[32,128]{1,0:T(8,128)(2,1)S(1)}, bf16[32,160,128]{2,1,0:T(8,128)(2,1)}) custom-call(s32[3]{0:T(128)S(1)} %pad_add_fusion.place_ref, bf16[16,160,128]{2,1,0:T(8,128)(2,1)S(1)} %bitcast.10, bf16[128,128]{1,0:T(8,128)(2,1)S(1)} %copy-done.2), custom_call_target="tpu_custom_call" | custom-call | flops 1000000 | bytes 1000000 | tf_op jit(solution)/shard_map/pallas_call | solution.py:231
  72.8 4.8 %all-to-all-start.1 = ((bf16[32,160,128]{2,1,0:T(8,128)(2,1)}), bf16[32,160,128]{2,1,0:T(8,128)(2,1)S(1)}, u32[]{:S(2)}, u32[]{:S(2)}) async-start(bf16[32,160,128]{2,1,0:T(8,128)(2,1)} %get-tuple-element.12), calls=%async_computation.1 | async-start | bytes 2621440 | tf_op jit(solution)/shard_map/all_to_all | solution.py:237
  77.6 0.1 copy.10.pos_ref
  77.7 0.7 copy.11.neg_ref
  78.4 0.0 copy-start.3
  78.4 0.8 copy-done.3
  79.3 4.4 %shard_map.97 = (bf16[32,128,128]{2,1,0:T(8,128)(2,1)S(1)}, bf16[32,128,128]{2,1,0:T(8,128)(2,1)S(1)}) custom-call(s32[3]{0:T(128)S(1)} %pad_add_fusion.place_ref, s32[128,8]{1,0:T(8,128)S(1)} %copy.10.pos_ref, s32[128,8]{1,0:T(8,128)S(1)} %copy-done.3), custom_call_target="tpu_custom_call" | custom-call | flops 100000000 | bytes 1000000 | tf_op jit(solution)/shard_map/pallas_call | solution.py:217
  83.7 25.7 %all-to-all-done.1.got_ref = bf16[32,160,128]{2,1,0:T(8,128)(2,1)S(1)} async-done(((bf16[32,160,128]{2,1,0:T(8,128)(2,1)}), bf16[32,160,128]{2,1,0:T(8,128)(2,1)S(1)}, u32[]{:S(2)}, u32[]{:S(2)}) %all-to-all-start.1) | async-done | bytes 1310752 | tf_op jit(solution)/shard_map/all_to_all | solution.py:237
  109.4 6.5 %shard_map.98 = f32[128,128]{1,0:T(8,128)S(1)} custom-call(s32[3]{0:T(128)S(1)} %pad_add_fusion.place_ref, bf16[32,160,128]{2,1,0:T(8,128)(2,1)S(1)} %all-to-all-done.1.got_ref, bf16[128,128]{1,0:T(8,128)(2,1)S(1)} %get-tuple-element.13.eown_ref, bf16[32,128,128]{2,1,0:T(8,128)(2,1)S(1)} %get-tuple-element.14.cpos_ref, ...), custom_call_target="tpu_custom_call" | custom-call | flops 1000000 | bytes 1000000 | tf_op jit(solution)/shard_map/pallas_call | solution.py:240
  115.9 8.8 %all_gather.11.got_ref = f32[512,128]{1,0:T(8,128)S(1)} all-gather(f32[128,128]{1,0:T(8,128)S(1)} %shard_map.98), channel_id=1, replica_groups=mesh['zh'=4,'x'=4,'y'=8,'zl'=2,'core'=2] {'zl','core'}, dimensions={0}, use_global_device_ids=true | all-gather | bytes 327680 | tf_op jit(solution)/shard_map/all_gather | solution.py:245
  124.7 0.7 shard_map.99
  125.4 13.2 %all_to_all.20.got_ref = bf16[8,96,128]{2,1,0:T(8,128)(2,1)S(1)} all-to-all(bf16[8,96,128]{2,1,0:T(8,128)(2,1)S(1)} %shard_map.99), channel_id=1, replica_groups=mesh['zh'=4,'x'=4,'y'=8,'zl'=2,'core'=2] {'y'}, dimensions={0} | all-to-all | bytes 393216 | tf_op jit(solution)/shard_map/all_to_all | solution.py:252
  138.6 0.2 shard_map.100
  138.8 0.0 copy-start.1
  138.8 0.0 copy-start.8
  138.8 0.0 copy-start.10
  138.8 37.1 %all_to_all.21.got_ref = bf16[16,320,128]{2,1,0:T(8,128)(2,1)S(1)} all-to-all(bf16[16,320,128]{2,1,0:T(8,128)(2,1)S(1)} %shard_map.100), channel_id=1, replica_groups=mesh['zh'=4,'x'=4,'y'=8,'zl'=2,'core'=2] {'zh','x'}, dimensions={0} | all-to-all | bytes 2621440 | tf_op jit(solution)/shard_map/all_to_all | solution.py:254
  175.9 0.0 copy-done.1
  175.9 0.0 copy-done.8
  175.9 0.0 copy-done.10
  175.9 1.4 shard_map.101
Async XLA Ops:
  0.6 1.0 copy-start
  1.7 0.7 copy-start.6
  2.4 0.7 copy-start.7
  3.0 0.7 copy-start.9
  5.7 35.3 %copy-start.4 = (s32[128,8]{0,1:T(8,128)S(1)}, s32[128,8]{0,1:T(8,128)}, u32[]{:S(2)}) copy-start(s32[128,8]{0,1:T(8,128)} %param.12) | copy-start | bytes 12292
  5.7 35.3 %copy-start.5 = (s32[128,8]{0,1:T(8,128)S(1)}, s32[128,8]{0,1:T(8,128)}, u32[]{:S(2)}) copy-start(s32[128,8]{0,1:T(8,128)} %param.13) | copy-start | bytes 12292
  5.7 35.3 %all-to-all-start = ((bf16[32,128,128]{2,1,0:T(8,128)(2,1)}), bf16[32,128,128]{2,1,0:T(8,128)(2,1)S(1)}, u32[]{:S(2)}, u32[]{:S(2)}) async-start(bf16[32,128,128]{2,1,0:T(8,128)(2,1)} %bitcast.4), calls=%async_computation | async-start | bytes 2097152 | tf_op jit(solution)/shard_map/all_to_all | solution.py:215
  16.4 54.5 %copy-start.2 = (bf16[128,128]{1,0:T(8,128)(2,1)S(1)}, bf16[128,128]{1,0:T(8,128)(2,1)}, u32[]{:S(2)}) copy-start(bf16[128,128]{1,0:T(8,128)(2,1)} %w_ref.3) | copy-start | bytes 98308
  72.8 36.6 %all-to-all-start.1 = ((bf16[32,160,128]{2,1,0:T(8,128)(2,1)}), bf16[32,160,128]{2,1,0:T(8,128)(2,1)S(1)}, u32[]{:S(2)}, u32[]{:S(2)}) async-start(bf16[32,160,128]{2,1,0:T(8,128)(2,1)} %get-tuple-element.12), calls=%async_computation.1 | async-start | bytes 2621440 | tf_op jit(solution)/shard_map/all_to_all | solution.py:237
  78.4 0.8 copy-start.3
  138.8 37.1 %copy-start.1 = (bf16[1,16,128,128]{3,2,1,0:T(8,128)(2,1)S(1)}, bf16[1,16,128,128]{3,2,1,0:T(8,128)(2,1)}, u32[]{:S(2)}) copy-start(bf16[1,16,128,128]{3,2,1,0:T(8,128)(2,1)} %tiles_ref.3) | copy-start | bytes 1572868
  138.8 37.1 %copy-start.8 = (s32[1,16]{1,0:T(1,128)S(1)}, s32[1,16]{1,0:T(1,128)}, u32[]{:S(2)}) copy-start(s32[1,16]{1,0:T(1,128)} %rows_ref.3) | copy-start | bytes 196
  138.8 37.1 %copy-start.10 = (s32[1,16]{1,0:T(1,128)S(1)}, s32[1,16]{1,0:T(1,128)}, u32[]{:S(2)}) copy-start(s32[1,16]{1,0:T(1,128)} %live_ref.3) | copy-start | bytes 196

commit v2 on v0

v2 whole, which is shorter than its diff:
```python
import functools
import math

import jax
import jax.numpy as jnp
from jax import lax
from jax.experimental import pallas as pl
from jax.experimental.pallas import tpu as pltpu
from jax.sharding import Mesh, PartitionSpec as P

BF = jnp.bfloat16
F32 = jnp.float32
B = 128
F = 128
W32 = 32
ROWS = ("zh", "x", "y")
REP = ("zl", "core")
PARAMS = pltpu.CompilerParams(vmem_limit_bytes=40 * 1024 * 1024)
VMEM = pl.BlockSpec(memory_space=pltpu.VMEM)
SMEM = pl.BlockSpec(memory_space=pltpu.SMEM)


def tn(a, b):
    return lax.dot_general(a, b, (((0,), (0,)), ((), ())), preferred_element_type=F32)


def nt(a, b):
    return lax.dot_general(a, b, (((1,), (1,)), ((), ())), preferred_element_type=F32)


def nn(a, b):
    return lax.dot_general(a, b, (((1,), (0,)), ((), ())), preferred_element_type=F32)


def call(body, in_specs, out_shape, scratch=(), flops=1000000, nbytes=1000000):
    multi = isinstance(out_shape, (tuple, list))
    return pl.pallas_call(
        body,
        out_shape=out_shape,
        in_specs=in_specs,
        out_specs=[VMEM] * len(out_shape) if multi else VMEM,
        scratch_shapes=list(scratch),
        compiler_params=PARAMS,
        cost_estimate=pl.CostEstimate(flops=flops, bytes_accessed=nbytes, transcendentals=0),
    )


def split(value):
    high = value.astype(BF).astype(F32)
    return high, value - high


def products_kernel(rows_ref, live_ref, feat_ref, tiles_ref, out_ref, acc):
    acc[...] = jnp.zeros_like(acc)
    for s in range(tiles_ref.shape[1]):
        prod = nt(feat_ref[...], tiles_ref[0, s]) * live_ref[0, s].astype(F32)
        acc[rows_ref[0, s]] += prod
    out_ref[...] = acc[...].astype(BF)


def aggregate_kernel(place_ref, recv_ref, pos_ref, neg_ref, out_ref):
    part = place_ref[0]
    total = recv_ref[0].astype(F32)
    for r in range(1, recv_ref.shape[0]):
        total = total + recv_ref[r].astype(F32)
    table = jnp.concatenate([pos_ref[...], neg_ref[...]], axis=0)
    block = lax.shift_right_logical(table, 7)
    sent = jnp.where(part == 0, block, table - block * B).astype(F32).astype(BF)
    total = total.astype(BF)
    for d in range(out_ref.shape[0]):
        out_ref[d, 0:W32, :] = total
        out_ref[d, W32:, :] = sent


def embed_kernel(q, place_ref, got_ref, w_ref, enodes_ref, agg_ref, embt_ref, send_ref, et_s, piece_s):
    part, plane = place_ref[0], place_ref[1]
    slots = got_ref.shape[1] - W32
    for b in range(q):
        for p in range(q):
            agg_ref[b, p * W32 : (p + 1) * W32, :] = got_ref[b * q + p, 0:W32, :]
        et = tn(w_ref[...], agg_ref[b])
        et_s[b] = et.astype(BF)
        enodes_ref[b * B : (b + 1) * B, :] = et.T.astype(BF)
    mine = pl.ds(pl.multiple_of(part * W32, W32), W32)
    embt_ref[...] = et_s[plane, mine, :]
    blocks = got_ref[part * q, W32:, :].astype(F32)
    places = got_ref[part * q + 1, W32:, :].astype(F32)
    table = jnp.concatenate([blocks, places, jnp.zeros((B - 2 * slots, B), F32)], axis=0)
    piece_s[...] = table.T.astype(BF)
    rows = pl.multiple_of(plane * W32, W32)
    nodes = enodes_ref[pl.ds(pl.multiple_of(part * B + plane * W32, W32), W32), :]
    partners = piece_s[pl.ds(rows, W32), :]
    for d in range(send_ref.shape[0]):
        send_ref[d, 0:W32, :] = nodes
        send_ref[d, W32:, :] = partners


def direct_kernel(q, xy, place_ref, got_ref, cpos_ref, ctot_ref):
    part, plane = place_ref[0], place_ref[1]
    slots = got_ref.shape[1] - W32
    pk = slots // 2
    first_block = (part * xy).astype(F32)
    first_place = (plane * W32).astype(F32)
    sub = lax.broadcasted_iota(jnp.int32, (B, B), 0).astype(F32)
    chunks = cpos_ref.shape[1] // B
    for b in range(q):
        block = got_ref[b * q, W32:, :].astype(F32) - first_block
        place = got_ref[b * q + 1, W32:, :].astype(F32) - first_place
        inside = (block >= 0.0) & (block < float(xy)) & (place >= 0.0) & (place < float(W32))
        want = jnp.where(inside, block * W32 + place, -1.0)

        def step(c, carry):
            at = sub + (c * B).astype(F32)
            cpos = jnp.zeros((B, B), F32)
            cneg = jnp.zeros((B, B), F32)
            for k in range(pk):
                cpos = jnp.where(at == want[k : k + 1], cpos + 1.0, cpos)
                cneg = jnp.where(at == want[pk + k : pk + k + 1], cneg + 1.0, cneg)
            rows = pl.ds(pl.multiple_of(c * B, B), B)
            cpos_ref[b, rows, :] = cpos.astype(BF)
            ctot_ref[b, rows, :] = (cpos + cneg).astype(BF)
            return carry

        lax.fori_loop(0, chunks, step, 0)


def decoder_kernel(
    q, xy, place_ref, got_ref, en_ref, agg_ref, w_ref, cpos_ref, ctot_ref, out_ref,
    em_s, code_s, wide_s, logit_s, high_s, low_s,
):
    slots = wide_s.shape[0]
    pk = slots // 2
    col = place_ref[2]
    pieces = got_ref.shape[0]
    count = pieces * W32
    em_s[...] = got_ref[:, 0:W32, :].reshape(count, F)
    table = got_ref[:, W32:, :].reshape(count, B).astype(F32)
    places = pltpu.roll(table, B - slots, 1)
    code = jnp.full((count, B), -1.0, F32)
    for b in range(q):
        code = jnp.where(table == (b * xy + col).astype(F32), places + float(b * B), code)
    code_s[...] = code
    logit_s[...] = nt(em_s[...], en_ref[...])
    lane = lax.broadcasted_iota(jnp.int32, (B, B), 1).astype(F32)
    scale = 1.0 / math.sqrt(F)

    def step(c, carry):
        rows = pl.ds(pl.multiple_of(c * B, B), B)
        for k in range(slots):
            wide_s[k] = jnp.broadcast_to(code_s[rows, k : k + 1], (B, B))
        for b in range(q):
            at = lane + float(b * B)
            ipos = cpos_ref[b, rows, :].astype(F32)
            itot = ctot_ref[b, rows, :].astype(F32)
            ineg = jnp.zeros((B, B), F32)
            both = jnp.zeros((B, B), F32)
            for k in range(pk):
                both = jnp.where(wide_s[k] == at, both + 1.0, both)
                ineg = jnp.where(wide_s[pk + k] == at, ineg + 1.0, ineg)
            cols = slice(b * B, (b + 1) * B)
            sig = jax.nn.sigmoid(logit_s[rows, cols] * scale)
            coef = (itot + both + ineg) * sig - (ipos + both)
            high, low = split(coef)
            high_s[rows, cols] = high.astype(BF)
            low_s[rows, cols] = low.astype(BF)
        return carry

    lax.fori_loop(0, count // B, step, 0)
    em_t = em_s[...].astype(F32).T.astype(BF)
    grad = (nn(em_t, high_s[...]) + nn(em_t, low_s[...])) * (1.0 / pk)
    high, low = split(grad)
    high, low = high.astype(BF), low.astype(BF)
    grad_agg = nn(w_ref[...], high) + nn(w_ref[...], low)
    terms = jnp.zeros((F, F), F32)
    for b in range(q):
        cols = slice(b * B, (b + 1) * B)
        terms = terms + nt(agg_ref[b], high[:, cols]) + nt(agg_ref[b], low[:, cols])
    thigh, tlow = split(terms)
    eighth = W32 // q
    for z in range(q):
        for p in range(q):
            first = p * W32 + z * eighth
            piece = [
                grad_agg[p * W32 : (p + 1) * W32, z * B : (z + 1) * B],
                thigh[first : first + eighth],
                tlow[first : first + eighth],
            ]
            out_ref[z * q + p] = jnp.concatenate(piece, axis=0).astype(BF)


def owner_kernel(q, got_ref, out_ref):
    total = got_ref[0].astype(F32)
    for r in range(1, got_ref.shape[0]):
        total = total + got_ref[r].astype(F32)
    eighth = W32 // q
    high, low = split(total[W32 : W32 + eighth] + total[W32 + eighth :])
    sent = jnp.concatenate([total[:W32], high, low], axis=0).astype(BF)
    for d in range(out_ref.shape[0]):
        out_ref[d] = sent


def merge_kernel(q, got_ref, out_ref):
    count = got_ref.shape[0]
    ny = count // q
    eighth = W32 // q
    out_ref[0 : count * W32, :] = got_ref[:, 0:W32, :].reshape(count * W32, B)
    rows = []
    for z in range(q):
        total = got_ref[z * ny, W32:, :].astype(F32)
        for y in range(1, ny):
            total = total + got_ref[z * ny + y, W32:, :].astype(F32)
        rows.append(total[:eighth] + total[eighth:])
    high, low = split(jnp.concatenate(rows, axis=0))
    out_ref[count * W32 : (count + 1) * W32, :] = high.astype(BF)
    out_ref[(count + 1) * W32 :, :] = low.astype(BF)


def features_kernel(q, nx, ny, place_ref, rows_ref, live_ref, *refs):
    got, (tiles_ref, gft_ref, gw_ref) = refs[:nx], refs[nx:]
    my_x = place_ref[3]
    total = jnp.zeros((W32, B), F32)
    for s in range(tiles_ref.shape[1]):
        row = rows_ref[0, s]
        plane = lax.div(row, nx * ny)
        line = lax.rem(lax.div(row, ny), nx)
        ahead = lax.rem(my_x - line + nx, nx)
        first = pl.multiple_of((plane * ny + lax.rem(row, ny)) * W32, W32)
        live = live_ref[0, s].astype(F32)
        block = jnp.zeros((W32, B), F32)
        for d in range(nx):
            use = jnp.where(ahead == d, live, 0.0)
            block = block + got[d][pl.ds(first, W32), :].astype(F32) * use
        total = total + nn(block.astype(BF), tiles_ref[0, s])
    gft_ref[...] = total.astype(BF)
    first = q * ny * W32
    terms = jnp.zeros((W32, F), F32)
    for d in range(nx):
        terms = terms + got[d][first : first + W32, :].astype(F32)
        terms = terms + got[d][first + W32 : first + 2 * W32, :].astype(F32)
    gw_ref[...] = terms * (1.0 / math.sqrt(q * nx * ny * B))


def on_device(features, weight, tiles, tile_rows, tile_live, pos_partner, neg_partner):
    q = lax.axis_size("zh")
    nx, ny = lax.axis_size("x"), lax.axis_size("y")
    xy = nx * ny
    plane, part = lax.axis_index("zh"), lax.axis_index(REP)
    column = lax.axis_index(("x", "y"))
    place = jnp.stack([part, plane, column, lax.axis_index("x")]).astype(jnp.int32)
    shape = jax.ShapeDtypeStruct
    slots = 2 * pos_partner.shape[1]
    count = xy * W32

    sent = call(
        products_kernel,
        [SMEM, SMEM, VMEM, VMEM],
        shape((q * xy, W32, B), BF),
        [pltpu.VMEM((q * xy, W32, B), F32)],
    )(tile_rows, tile_live, features.T, tiles)
    recv = lax.all_to_all(sent, ROWS, 0, 0, tiled=True)

    column_part = call(
        aggregate_kernel, [SMEM, VMEM, VMEM, VMEM], shape((q * q, W32 + slots, B), BF)
    )(place, recv, pos_partner.T, neg_partner.T)
    blocks = lax.all_to_all(column_part, ("zh",) + REP, 0, 0, tiled=True)

    enodes, agg, emb_t, slab_part = call(
        functools.partial(embed_kernel, q),
        [SMEM, VMEM, VMEM],
        (
            shape((q * B, F), BF),
            shape((q, F, B), BF),
            shape((W32, B), BF),
            shape((xy, 2 * W32, B), BF),
        ),
        [pltpu.VMEM((q, F, B), BF), pltpu.VMEM((B, B), BF)],
    )(place, blocks, weight)
    slab = lax.all_to_all(slab_part, ("x", "y"), 0, 0, tiled=True)

    cpos, ctot = call(
        functools.partial(direct_kernel, q, xy),
        [SMEM, VMEM],
        (shape((q, count, B), BF), shape((q, count, B), BF)),
        flops=100000000,
    )(place, blocks)

    pieces = call(
        functools.partial(decoder_kernel, q, xy),
        [SMEM] + [VMEM] * 6,
        shape((q * q, W32 + 2 * W32 // q, B), BF),
        [
            pltpu.VMEM((count, F), BF),
            pltpu.VMEM((count, B), F32),
            pltpu.VMEM((slots, B, B), F32),
            pltpu.VMEM((count, q * B), F32),
            pltpu.VMEM((count, q * B), BF),
            pltpu.VMEM((count, q * B), BF),
        ],
    )(place, slab, enodes, agg, weight, cpos, ctot)
    mine = lax.all_to_all(pieces, ("zh",) + REP, 0, 0, tiled=True)

    height = pieces.shape[1]
    plane_part = call(functools.partial(owner_kernel, q), [VMEM], shape((q * ny, height, B), BF))(mine)
    lines = lax.all_to_all(plane_part, ("zh", "y"), 0, 0, tiled=True)

    line = call(
        functools.partial(merge_kernel, q), [VMEM], shape(((q * ny + 2) * W32, B), BF)
    )(lines)
    ahead = [line]
    for d in range(1, nx):
        ahead.append(lax.ppermute(line, "x", [(i, (i + d) % nx) for i in range(nx)]))

    gf_t, grad_weight = call(
        functools.partial(features_kernel, q, nx, ny),
        [SMEM, SMEM, SMEM] + [VMEM] * (nx + 1),
        (shape((W32, B), BF), shape((W32, F), F32)),
    )(place, tile_rows, tile_live, *ahead, tiles)
    return (emb_t.T, grad_weight, gf_t.T)


def sharded(mesh):
    return jax.shard_map(
        on_device,
        mesh=mesh,
        in_specs=(
            P(ROWS, REP),
            P(),
            P(ROWS, None, None, None),
            P(ROWS, None),
            P(ROWS, None),
            P(ROWS, None),
            P(ROWS, None),
        ),
        out_specs=(P(ROWS, REP), P(REP, None), P(ROWS, REP)),
        check_vma=False,
    )


def solution(mesh):
    rows = mesh.shape["rows"]
    parts = mesh.devices.reshape(4, 4, rows // 16, 2, 2)
    return sharded(Mesh(parts, ("zh", "x", "y", "zl", "core")))
```

time: 2470 us -> 161 us (0.07)
  the two profiles are of different devices: /device:TPU:64 before, /device:TPU:8 now
where the time goes in v2:
time: 161 us; the launch traced here: 160 us
  waiting for transfers between devices  56.9 us (35%)
  blocking collectives  48.6 us (30%)
  starting transfers between devices  33.7 us (21%)
  Pallas kernels  17.9 us (11%)
  local copies, waits for them, and re-layouts  2.42 us (2%)
    all_to_all x1, waiting for transfers between devices, on_device(): recv = lax.all_to_all(sent, ROWS, 0, 0, tiled=True)  32.2 us
    all_to_all x1, blocking collectives, on_device(): lines = lax.all_to_all(plane_part, ('zh', 'y'), 0, 0, tiled=True)  22.8 us
    all_to_all x1, starting transfers between devices, on_device(): recv = lax.all_to_all(sent, ROWS, 0, 0, tiled=True)  19.8 us
    all_to_all x1, waiting for transfers between devices, on_device(): slab = lax.all_to_all(slab_part, ('x', 'y'), 0, 0, tiled=True)  14.5 us
    all_to_all x1, blocking collectives, on_device(): blocks = lax.all_to_all(column_part, ('zh',) + REP, 0, 0, tiled=True)  13.3 us
    all_to_all x1, blocking collectives, on_device(): mine = lax.all_to_all(pieces, ('zh',) + REP, 0, 0, tiled=True)  12.5 us
    ppermute x3, waiting for transfers between devices, on_device(): lax.ppermute(line, 'x', [(i, (i + d) % nx) for i in range(nx)])  10.2 us
    ppermute x3, starting transfers between devices, on_device(): lax.ppermute(line, 'x', [(i, (i + d) % nx) for i in range(nx)])  8.8 us
  transfers between devices with their start and end apart: 5, of which 5 were waited for; matrix products, arithmetic and copies ran while one was open for 0% of the time, Pallas kernels for 3%

profile of v2, /device:TPU:8, one launch (start us, length us, event | category | flops | bytes accessed | tf_op | source)
XLA Modules:
  0.0 160.4 jit_solution(7156180918051520835)
XLA Ops:
  0.6 0.0 copy-start.7
  0.6 0.0 copy-start.6
  0.7 0.6 copy-done.7
  1.3 0.0 copy-done.6
  1.3 0.0 copy-start
  1.3 1.0 copy-done
  2.3 0.0 copy-start.3
  2.3 0.7 copy-done.3
  3.0 2.0 %shard_map.94 = bf16[128,32,128]{2,1,0:T(8,128)(2,1)} custom-call(s32[1,16]{1,0:T(1,128)S(1)} %copy-done.6, s32[1,16]{1,0:T(1,128)S(1)} %copy-done.7, bf16[32,128]{1,0:T(8,128)(2,1)S(1)} %bitcast.9, bf16[1,16,128,128]{3,2,1,0:T(8,128)(2,1)S(1)} %copy-done), custom_call_target="tpu_custom_call" | custom-call | flops 1000000 | bytes 1000000 | tf_op jit(solution)/shard_map/pallas_call | solution.py:254
  5.1 19.8 %all-to-all-start = ((bf16[128,32,128]{2,1,0:T(8,128)(2,1)}), bf16[128,32,128]{2,1,0:T(8,128)(2,1)S(1)}, u32[]{:S(2)}, u32[]{:S(2)}) async-start(bf16[128,32,128]{2,1,0:T(8,128)(2,1)} %shard_map.94), calls=%async_computation | async-start | bytes 2097152 | tf_op jit(solution)/shard_map/all_to_all | solution.py:260
  24.9 0.0 copy-start.4
  24.9 0.0 copy-start.5
  24.9 0.1 pad_add_fusion.place_ref
  25.0 32.2 %all-to-all-done.recv_ref = bf16[128,32,128]{2,1,0:T(8,128)(2,1)S(1)} async-done(((bf16[128,32,128]{2,1,0:T(8,128)(2,1)}), bf16[128,32,128]{2,1,0:T(8,128)(2,1)S(1)}, u32[]{:S(2)}, u32[]{:S(2)}) %all-to-all-start) | async-done | bytes 1048608 | tf_op jit(solution)/shard_map/all_to_all | solution.py:260
  57.2 0.0 copy-done.4
  57.2 0.0 copy-done.5
  57.2 0.7 shard_map.95
  58.0 0.0 copy-start.2
  58.0 13.3 %all_to_all.25.got_ref = bf16[16,48,128]{2,1,0:T(8,128)(2,1)S(1)} all-to-all(bf16[16,48,128]{2,1,0:T(8,128)(2,1)S(1)} %shard_map.95), channel_id=1, replica_groups=mesh['zh'=4,'x'=4,'y'=8,'zl'=2,'core'=2] {'zh','zl','core'}, dimensions={0} | all-to-all | bytes 393216 | tf_op jit(solution)/shard_map/all_to_all | solution.py:265
  71.2 0.0 copy-done.2
  71.2 1.7 %shard_map.96 = (bf16[512,128]{1,0:T(8,128)(2,1)S(1)}, bf16[4,128,128]{2,1,0:T(8,128)(2,1)S(1)}, bf16[32,128]{1,0:T(8,128)(2,1)}, bf16[32,64,128]{2,1,0:T(8,128)(2,1)}) custom-call(s32[4]{0:T(128)S(1)} %pad_add_fusion.place_ref, bf16[16,48,128]{2,1,0:T(8,128)(2,1)S(1)} %all_to_all.25.got_ref, bf16[128,128]{1,0:T(8,128)(2,1)S(1)} %copy-done.2), custom_call_target="tpu_custom_call" | custom-call | flops 1000000 | bytes 1000000 | tf_op jit(solution)/shard_map/pallas_call | solution.py:267
  73.0 5.1 %all-to-all-start.2 = ((bf16[32,64,128]{2,1,0:T(8,128)(2,1)}), bf16[32,64,128]{2,1,0:T(8,128)(2,1)S(1)}, u32[]{:S(2)}, u32[]{:S(2)}) async-start(bf16[32,64,128]{2,1,0:T(8,128)(2,1)} %get-tuple-element.12), calls=%async_computation.2 | async-start | bytes 1048576 | tf_op jit(solution)/shard_map/all_to_all | solution.py:278
  78.1 4.2 %shard_map.97 = (bf16[4,1024,128]{2,1,0:T(8,128)(2,1)S(1)}, bf16[4,1024,128]{2,1,0:T(8,128)(2,1)S(1)}) custom-call(s32[4]{0:T(128)S(1)} %pad_add_fusion.place_ref, bf16[16,48,128]{2,1,0:T(8,128)(2,1)S(1)} %all_to_all.25.got_ref), custom_call_target="tpu_custom_call" | custom-call | flops 100000000 | bytes 1000000 | tf_op jit(solution)/shard_map/pallas_call | solution.py:280
  82.2 14.5 %all-to-all-done.2.got_ref = bf16[32,64,128]{2,1,0:T(8,128)(2,1)S(1)} async-done(((bf16[32,64,128]{2,1,0:T(8,128)(2,1)}), bf16[32,64,128]{2,1,0:T(8,128)(2,1)S(1)}, u32[]{:S(2)}, u32[]{:S(2)}) %all-to-all-start.2) | async-done | bytes 524320 | tf_op jit(solution)/shard_map/all_to_all | solution.py:278
  96.7 7.7 %shard_map.98 = bf16[16,48,128]{2,1,0:T(8,128)(2,1)S(1)} custom-call(s32[4]{0:T(128)S(1)} %pad_add_fusion.place_ref, bf16[32,64,128]{2,1,0:T(8,128)(2,1)S(1)} %all-to-all-done.2.got_ref, bf16[512,128]{1,0:T(8,128)(2,1)S(1)} %get-tuple-element.13.en_ref, bf16[4,128,128]{2,1,0:T(8,128)(2,1)S(1)} %get-tuple-element.14.agg_ref, bf16[128,128]{1,0:T(8,128)(2,1)S(1)} %copy-done.2, ...), custom_call_target="tpu_custom_call" | custom-call | flops 1000000 | bytes 1000000 | tf_op jit(solution)/shard_map/pallas_call | solution.py:287
  104.4 12.5 %all_to_all.26.got_ref = bf16[16,48,128]{2,1,0:T(8,128)(2,1)S(1)} all-to-all(bf16[16,48,128]{2,1,0:T(8,128)(2,1)S(1)} %shard_map.98), channel_id=1, replica_groups=mesh['zh'=4,'x'=4,'y'=8,'zl'=2,'core'=2] {'zh','zl','core'}, dimensions={0} | all-to-all | bytes 393216 | tf_op jit(solution)/shard_map/all_to_all | solution.py:300
  117.0 22.8 %all_to_all.27.got_ref = bf16[32,48,128]{2,1,0:T(8,128)(2,1)S(1)} all-to-all(bf16[32,48,128]{2,1,0:T(8,128)(2,1)S(1)} %shard_map.99), channel_id=1, replica_groups=mesh['zh'=4,'x'=4,'y'=8,'zl'=2,'core'=2] {'zh','y'}, dimensions={0} | all-to-all | bytes 786432 | tf_op jit(solution)/shard_map/all_to_all | solution.py:304
  139.8 0.0 copy-start.1
  139.8 3.2 %collective-permute-start.2 = (bf16[1088,128]{1,0:T(8,128)(2,1)S(1)}, bf16[1088,128]{1,0:T(8,128)(2,1)S(1)}, u32[]{:S(2)}, u32[]{:S(2)}) collective-permute-start(bf16[1088,128]{1,0:T(8,128)(2,1)S(1)} %shard_map.100.refs_0_), channel_id=1, source_target_pairs={{0,96},{32,0},{64,32},{96,64},{1,97},{33,1},{65,33},{97,65},{2,98}... | collective-permute-start | bytes 835592 | tf_op jit(solution)/shard_map/ppermute | solution.py:311
  143.0 3.4 %collective-permute-start.1 = (bf16[1088,128]{1,0:T(8,128)(2,1)S(1)}, bf16[1088,128]{1,0:T(8,128)(2,1)S(1)}, u32[]{:S(2)}, u32[]{:S(2)}) collective-permute-start(bf16[1088,128]{1,0:T(8,128)(2,1)S(1)} %shard_map.100.refs_0_), channel_id=1, source_target_pairs={{0,64},{32,96},{64,0},{96,32},{1,65},{33,97},{65,1},{97,33},{2,66}... | collective-permute-start | bytes 835592 | tf_op jit(solution)/shard_map/ppermute | solution.py:311
  146.5 2.2 %collective-permute-start = (bf16[1088,128]{1,0:T(8,128)(2,1)S(1)}, bf16[1088,128]{1,0:T(8,128)(2,1)S(1)}, u32[]{:S(2)}, u32[]{:S(2)}) collective-permute-start(bf16[1088,128]{1,0:T(8,128)(2,1)S(1)} %shard_map.100.refs_0_), channel_id=1, source_target_pairs={{0,32},{32,64},{64,96},{96,0},{1,33},{33,65},{65,97},{97,1},{2,34}... | collective-permute-start | bytes 835592 | tf_op jit(solution)/shard_map/ppermute | solution.py:311
  148.7 2.8 %collective-permute-done.2.refs_3_ = bf16[1088,128]{1,0:T(8,128)(2,1)S(1)} collective-permute-done((bf16[1088,128]{1,0:T(8,128)(2,1)S(1)}, bf16[1088,128]{1,0:T(8,128)(2,1)S(1)}, u32[]{:S(2)}, u32[]{:S(2)}) %collective-permute-start.2) | collective-permute-done | bytes 278560 | tf_op jit(solution)/shard_map/ppermute | solution.py:311
  151.5 4.4 %collective-permute-done.1.refs_2_ = bf16[1088,128]{1,0:T(8,128)(2,1)S(1)} collective-permute-done((bf16[1088,128]{1,0:T(8,128)(2,1)S(1)}, bf16[1088,128]{1,0:T(8,128)(2,1)S(1)}, u32[]{:S(2)}, u32[]{:S(2)}) %collective-permute-start.1) | collective-permute-done | bytes 278560 | tf_op jit(solution)/shard_map/ppermute | solution.py:311
  155.9 3.0 %collective-permute-done.refs_1_ = bf16[1088,128]{1,0:T(8,128)(2,1)S(1)} collective-permute-done((bf16[1088,128]{1,0:T(8,128)(2,1)S(1)}, bf16[1088,128]{1,0:T(8,128)(2,1)S(1)}, u32[]{:S(2)}, u32[]{:S(2)}) %collective-permute-start) | collective-permute-done | bytes 278560 | tf_op jit(solution)/shard_map/ppermute | solution.py:311
  158.9 0.0 copy-done.1
  158.9 1.5 shard_map.101
  (2 shorter events, 0.1 us)
Async XLA Ops:
  0.6 0.7 copy-start.7
  0.6 0.7 copy-start.6
  1.3 1.0 copy-start
  2.3 0.7 copy-start.3
  5.1 52.2 %all-to-all-start = ((bf16[128,32,128]{2,1,0:T(8,128)(2,1)}), bf16[128,32,128]{2,1,0:T(8,128)(2,1)S(1)}, u32[]{:S(2)}, u32[]{:S(2)}) async-start(bf16[128,32,128]{2,1,0:T(8,128)(2,1)} %shard_map.94), calls=%async_computation | async-start | bytes 2097152 | tf_op jit(solution)/shard_map/all_to_all | solution.py:260
  24.9 32.3 %copy-start.4 = (s32[128,8]{0,1:T(8,128)S(1)}, s32[128,8]{0,1:T(8,128)}, u32[]{:S(2)}) copy-start(s32[128,8]{0,1:T(8,128)} %param.12) | copy-start | bytes 12292
  24.9 32.3 %copy-start.5 = (s32[128,8]{0,1:T(8,128)S(1)}, s32[128,8]{0,1:T(8,128)}, u32[]{:S(2)}) copy-start(s32[128,8]{0,1:T(8,128)} %param.13) | copy-start | bytes 12292
  58.0 13.3 %copy-start.2 = (bf16[128,128]{1,0:T(8,128)(2,1)S(1)}, bf16[128,128]{1,0:T(8,128)(2,1)}, u32[]{:S(2)}) copy-start(bf16[128,128]{1,0:T(8,128)(2,1)} %w_ref.3) | copy-start | bytes 98308
  73.0 23.7 %all-to-all-start.2 = ((bf16[32,64,128]{2,1,0:T(8,128)(2,1)}), bf16[32,64,128]{2,1,0:T(8,128)(2,1)S(1)}, u32[]{:S(2)}, u32[]{:S(2)}) async-start(bf16[32,64,128]{2,1,0:T(8,128)(2,1)} %get-tuple-element.12), calls=%async_computation.2 | async-start | bytes 1048576 | tf_op jit(solution)/shard_map/all_to_all | solution.py:278
  139.8 19.1 %copy-start.1 = (bf16[1,16,128,128]{3,2,1,0:T(8,128)(2,1)S(1)}, bf16[1,16,128,128]{3,2,1,0:T(8,128)(2,1)}, u32[]{:S(2)}) copy-start(bf16[1,16,128,128]{3,2,1,0:T(8,128)(2,1)} %refs_4_.1) | copy-start | bytes 1572868
  139.8 11.6 %collective-permute-start.2 = (bf16[1088,128]{1,0:T(8,128)(2,1)S(1)}, bf16[1088,128]{1,0:T(8,128)(2,1)S(1)}, u32[]{:S(2)}, u32[]{:S(2)}) collective-permute-start(bf16[1088,128]{1,0:T(8,128)(2,1)S(1)} %shard_map.100.refs_0_), channel_id=1, source_target_pairs={{0,96},{32,0},{64,32},{96,64},{1,97},{33,1},{65,33},{97,65},{2,98}... | collective-permute-start | bytes 835592 | tf_op jit(solution)/shard_map/ppermute | solution.py:311
  143.0 12.8 %collective-permute-start.1 = (bf16[1088,128]{1,0:T(8,128)(2,1)S(1)}, bf16[1088,128]{1,0:T(8,128)(2,1)S(1)}, u32[]{:S(2)}, u32[]{:S(2)}) collective-permute-start(bf16[1088,128]{1,0:T(8,128)(2,1)S(1)} %shard_map.100.refs_0_), channel_id=1, source_target_pairs={{0,64},{32,96},{64,0},{96,32},{1,65},{33,97},{65,1},{97,33},{2,66}... | collective-permute-start | bytes 835592 | tf_op jit(solution)/shard_map/ppermute | solution.py:311
  146.5 12.4 %collective-permute-start = (bf16[1088,128]{1,0:T(8,128)(2,1)S(1)}, bf16[1088,128]{1,0:T(8,128)(2,1)S(1)}, u32[]{:S(2)}, u32[]{:S(2)}) collective-permute-start(bf16[1088,128]{1,0:T(8,128)(2,1)S(1)} %shard_map.100.refs_0_), channel_id=1, source_target_pairs={{0,32},{32,64},{64,96},{96,0},{1,33},{33,65},{65,97},{97,1},{2,34}... | collective-permute-start | bytes 835592 | tf_op jit(solution)/shard_map/ppermute | solution.py:311

commit v3 on v2

v3 whole, which is shorter than its diff:
```python
import functools
import math

import jax
import jax.numpy as jnp
from jax import lax
from jax.experimental import pallas as pl
from jax.experimental.pallas import tpu as pltpu
from jax.sharding import Mesh, PartitionSpec as P

BF = jnp.bfloat16
F32 = jnp.float32
B = 128
F = 128
W32 = 32
ROWS = ("zh", "x", "y")
REP = ("zl", "core")
PARAMS = pltpu.CompilerParams(vmem_limit_bytes=40 * 1024 * 1024)
VMEM = pl.BlockSpec(memory_space=pltpu.VMEM)
SMEM = pl.BlockSpec(memory_space=pltpu.SMEM)


def tn(a, b):
    return lax.dot_general(a, b, (((0,), (0,)), ((), ())), preferred_element_type=F32)


def nt(a, b):
    return lax.dot_general(a, b, (((1,), (1,)), ((), ())), preferred_element_type=F32)


def nn(a, b):
    return lax.dot_general(a, b, (((1,), (0,)), ((), ())), preferred_element_type=F32)


def call(body, in_specs, out_shape, scratch=(), flops=1000000, nbytes=1000000):
    multi = isinstance(out_shape, (tuple, list))
    return pl.pallas_call(
        body,
        out_shape=out_shape,
        in_specs=in_specs,
        out_specs=[VMEM] * len(out_shape) if multi else VMEM,
        scratch_shapes=list(scratch),
        compiler_params=PARAMS,
        cost_estimate=pl.CostEstimate(flops=flops, bytes_accessed=nbytes, transcendentals=0),
    )


def split(value):
    high = value.astype(BF).astype(F32)
    return high, value - high


def products_kernel(rows_ref, live_ref, feat_ref, tiles_ref, out_ref, acc):
    acc[...] = jnp.zeros_like(acc)
    for s in range(tiles_ref.shape[1]):
        prod = nt(feat_ref[...], tiles_ref[0, s]) * live_ref[0, s].astype(F32)
        acc[rows_ref[0, s]] += prod
    out_ref[...] = acc[...].astype(BF)


def aggregate_kernel(recv_ref, out_ref):
    total = recv_ref[0].astype(F32)
    for r in range(1, recv_ref.shape[0]):
        total = total + recv_ref[r].astype(F32)
    out_ref[...] = total.astype(BF)


def embed_kernel(place_ref, agg_ref, w_ref, pos_ref, neg_ref, embt_ref, send_ref, et_s, e_s):
    part, column = place_ref[0], place_ref[2]
    et = tn(w_ref[...], agg_ref[...])
    et_s[...] = et.astype(BF)
    e_s[...] = et.T.astype(BF)
    mine = pl.ds(pl.multiple_of(part * W32, W32), W32)
    embt_ref[...] = et_s[mine, :]
    nodes = e_s[mine, :]
    ids = jnp.concatenate([pos_ref[...], neg_ref[...]], axis=0)
    block = lax.shift_right_logical(ids, 7)
    table = jnp.concatenate([block, ids - block * B], axis=0).astype(F32)
    lane = lax.broadcasted_iota(jnp.int32, table.shape, 1)
    first = part * W32
    table = jnp.where((lane >= first) & (lane < first + W32), table, 0.0)
    quarters = B // W32
    turn = lax.rem(lax.rem(column, quarters) - part + quarters, quarters) * W32
    partners = pltpu.roll(table, turn, 1).astype(BF)
    for d in range(send_ref.shape[0]):
        send_ref[d, 0:W32, :] = nodes
        send_ref[d, W32:, :] = partners


def nodes_kernel(w_ref, *refs):
    aggs, out_ref = refs[:-1], refs[-1]
    for d, agg_ref in enumerate(aggs):
        out_ref[d * B : (d + 1) * B, :] = tn(w_ref[...], agg_ref[...]).T.astype(BF)


def direct_kernel(xy, place_ref, *refs):
    tables, (cpos_ref, ctot_ref, want_s, wide_s) = refs[:-4], refs[-4:]
    part, plane = place_ref[0], place_ref[1]
    slots = tables[0].shape[0]
    pk = slots // 2
    lane = lax.broadcasted_iota(jnp.int32, (B, B), 1).astype(F32)
    for d, table_ref in enumerate(tables):
        ids = table_ref[...]
        block = lax.shift_right_logical(ids, 7)
        piece = block - plane * xy
        place = ids - block * B - part * W32
        inside = (piece >= 0) & (piece < xy) & (place >= 0) & (place < W32)
        want = jnp.where(inside, piece * W32 + place, -1).astype(F32)
        want_s[...] = jnp.concatenate([want, jnp.zeros((B - slots, B), F32)], axis=0).T
        for k in range(slots):
            wide_s[k] = jnp.broadcast_to(want_s[:, k : k + 1], (B, B))

        def step(g, carry):
            at = lane + (g * B).astype(F32)
            cpos = jnp.zeros((B, B), F32)
            cneg = jnp.zeros((B, B), F32)
            for k in range(pk):
                cpos = jnp.where(wide_s[k] == at, cpos + 1.0, cpos)
                cneg = jnp.where(wide_s[pk + k] == at, cneg + 1.0, cneg)
            cpos_ref[g, d * B : (d + 1) * B, :] = cpos.astype(BF)
            ctot_ref[g, d * B : (d + 1) * B, :] = (cpos + cneg).astype(BF)
            return carry

        lax.fori_loop(0, cpos_ref.shape[0], step, 0)


def decoder_kernel(q, xy, slots, place_ref, got_ref, en_ref, w_ref, cpos_ref, ctot_ref, *refs):
    aggs, (out_ref, logit_s, high_s, low_s) = refs[:q], refs[q:]
    pk = slots // 2
    plane, column = place_ref[1], place_ref[2]
    quarters = B // W32
    groups = got_ref.shape[0] // quarters
    tile = 16
    sub = [
        (lax.broadcasted_iota(jnp.int32, (tile, B), 0) + i * tile).astype(F32).astype(BF)
        for i in range(B // tile)
    ]
    en = en_ref[...]
    for g in range(groups):
        em = got_ref[g * quarters : (g + 1) * quarters, 0:W32, :].reshape(B, F)
        logit_s[g] = nt(en, em)
    half = 0.5 / math.sqrt(F)
    one, zero = jnp.ones((tile, B), BF), jnp.zeros((tile, B), BF)

    def step(g, carry):
        table = got_ref[g * quarters, W32:, :].astype(F32)
        for j in range(1, quarters):
            table = table + got_ref[g * quarters + j, W32:, :].astype(F32)
        for d in range(q):
            block = lax.rem(plane - d + q, q) * xy + column
            code = jnp.where(table[:slots] == block.astype(F32), table[slots:], -1.0)
            wide = [
                jnp.broadcast_to(code[k : k + 1], (tile, B)).astype(BF) for k in range(slots)
            ]
            both, ineg = [], []
            for i in range(B // tile):
                cp, cn = zero, zero
                for k in range(pk):
                    cp = jnp.where(wide[k] == sub[i], cp + one, cp)
                    cn = jnp.where(wide[pk + k] == sub[i], cn + one, cn)
                both.append(cp)
                ineg.append(cp + cn)
            rows = slice(d * B, (d + 1) * B)
            cpos = (cpos_ref[g, rows, :] + jnp.concatenate(both, axis=0)).astype(F32)
            ctot = (ctot_ref[g, rows, :] + jnp.concatenate(ineg, axis=0)).astype(F32)
            sig = 0.5 * jnp.tanh(logit_s[g, rows, :] * half) + 0.5
            high, low = split(ctot * sig - cpos)
            high_s[g, rows, :] = high.astype(BF)
            low_s[g, rows, :] = low.astype(BF)
        return carry

    lax.fori_loop(0, groups, step, 0)
    grad = jnp.zeros((q * B, F), F32)
    for g in range(groups):
        em = got_ref[g * quarters : (g + 1) * quarters, 0:W32, :].reshape(B, F)
        grad = grad + nn(high_s[g], em) + nn(low_s[g], em)
    high, low = split(grad * (1.0 / pk))
    high, low = high.astype(BF), low.astype(BF)
    grad_agg = nt(w_ref[...], high) + nt(w_ref[...], low)
    terms = jnp.zeros((F, F), F32)
    for d in range(q):
        rows = slice(d * B, (d + 1) * B)
        terms = terms + nn(aggs[d][...], high[rows]) + nn(aggs[d][...], low[rows])
    thigh, tlow = split(terms)
    eighth = W32 // q
    for d in range(q):
        z = lax.rem(plane - d + q, q)
        for p in range(q):
            cols = grad_agg[p * W32 : (p + 1) * W32, d * B : (d + 1) * B]
            out_ref[z * q + p, 0:W32, :] = cols.astype(BF)
    for z in range(q):
        for p in range(q):
            first = p * W32 + z * eighth
            piece = [thigh[first : first + eighth], tlow[first : first + eighth]]
            out_ref[z * q + p, W32:, :] = jnp.concatenate(piece, axis=0).astype(BF)


def owner_kernel(q, got_ref, out_ref):
    total = got_ref[0].astype(F32)
    for r in range(1, got_ref.shape[0]):
        total = total + got_ref[r].astype(F32)
    eighth = W32 // q
    high, low = split(total[W32 : W32 + eighth] + total[W32 + eighth :])
    sent = jnp.concatenate([total[:W32], high, low], axis=0).astype(BF)
    for d in range(out_ref.shape[0]):
        out_ref[d] = sent


def merge_kernel(q, got_ref, out_ref):
    count = got_ref.shape[0]
    ny = count // q
    eighth = W32 // q
    blocks = got_ref[:, 0:W32, :].reshape(count * W32, B)
    rows = []
    for z in range(q):
        total = got_ref[z * ny, W32:, :].astype(F32)
        for y in range(1, ny):
            total = total + got_ref[z * ny + y, W32:, :].astype(F32)
        rows.append(total[:eighth] + total[eighth:])
    high, low = split(jnp.concatenate(rows, axis=0))
    for d in range(out_ref.shape[0]):
        out_ref[d, 0 : count * W32, :] = blocks
        out_ref[d, count * W32 : (count + 1) * W32, :] = high.astype(BF)
        out_ref[d, (count + 1) * W32 :, :] = low.astype(BF)


def features_kernel(q, nx, ny, rows_ref, live_ref, got_ref, tiles_ref, gft_ref, gw_ref):
    total = jnp.zeros((W32, B), F32)
    for s in range(tiles_ref.shape[1]):
        row = rows_ref[0, s]
        plane = lax.div(row, nx * ny)
        line = lax.rem(lax.div(row, ny), nx)
        first = pl.multiple_of((plane * ny + lax.rem(row, ny)) * W32, W32)
        live = live_ref[0, s].astype(F32)
        block = got_ref[line, pl.ds(first, W32), :].astype(F32) * live
        total = total + nn(block.astype(BF), tiles_ref[0, s])
    gft_ref[...] = total.astype(BF)
    first = q * ny * W32
    terms = got_ref[:, first : first + W32, :].astype(F32) + got_ref[:, first + W32 :, :].astype(F32)
    gw_ref[...] = jnp.sum(terms, axis=0) * (1.0 / math.sqrt(q * nx * ny * B))


def ring(value, axis, size):
    out = [value]
    for d in range(1, size):
        out.append(lax.ppermute(value, axis, [(i, (i + d) % size) for i in range(size)]))
    return out


def on_device(features, weight, tiles, tile_rows, tile_live, pos_partner, neg_partner):
    q = lax.axis_size("zh")
    nx, ny = lax.axis_size("x"), lax.axis_size("y")
    xy = nx * ny
    place = jnp.stack([lax.axis_index(REP), lax.axis_index("zh"), lax.axis_index(("x", "y"))])
    place = place.astype(jnp.int32)
    shape = jax.ShapeDtypeStruct
    slots = 2 * pos_partner.shape[1]
    groups = xy * W32 // B
    pos_t, neg_t = pos_partner.T, neg_partner.T

    sent = call(
        products_kernel,
        [SMEM, SMEM, VMEM, VMEM],
        shape((q * xy, W32, B), BF),
        [pltpu.VMEM((q * xy, W32, B), F32)],
    )(tile_rows, tile_live, features.T, tiles)
    recv = lax.all_to_all(sent, ROWS, 0, 0, tiled=True)

    tables = ring(jnp.concatenate([pos_t, neg_t], axis=0), "zh", q)
    cpos, ctot = call(
        functools.partial(direct_kernel, xy),
        [SMEM] + [VMEM] * q,
        (shape((groups, q * B, B), BF), shape((groups, q * B, B), BF)),
        [pltpu.VMEM((B, B), F32), pltpu.VMEM((slots, B, B), F32)],
        flops=100000000,
    )(place, *tables)

    agg_own = call(aggregate_kernel, [VMEM], shape((W32, B), BF))(recv)
    agg = lax.all_gather(agg_own, REP, axis=0, tiled=True)
    aggs = ring(agg, "zh", q)
    emb_t, slab_part = call(
        embed_kernel,
        [SMEM] + [VMEM] * 4,
        (shape((W32, B), BF), shape((xy, W32 + 2 * slots, B), BF)),
        [pltpu.VMEM((F, B), BF), pltpu.VMEM((B, F), BF)],
    )(place, agg, weight, pos_t, neg_t)
    slab = lax.all_to_all(slab_part, ("x", "y"), 0, 0, tiled=True)
    nodes = call(nodes_kernel, [VMEM] * (1 + q), shape((q * B, F), BF))(weight, *aggs)

    pieces = call(
        functools.partial(decoder_kernel, q, xy, slots),
        [SMEM] + [VMEM] * (5 + q),
        shape((q * q, W32 + 2 * W32 // q, B), BF),
        [
            pltpu.VMEM((groups, q * B, B), F32),
            pltpu.VMEM((groups, q * B, B), BF),
            pltpu.VMEM((groups, q * B, B), BF),
        ],
    )(place, slab, nodes, weight, cpos, ctot, *aggs)
    mine = lax.all_to_all(pieces, ("zh",) + REP, 0, 0, tiled=True)

    height = pieces.shape[1]
    plane_part = call(functools.partial(owner_kernel, q), [VMEM], shape((q * ny, height, B), BF))(mine)
    lines = lax.all_to_all(plane_part, ("zh", "y"), 0, 0, tiled=True)

    line_part = call(
        functools.partial(merge_kernel, q), [VMEM], shape((nx, (q * ny + 2) * W32, B), BF)
    )(lines)
    every = lax.all_to_all(line_part, "x", 0, 0, tiled=True)

    gf_t, grad_weight = call(
        functools.partial(features_kernel, q, nx, ny),
        [SMEM, SMEM, VMEM, VMEM],
        (shape((W32, B), BF), shape((W32, F), F32)),
    )(tile_rows, tile_live, every, tiles)
    return (emb_t.T, grad_weight, gf_t.T)


def sharded(mesh):
    return jax.shard_map(
        on_device,
        mesh=mesh,
        in_specs=(
            P(ROWS, REP),
            P(),
            P(ROWS, None, None, None),
            P(ROWS, None),
            P(ROWS, None),
            P(ROWS, None),
            P(ROWS, None),
        ),
        out_specs=(P(ROWS, REP), P(REP, None), P(ROWS, REP)),
        check_vma=False,
    )


def solution(mesh):
    rows = mesh.shape["rows"]
    parts = mesh.devices.reshape(4, 4, rows // 16, 2, 2)
    return sharded(Mesh(parts, ("zh", "x", "y", "zl", "core")))
```

time: 161 us -> 172 us (1.068)
  waiting for transfers between devices: 56.9 us -> 37.7 us
  blocking collectives: 48.6 us -> 63.9 us
  starting transfers between devices: 33.7 us -> 48.9 us
    all_to_all x1, waiting for transfers between devices: 14.5 us -> 0.01 us  [on_device(): slab = lax.all_to_all(slab_part, ('x', 'y'), 0, 0, tiled=True)]
    ppermute x3 -> x6, starting transfers between devices: 8.8 us -> 23.2 us  [ring(): lax.ppermute(value, axis, [(i, (i + d) % size) for i in range(size)])]
    all_gather x0 -> x1, blocking collectives: none -> 5.19 us  [on_device(): agg = lax.all_gather(agg_own, REP, axis=0, tiled=True)]
    all_to_all x1, blocking collectives: 13.3 us -> 18.4 us  [on_device(): every = lax.all_to_all(line_part, 'x', 0, 0, tiled=True)]
    ppermute x3 -> x6, waiting for transfers between devices: 10.2 us -> 5.41 us  [ring(): lax.ppermute(value, axis, [(i, (i + d) % size) for i in range(size)])]
    all_to_all x1, blocking collectives: 22.8 us -> 26.2 us  [on_device(): lines = lax.all_to_all(plane_part, ('zh', 'y'), 0, 0, tiled=True)]
    pallas_call x6 -> x7, Pallas kernels: 15.8 us -> 15.2 us  [the longest x1 5.97 us: on_device(): call(functools.partial(direct_kernel, xy), [SMEM] + [VMEM] * q, (shape((g...]
  transfers between devices with their start and end apart: 5 -> 8, of which waited for: 5 -> 3; matrix products, arithmetic and copies ran while one was open for 0% -> 0% of each run, Pallas kernels for 3% -> 4%
where the time goes in v3:
time: 172 us
  blocking collectives  63.9 us (37%)
  starting transfers between devices  48.9 us (28%)
  waiting for transfers between devices  37.7 us (22%)
  Pallas kernels  17.3 us (10%)
  local copies, waits for them, and re-layouts  3.07 us (2%)
    all_to_all x1, waiting for transfers between devices, on_device(): recv = lax.all_to_all(sent, ROWS, 0, 0, tiled=True)  32.3 us
    all_to_all x1, blocking collectives, on_device(): lines = lax.all_to_all(plane_part, ('zh', 'y'), 0, 0, tiled=True)  26.2 us
    ppermute x6, starting transfers between devices, ring(): lax.ppermute(value, axis, [(i, (i + d) % size) for i in range(size)])  23.2 us
    all_to_all x1, starting transfers between devices, on_device(): recv = lax.all_to_all(sent, ROWS, 0, 0, tiled=True)  19.9 us
    all_to_all x1, blocking collectives, on_device(): every = lax.all_to_all(line_part, 'x', 0, 0, tiled=True)  18.4 us
    all_to_all x1, blocking collectives, on_device(): mine = lax.all_to_all(pieces, ('zh',) + REP, 0, 0, tiled=True)  14.1 us
    pallas_call x1, Pallas kernels, on_device(): call(functools.partial(direct_kernel, xy), [SMEM] + [VMEM] * q, (shape((g...  5.97 us
    all_to_all x1, starting transfers between devices, on_device(): slab = lax.all_to_all(slab_part, ('x', 'y'), 0, 0, tiled=True)  5.68 us
  transfers between devices with their start and end apart: 8, of which 3 were waited for; matrix products, arithmetic and copies ran while one was open for 0% of the time, Pallas kernels for 4%

profile of v3, /device:TPU:8, one launch (start us, length us, event | category | flops | bytes accessed | tf_op | source)
XLA Modules:
  0.0 171.7 jit_solution(18111011356471740229)
XLA Ops:
  0.6 0.0 copy-start
  0.6 1.0 copy-done
  1.7 0.0 copy-start.5
  1.7 0.7 copy-done.5
  2.4 0.0 copy-start.6
  2.4 0.7 copy-done.6
  3.0 0.0 copy-start.8
  3.0 0.7 copy-done.8
  3.7 2.0 %shard_map.94 = bf16[128,32,128]{2,1,0:T(8,128)(2,1)} custom-call(s32[1,16]{1,0:T(1,128)S(1)} %copy-done.6, s32[1,16]{1,0:T(1,128)S(1)} %copy-done.8, bf16[32,128]{1,0:T(8,128)(2,1)S(1)} %bitcast.12, bf16[1,16,128,128]{3,2,1,0:T(8,128)(2,1)S(1)} %copy-done), custom_call_target="tpu_custom_call" | custom-call | flops 1000000 | bytes 1000000 | tf_op jit(solution)/shard_map/pallas_call | solution.py:261
  5.7 0.0 copy-start.2
  5.7 0.0 copy-start.3
  5.7 0.0 copy-start.4
  5.7 19.9 %all-to-all-start = ((bf16[128,32,128]{2,1,0:T(8,128)(2,1)}), bf16[128,32,128]{2,1,0:T(8,128)(2,1)S(1)}, u32[]{:S(2)}, u32[]{:S(2)}) async-start(bf16[128,32,128]{2,1,0:T(8,128)(2,1)} %shard_map.94), calls=%async_computation | async-start | bytes 2097152 | tf_op jit(solution)/shard_map/all_to_all | solution.py:267
  25.7 0.1 pad_add_fusion.1.place_ref
  25.8 32.3 %all-to-all-done.recv_ref = bf16[128,32,128]{2,1,0:T(8,128)(2,1)S(1)} async-done(((bf16[128,32,128]{2,1,0:T(8,128)(2,1)}), bf16[128,32,128]{2,1,0:T(8,128)(2,1)S(1)}, u32[]{:S(2)}, u32[]{:S(2)}) %all-to-all-start) | async-done | bytes 1048608 | tf_op jit(solution)/shard_map/all_to_all | solution.py:267
  58.0 0.2 shard_map.95
  58.2 5.2 %all_gather.3.agg_ref.refs_0_ = bf16[128,128]{1,0:T(8,128)(2,1)S(1)} all-gather(bf16[32,128]{1,0:T(8,128)(2,1)S(1)} %shard_map.95), channel_id=1, replica_groups=mesh['zh'=4,'x'=4,'y'=8,'zl'=2,'core'=2] {'zl','core'}, dimensions={0}, use_global_device_ids=true | all-gather | bytes 40960 | tf_op jit(solution)/shard_map/all_gather | solution.py:279
  63.4 0.0 copy-done.2
  63.4 0.0 copy-done.3
  63.4 0.0 copy-done.4
  63.4 1.7 shard_map.96
  65.1 5.7 %all-to-all-start.1 = ((bf16[32,64,128]{2,1,0:T(8,128)(2,1)}), bf16[32,64,128]{2,1,0:T(8,128)(2,1)S(1)}, u32[]{:S(2)}, u32[]{:S(2)}) async-start(bf16[32,64,128]{2,1,0:T(8,128)(2,1)} %get-tuple-element.10), calls=%async_computation.1 | async-start | bytes 1048576 | tf_op jit(solution)/shard_map/all_to_all | solution.py:287
  70.7 3.3 %collective-permute-start.2 = (bf16[128,128]{1,0:T(8,128)(2,1)S(1)}, bf16[128,128]{1,0:T(8,128)(2,1)S(1)}, u32[]{:S(2)}, u32[]{:S(2)}) collective-permute-start(bf16[128,128]{1,0:T(8,128)(2,1)S(1)} %all_gather.3.agg_ref.refs_0_), channel_id=1, source_target_pairs={{0,384},{128,0},{256,128},{384,256},{1,385},{129,1},{257,129},{385... | collective-permute-start | bytes 98312 | tf_op jit(solution)/shard_map/ppermute | solution.py:246
  74.0 4.9 %collective-permute-start.1 = (bf16[128,128]{1,0:T(8,128)(2,1)S(1)}, bf16[128,128]{1,0:T(8,128)(2,1)S(1)}, u32[]{:S(2)}, u32[]{:S(2)}) collective-permute-start(bf16[128,128]{1,0:T(8,128)(2,1)S(1)} %all_gather.3.agg_ref.refs_0_), channel_id=1, source_target_pairs={{0,256},{128,384},{256,0},{384,128},{1,257},{129,385},{257,1},{385... | collective-permute-start | bytes 98312 | tf_op jit(solution)/shard_map/ppermute | solution.py:246
  79.0 1.9 %collective-permute-start = (bf16[128,128]{1,0:T(8,128)(2,1)S(1)}, bf16[128,128]{1,0:T(8,128)(2,1)S(1)}, u32[]{:S(2)}, u32[]{:S(2)}) collective-permute-start(bf16[128,128]{1,0:T(8,128)(2,1)S(1)} %all_gather.3.agg_ref.refs_0_), channel_id=1, source_target_pairs={{0,128},{128,256},{256,384},{384,0},{1,129},{129,257},{257,385},{3... | collective-permute-start | bytes 98312 | tf_op jit(solution)/shard_map/ppermute | solution.py:246
  80.9 6.0 %collective-permute-start.5 = (s32[16,128]{1,0:T(8,128)S(1)}, s32[16,128]{1,0:T(8,128)S(1)}, u32[]{:S(2)}, u32[]{:S(2)}) collective-permute-start(s32[16,128]{1,0:T(8,128)S(1)} %pad_add_fusion.refs_0_), channel_id=1, source_target_pairs={{0,384},{128,0},{256,128},{384,256},{1,385},{129,1},{257,129},{385... | collective-permute-start | bytes 24584 | tf_op jit(solution)/shard_map/ppermute | solution.py:246
  86.9 4.8 %collective-permute-start.4 = (s32[16,128]{1,0:T(8,128)S(1)}, s32[16,128]{1,0:T(8,128)S(1)}, u32[]{:S(2)}, u32[]{:S(2)}) collective-permute-start(s32[16,128]{1,0:T(8,128)S(1)} %pad_add_fusion.refs_0_), channel_id=1, source_target_pairs={{0,256},{128,384},{256,0},{384,128},{1,257},{129,385},{257,1},{385... | collective-permute-start | bytes 24584 | tf_op jit(solution)/shard_map/ppermute | solution.py:246
  91.8 0.0 collective-permute-done.5.refs_3_
  91.8 2.3 %collective-permute-start.3 = (s32[16,128]{1,0:T(8,128)S(1)}, s32[16,128]{1,0:T(8,128)S(1)}, u32[]{:S(2)}, u32[]{:S(2)}) collective-permute-start(s32[16,128]{1,0:T(8,128)S(1)} %pad_add_fusion.refs_0_), channel_id=1, source_target_pairs={{0,128},{128,256},{256,384},{384,0},{1,129},{129,257},{257,385},{3... | collective-permute-start | bytes 24584 | tf_op jit(solution)/shard_map/ppermute | solution.py:246
  94.1 2.3 %collective-permute-done.4.refs_2_ = s32[16,128]{1,0:T(8,128)S(1)} collective-permute-done((s32[16,128]{1,0:T(8,128)S(1)}, s32[16,128]{1,0:T(8,128)S(1)}, u32[]{:S(2)}, u32[]{:S(2)}) %collective-permute-start.4) | collective-permute-done | bytes 8224 | tf_op jit(solution)/shard_map/ppermute | solution.py:246
  96.4 3.1 %collective-permute-done.3.refs_1_ = s32[16,128]{1,0:T(8,128)S(1)} collective-permute-done((s32[16,128]{1,0:T(8,128)S(1)}, s32[16,128]{1,0:T(8,128)S(1)}, u32[]{:S(2)}, u32[]{:S(2)}) %collective-permute-start.3) | collective-permute-done | bytes 8224 | tf_op jit(solution)/shard_map/ppermute | solution.py:246
  99.4 6.0 %shard_map.98 = (bf16[8,512,128]{2,1,0:T(8,128)(2,1)S(1)}, bf16[8,512,128]{2,1,0:T(8,128)(2,1)S(1)}) custom-call(s32[3]{0:T(128)S(1)} %pad_add_fusion.1.place_ref, s32[16,128]{1,0:T(8,128)S(1)} %pad_add_fusion.refs_0_, s32[16,128]{1,0:T(8,128)S(1)} %collective-permute-done.3.refs_1_, s32[16,128]{1,0:T(8,128)S(1)} %collective-permute-done.4.refs_2_, ...), custom_call_target="tpu_custom_call" | custom-call | flops 100000000 | bytes 1000000 | tf_op jit(solution)/shard_map/pallas_call | solution.py:270
  105.4 0.0 collective-permute-done.2.refs_3_
  105.4 0.0 collective-permute-done.1.refs_2_
  105.4 0.0 collective-permute-done.refs_1_
  105.5 0.3 shard_map.97.en_ref
  105.8 0.0 all-to-all-done.1.got_ref
  105.8 5.6 %shard_map.99 = bf16[16,48,128]{2,1,0:T(8,128)(2,1)S(1)} custom-call(s32[3]{0:T(128)S(1)} %pad_add_fusion.1.place_ref, bf16[32,64,128]{2,1,0:T(8,128)(2,1)S(1)} %all-to-all-done.1.got_ref, bf16[512,128]{1,0:T(8,128)(2,1)S(1)} %shard_map.97.en_ref, bf16[128,128]{1,0:T(8,128)(2,1)S(1)} %copy-done.2, bf16[8,512,128]{2,1,0:T(8,128)(2,1)S(1)} %get-tuple-element.11.cpos_ref, ...), custom_call_target="tpu_custom_call" | custom-call | flops 1000000 | bytes 1000000 | tf_op jit(solution)/shard_map/pallas_call | solution.py:290
  111.4 14.1 %all_to_all.25.got_ref = bf16[16,48,128]{2,1,0:T(8,128)(2,1)S(1)} all-to-all(bf16[16,48,128]{2,1,0:T(8,128)(2,1)S(1)} %shard_map.99), channel_id=1, replica_groups=mesh['zh'=4,'x'=4,'y'=8,'zl'=2,'core'=2] {'zh','zl','core'}, dimensions={0} | all-to-all | bytes 393216 | tf_op jit(solution)/shard_map/all_to_all | solution.py:300
  125.5 26.2 %all_to_all.26.got_ref = bf16[32,48,128]{2,1,0:T(8,128)(2,1)S(1)} all-to-all(bf16[32,48,128]{2,1,0:T(8,128)(2,1)S(1)} %shard_map.100), channel_id=1, replica_groups=mesh['zh'=4,'x'=4,'y'=8,'zl'=2,'core'=2] {'zh','y'}, dimensions={0} | all-to-all | bytes 786432 | tf_op jit(solution)/shard_map/all_to_all | solution.py:304
  151.7 0.2 shard_map.101
  151.9 0.0 copy-start.1
  151.9 0.0 copy-start.7
  151.9 0.0 copy-start.9
  151.9 18.4 %all_to_all.27.got_ref = bf16[4,1088,128]{2,1,0:T(8,128)(2,1)S(1)} all-to-all(bf16[4,1088,128]{2,1,0:T(8,128)(2,1)S(1)} %shard_map.101), channel_id=1, replica_groups=mesh['zh'=4,'x'=4,'y'=8,'zl'=2,'core'=2] {'x'}, dimensions={0} | all-to-all | bytes 2228224 | tf_op jit(solution)/shard_map/all_to_all | solution.py:309
  170.3 0.0 copy-done.1
  170.3 0.0 copy-done.7
  170.3 0.0 copy-done.9
  170.3 1.4 shard_map.102
  (2 shorter events, 0.0 us)
Async XLA Ops:
  0.6 1.0 copy-start
  1.7 0.7 copy-start.5
  2.4 0.7 copy-start.6
  3.0 0.7 copy-start.8
  5.7 57.7 %copy-start.2 = (bf16[128,128]{1,0:T(8,128)(2,1)S(1)}, bf16[128,128]{1,0:T(8,128)(2,1)}, u32[]{:S(2)}) copy-start(bf16[128,128]{1,0:T(8,128)(2,1)} %w_ref.5) | copy-start | bytes 98308
  5.7 57.7 %copy-start.3 = (s32[128,8]{0,1:T(8,128)S(1)}, s32[128,8]{0,1:T(8,128)}, u32[]{:S(2)}) copy-start(s32[128,8]{0,1:T(8,128)} %param.12) | copy-start | bytes 12292
  5.7 57.7 %copy-start.4 = (s32[128,8]{0,1:T(8,128)S(1)}, s32[128,8]{0,1:T(8,128)}, u32[]{:S(2)}) copy-start(s32[128,8]{0,1:T(8,128)} %param.13) | copy-start | bytes 12292
  5.7 52.3 %all-to-all-start = ((bf16[128,32,128]{2,1,0:T(8,128)(2,1)}), bf16[128,32,128]{2,1,0:T(8,128)(2,1)S(1)}, u32[]{:S(2)}, u32[]{:S(2)}) async-start(bf16[128,32,128]{2,1,0:T(8,128)(2,1)} %shard_map.94), calls=%async_computation | async-start | bytes 2097152 | tf_op jit(solution)/shard_map/all_to_all | solution.py:267
  65.1 40.7 %all-to-all-start.1 = ((bf16[32,64,128]{2,1,0:T(8,128)(2,1)}), bf16[32,64,128]{2,1,0:T(8,128)(2,1)S(1)}, u32[]{:S(2)}, u32[]{:S(2)}) async-start(bf16[32,64,128]{2,1,0:T(8,128)(2,1)} %get-tuple-element.10), calls=%async_computation.1 | async-start | bytes 1048576 | tf_op jit(solution)/shard_map/all_to_all | solution.py:287
  70.7 34.7 %collective-permute-start.2 = (bf16[128,128]{1,0:T(8,128)(2,1)S(1)}, bf16[128,128]{1,0:T(8,128)(2,1)S(1)}, u32[]{:S(2)}, u32[]{:S(2)}) collective-permute-start(bf16[128,128]{1,0:T(8,128)(2,1)S(1)} %all_gather.3.agg_ref.refs_0_), channel_id=1, source_target_pairs={{0,384},{128,0},{256,128},{384,256},{1,385},{129,1},{257,129},{385... | collective-permute-start | bytes 98312 | tf_op jit(solution)/shard_map/ppermute | solution.py:246
  74.0 31.4 %collective-permute-start.1 = (bf16[128,128]{1,0:T(8,128)(2,1)S(1)}, bf16[128,128]{1,0:T(8,128)(2,1)S(1)}, u32[]{:S(2)}, u32[]{:S(2)}) collective-permute-start(bf16[128,128]{1,0:T(8,128)(2,1)S(1)} %all_gather.3.agg_ref.refs_0_), channel_id=1, source_target_pairs={{0,256},{128,384},{256,0},{384,128},{1,257},{129,385},{257,1},{385... | collective-permute-start | bytes 98312 | tf_op jit(solution)/shard_map/ppermute | solution.py:246
  79.0 26.5 %collective-permute-start = (bf16[128,128]{1,0:T(8,128)(2,1)S(1)}, bf16[128,128]{1,0:T(8,128)(2,1)S(1)}, u32[]{:S(2)}, u32[]{:S(2)}) collective-permute-start(bf16[128,128]{1,0:T(8,128)(2,1)S(1)} %all_gather.3.agg_ref.refs_0_), channel_id=1, source_target_pairs={{0,128},{128,256},{256,384},{384,0},{1,129},{129,257},{257,385},{3... | collective-permute-start | bytes 98312 | tf_op jit(solution)/shard_map/ppermute | solution.py:246
  80.9 10.9 %collective-permute-start.5 = (s32[16,128]{1,0:T(8,128)S(1)}, s32[16,128]{1,0:T(8,128)S(1)}, u32[]{:S(2)}, u32[]{:S(2)}) collective-permute-start(s32[16,128]{1,0:T(8,128)S(1)} %pad_add_fusion.refs_0_), channel_id=1, source_target_pairs={{0,384},{128,0},{256,128},{384,256},{1,385},{129,1},{257,129},{385... | collective-permute-start | bytes 24584 | tf_op jit(solution)/shard_map/ppermute | solution.py:246
  86.9 9.5 %collective-permute-start.4 = (s32[16,128]{1,0:T(8,128)S(1)}, s32[16,128]{1,0:T(8,128)S(1)}, u32[]{:S(2)}, u32[]{:S(2)}) collective-permute-start(s32[16,128]{1,0:T(8,128)S(1)} %pad_add_fusion.refs_0_), channel_id=1, source_target_pairs={{0,256},{128,384},{256,0},{384,128},{1,257},{129,385},{257,1},{385... | collective-permute-start | bytes 24584 | tf_op jit(solution)/shard_map/ppermute | solution.py:246
  91.8 7.7 %collective-permute-start.3 = (s32[16,128]{1,0:T(8,128)S(1)}, s32[16,128]{1,0:T(8,128)S(1)}, u32[]{:S(2)}, u32[]{:S(2)}) collective-permute-start(s32[16,128]{1,0:T(8,128)S(1)} %pad_add_fusion.refs_0_), channel_id=1, source_target_pairs={{0,128},{128,256},{256,384},{384,0},{1,129},{129,257},{257,385},{3... | collective-permute-start | bytes 24584 | tf_op jit(solution)/shard_map/ppermute | solution.py:246
  151.9 18.4 %copy-start.1 = (bf16[1,16,128,128]{3,2,1,0:T(8,128)(2,1)S(1)}, bf16[1,16,128,128]{3,2,1,0:T(8,128)(2,1)}, u32[]{:S(2)}) copy-start(bf16[1,16,128,128]{3,2,1,0:T(8,128)(2,1)} %tiles_ref.3) | copy-start | bytes 1572868
  151.9 18.4 %copy-start.7 = (s32[1,16]{1,0:T(1,128)S(1)}, s32[1,16]{1,0:T(1,128)}, u32[]{:S(2)}) copy-start(s32[1,16]{1,0:T(1,128)} %rows_ref.3) | copy-start | bytes 196
  151.9 18.4 %copy-start.9 = (s32[1,16]{1,0:T(1,128)S(1)}, s32[1,16]{1,0:T(1,128)}, u32[]{:S(2)}) copy-start(s32[1,16]{1,0:T(1,128)} %live_ref.3) | copy-start | bytes 196

commit v4 on v3

--- a/solution.py
+++ b/solution.py
@@ -18,6 +18,7 @@
 PARAMS = pltpu.CompilerParams(vmem_limit_bytes=40 * 1024 * 1024)
 VMEM = pl.BlockSpec(memory_space=pltpu.VMEM)
 SMEM = pl.BlockSpec(memory_space=pltpu.SMEM)
+ANY = pl.BlockSpec(memory_space=pl.ANY)
 
 
 def tn(a, b):
@@ -58,7 +59,11 @@
     out_ref[...] = acc[...].astype(BF)
 
 
-def aggregate_kernel(recv_ref, out_ref):
+def table_kernel(after_ref, pos_ref, neg_ref, out_ref):
+    out_ref[...] = jnp.concatenate([pos_ref[...], neg_ref[...]], axis=0)
+
+
+def aggregate_kernel(after_ref, recv_ref, out_ref):
     total = recv_ref[0].astype(F32)
     for r in range(1, recv_ref.shape[0]):
         total = total + recv_ref[r].astype(F32)
@@ -266,7 +271,8 @@
     )(tile_rows, tile_live, features.T, tiles)
     recv = lax.all_to_all(sent, ROWS, 0, 0, tiled=True)
 
-    tables = ring(jnp.concatenate([pos_t, neg_t], axis=0), "zh", q)
+    table = call(table_kernel, [ANY, VMEM, VMEM], shape((slots, B), jnp.int32))(sent, pos_t, neg_t)
+    tables = ring(table, "zh", q)
     cpos, ctot = call(
         functools.partial(direct_kernel, xy),
         [SMEM] + [VMEM] * q,
@@ -275,7 +281,7 @@
         flops=100000000,
     )(place, *tables)
 
-    agg_own = call(aggregate_kernel, [VMEM], shape((W32, B), BF))(recv)
+    agg_own = call(aggregate_kernel, [ANY, VMEM], shape((W32, B), BF))(cpos, recv)
     agg = lax.all_gather(agg_own, REP, axis=0, tiled=True)
     aggs = ring(agg, "zh", q)
     emb_t, slab_part = call(

time: 172 us -> 160 us (0.930)
  waiting for transfers between devices: 37.7 us -> 19.8 us
  starting transfers between devices: 48.9 us -> 55.9 us
  blocking collectives: 63.9 us -> 61.7 us
    all_to_all x1, waiting for transfers between devices: 32.3 us -> 6.28 us  [on_device(): recv = lax.all_to_all(sent, ROWS, 0, 0, tiled=True)]
    ppermute x6, waiting for transfers between devices: 5.41 us -> 11.6 us  [ring(): lax.ppermute(value, axis, [(i, (i + d) % size) for i in range(size)])]
    all_to_all x1, starting transfers between devices: 5.68 us -> 11.8 us  [on_device(): slab = lax.all_to_all(slab_part, ('x', 'y'), 0, 0, tiled=True)]
    all_to_all x1, waiting for transfers between devices: 0.01 us -> 1.95 us  [on_device(): slab = lax.all_to_all(slab_part, ('x', 'y'), 0, 0, tiled=True)]
    unnamed x20 -> x22, local copies, waits for them, and re-layouts: 3.07 us -> 3.88 us
  transfers between devices with their start and end apart: 8 -> 8, of which waited for: 3 -> 5; matrix products, arithmetic and copies ran while one was open for 0% -> 0% of each run, Pallas kernels for 4% -> 4%
where the time goes in v4:
time: 160 us; the launch traced here: 159 us
  blocking collectives  61.7 us (39%)
  starting transfers between devices  55.9 us (35%)
  waiting for transfers between devices  19.8 us (12%)
  Pallas kernels  17 us (11%)
  local copies, waits for them, and re-layouts  3.88 us (2%)
    all_to_all x1, blocking collectives, on_device(): lines = lax.all_to_all(plane_part, ('zh', 'y'), 0, 0, tiled=True)  25.7 us
    ppermute x6, starting transfers between devices, ring(): lax.ppermute(value, axis, [(i, (i + d) % size) for i in range(size)])  24.2 us
    all_to_all x1, starting transfers between devices, on_device(): recv = lax.all_to_all(sent, ROWS, 0, 0, tiled=True)  19.9 us
    all_to_all x1, blocking collectives, on_device(): every = lax.all_to_all(line_part, 'x', 0, 0, tiled=True)  18.4 us
    all_to_all x1, blocking collectives, on_device(): mine = lax.all_to_all(pieces, ('zh',) + REP, 0, 0, tiled=True)  12.5 us
    all_to_all x1, starting transfers between devices, on_device(): slab = lax.all_to_all(slab_part, ('x', 'y'), 0, 0, tiled=True)  11.8 us
    ppermute x6, waiting for transfers between devices, ring(): lax.ppermute(value, axis, [(i, (i + d) % size) for i in range(size)])  11.6 us
    all_to_all x1, waiting for transfers between devices, on_device(): recv = lax.all_to_all(sent, ROWS, 0, 0, tiled=True)  6.28 us
  transfers between devices with their start and end apart: 8, of which 5 were waited for; matrix products, arithmetic and copies ran while one was open for 0% of the time, Pallas kernels for 4%

profile of v4, /device:TPU:8, one launch (start us, length us, event | category | flops | bytes accessed | tf_op | source)
XLA Modules:
  0.0 159.2 jit_solution(4120088801551289909)
XLA Ops:
  0.6 0.0 copy-start
  0.6 1.0 copy-done
  1.7 0.0 copy-start.6
  1.7 0.7 copy-done.6
  2.4 0.0 copy-start.7
  2.4 0.7 copy-done.7
  3.0 0.0 copy-start.9
  3.0 0.7 copy-done.9
  3.7 2.0 %shard_map.94.after_ref = bf16[128,32,128]{2,1,0:T(8,128)(2,1)} custom-call(s32[1,16]{1,0:T(1,128)S(1)} %copy-done.7, s32[1,16]{1,0:T(1,128)S(1)} %copy-done.9, bf16[32,128]{1,0:T(8,128)(2,1)S(1)} %bitcast.12, bf16[1,16,128,128]{3,2,1,0:T(8,128)(2,1)S(1)} %copy-done), custom_call_target="tpu_custom_call" | custom-call | flops 1000000 | bytes 1000000 | tf_op jit(solution)/shard_map/pallas_call | solution.py:266
  5.7 0.0 copy-start.4
  5.7 0.0 copy-start.5
  5.7 19.9 %all-to-all-start = ((bf16[128,32,128]{2,1,0:T(8,128)(2,1)}), bf16[128,32,128]{2,1,0:T(8,128)(2,1)S(1)}, u32[]{:S(2)}, u32[]{:S(2)}) async-start(bf16[128,32,128]{2,1,0:T(8,128)(2,1)} %shard_map.94.after_ref), calls=%async_computation | async-start | bytes 2097152 | tf_op jit(solution)/shard_map/all_to_all | solution.py:272
  25.7 0.0 copy-done.4
  25.7 0.0 copy-done.5
  25.7 6.0 %collective-permute-start.2 = (s32[16,128]{1,0:T(8,128)S(1)}, s32[16,128]{1,0:T(8,128)S(1)}, u32[]{:S(2)}, u32[]{:S(2)}) collective-permute-start(s32[16,128]{1,0:T(8,128)S(1)} %shard_map.95.refs_0_), channel_id=1, source_target_pairs={{0,384},{128,0},{256,128},{384,256},{1,385},{129,1},{257,129},{385... | collective-permute-start | bytes 24584 | tf_op jit(solution)/shard_map/ppermute | solution.py:251
  31.7 3.8 %collective-permute-start.1 = (s32[16,128]{1,0:T(8,128)S(1)}, s32[16,128]{1,0:T(8,128)S(1)}, u32[]{:S(2)}, u32[]{:S(2)}) collective-permute-start(s32[16,128]{1,0:T(8,128)S(1)} %shard_map.95.refs_0_), channel_id=1, source_target_pairs={{0,256},{128,384},{256,0},{384,128},{1,257},{129,385},{257,1},{385... | collective-permute-start | bytes 24584 | tf_op jit(solution)/shard_map/ppermute | solution.py:251
  35.6 4.5 %collective-permute-start = (s32[16,128]{1,0:T(8,128)S(1)}, s32[16,128]{1,0:T(8,128)S(1)}, u32[]{:S(2)}, u32[]{:S(2)}) collective-permute-start(s32[16,128]{1,0:T(8,128)S(1)} %shard_map.95.refs_0_), channel_id=1, source_target_pairs={{0,128},{128,256},{256,384},{384,0},{1,129},{129,257},{257,385},{3... | collective-permute-start | bytes 24584 | tf_op jit(solution)/shard_map/ppermute | solution.py:251
  40.1 0.1 pad_add_fusion.place_ref
  40.2 0.0 collective-permute-done.2.refs_3_
  40.2 5.6 %collective-permute-done.1.refs_2_ = s32[16,128]{1,0:T(8,128)S(1)} collective-permute-done((s32[16,128]{1,0:T(8,128)S(1)}, s32[16,128]{1,0:T(8,128)S(1)}, u32[]{:S(2)}, u32[]{:S(2)}) %collective-permute-start.1) | collective-permute-done | bytes 8224 | tf_op jit(solution)/shard_map/ppermute | solution.py:251
  45.7 0.0 collective-permute-done.refs_1_
  45.7 6.0 %shard_map.96 = (bf16[8,512,128]{2,1,0:T(8,128)(2,1)S(1)}, bf16[8,512,128]{2,1,0:T(8,128)(2,1)S(1)}) custom-call(s32[3]{0:T(128)S(1)} %pad_add_fusion.place_ref, s32[16,128]{1,0:T(8,128)S(1)} %shard_map.95.refs_0_, s32[16,128]{1,0:T(8,128)S(1)} %collective-permute-done.refs_1_, s32[16,128]{1,0:T(8,128)S(1)} %collective-permute-done.1.refs_2_, ...), custom_call_target="tpu_custom_call" | custom-call | flops 100000000 | bytes 1000000 | tf_op jit(solution)/shard_map/pallas_call | solution.py:276
  51.7 0.0 copy-start.3
  51.7 6.3 %all-to-all-done.recv_ref = bf16[128,32,128]{2,1,0:T(8,128)(2,1)S(1)} async-done(((bf16[128,32,128]{2,1,0:T(8,128)(2,1)}), bf16[128,32,128]{2,1,0:T(8,128)(2,1)S(1)}, u32[]{:S(2)}, u32[]{:S(2)}) %all-to-all-start) | async-done | bytes 1048608 | tf_op jit(solution)/shard_map/all_to_all | solution.py:272
  58.0 0.2 shard_map.97
  58.2 5.2 %all_gather.3.agg_ref.refs_0_ = bf16[128,128]{1,0:T(8,128)(2,1)S(1)} all-gather(bf16[32,128]{1,0:T(8,128)(2,1)S(1)} %shard_map.97), channel_id=1, replica_groups=mesh['zh'=4,'x'=4,'y'=8,'zl'=2,'core'=2] {'zl','core'}, dimensions={0}, use_global_device_ids=true | all-gather | bytes 40960 | tf_op jit(solution)/shard_map/all_gather | solution.py:285
  63.4 0.0 copy-done.3
  63.4 1.3 shard_map.98
  64.7 0.0 copy-start.2
  64.7 0.8 copy-done.2
  65.5 11.8 %all-to-all-start.1 = ((bf16[32,64,128]{2,1,0:T(8,128)(2,1)}), bf16[32,64,128]{2,1,0:T(8,128)(2,1)S(1)}, u32[]{:S(2)}, u32[]{:S(2)}) async-start(bf16[32,64,128]{2,1,0:T(8,128)(2,1)} %copy-done.2), calls=%async_computation.1 | async-start | bytes 1048576 | tf_op jit(solution)/shard_map/all_to_all | solution.py:293
  77.3 2.6 %collective-permute-start.5 = (bf16[128,128]{1,0:T(8,128)(2,1)S(1)}, bf16[128,128]{1,0:T(8,128)(2,1)S(1)}, u32[]{:S(2)}, u32[]{:S(2)}) collective-permute-start(bf16[128,128]{1,0:T(8,128)(2,1)S(1)} %all_gather.3.agg_ref.refs_0_), channel_id=1, source_target_pairs={{0,384},{128,0},{256,128},{384,256},{1,385},{129,1},{257,129},{385... | collective-permute-start | bytes 98312 | tf_op jit(solution)/shard_map/ppermute | solution.py:251
  79.9 5.4 %collective-permute-start.4 = (bf16[128,128]{1,0:T(8,128)(2,1)S(1)}, bf16[128,128]{1,0:T(8,128)(2,1)S(1)}, u32[]{:S(2)}, u32[]{:S(2)}) collective-permute-start(bf16[128,128]{1,0:T(8,128)(2,1)S(1)} %all_gather.3.agg_ref.refs_0_), channel_id=1, source_target_pairs={{0,256},{128,384},{256,0},{384,128},{1,257},{129,385},{257,1},{385... | collective-permute-start | bytes 98312 | tf_op jit(solution)/shard_map/ppermute | solution.py:251
  85.3 1.9 %collective-permute-start.3 = (bf16[128,128]{1,0:T(8,128)(2,1)S(1)}, bf16[128,128]{1,0:T(8,128)(2,1)S(1)}, u32[]{:S(2)}, u32[]{:S(2)}) collective-permute-start(bf16[128,128]{1,0:T(8,128)(2,1)S(1)} %all_gather.3.agg_ref.refs_0_), channel_id=1, source_target_pairs={{0,128},{128,256},{256,384},{384,0},{1,129},{129,257},{257,385},{3... | collective-permute-start | bytes 98312 | tf_op jit(solution)/shard_map/ppermute | solution.py:251
  87.2 0.0 collective-permute-done.5.refs_3_
  87.2 2.6 %collective-permute-done.4.refs_2_ = bf16[128,128]{1,0:T(8,128)(2,1)S(1)} collective-permute-done((bf16[128,128]{1,0:T(8,128)(2,1)S(1)}, bf16[128,128]{1,0:T(8,128)(2,1)S(1)}, u32[]{:S(2)}, u32[]{:S(2)}) %collective-permute-start.4) | collective-permute-done | bytes 32800 | tf_op jit(solution)/shard_map/ppermute | solution.py:251
  89.8 3.4 %collective-permute-done.3.refs_1_ = bf16[128,128]{1,0:T(8,128)(2,1)S(1)} collective-permute-done((bf16[128,128]{1,0:T(8,128)(2,1)S(1)}, bf16[128,128]{1,0:T(8,128)(2,1)S(1)}, u32[]{:S(2)}, u32[]{:S(2)}) %collective-permute-start.3) | collective-permute-done | bytes 32800 | tf_op jit(solution)/shard_map/ppermute | solution.py:251
  93.2 0.3 shard_map.99.en_ref
  93.5 1.9 %all-to-all-done.1.got_ref = bf16[32,64,128]{2,1,0:T(8,128)(2,1)S(1)} async-done(((bf16[32,64,128]{2,1,0:T(8,128)(2,1)}), bf16[32,64,128]{2,1,0:T(8,128)(2,1)S(1)}, u32[]{:S(2)}, u32[]{:S(2)}) %all-to-all-start.1) | async-done | bytes 524320 | tf_op jit(solution)/shard_map/all_to_all | solution.py:293
  95.5 5.6 %shard_map.100 = bf16[16,48,128]{2,1,0:T(8,128)(2,1)S(1)} custom-call(s32[3]{0:T(128)S(1)} %pad_add_fusion.place_ref, bf16[32,64,128]{2,1,0:T(8,128)(2,1)S(1)} %all-to-all-done.1.got_ref, bf16[512,128]{1,0:T(8,128)(2,1)S(1)} %shard_map.99.en_ref, bf16[128,128]{1,0:T(8,128)(2,1)S(1)} %copy-done.3, ...), custom_call_target="tpu_custom_call" | custom-call | flops 1000000 | bytes 1000000 | tf_op jit(solution)/shard_map/pallas_call | solution.py:296
  101.0 12.5 %all_to_all.25.got_ref = bf16[16,48,128]{2,1,0:T(8,128)(2,1)S(1)} all-to-all(bf16[16,48,128]{2,1,0:T(8,128)(2,1)S(1)} %shard_map.100), channel_id=1, replica_groups=mesh['zh'=4,'x'=4,'y'=8,'zl'=2,'core'=2] {'zh','zl','core'}, dimensions={0} | all-to-all | bytes 393216 | tf_op jit(solution)/shard_map/all_to_all | solution.py:306
  113.5 25.7 %all_to_all.26.got_ref = bf16[32,48,128]{2,1,0:T(8,128)(2,1)S(1)} all-to-all(bf16[32,48,128]{2,1,0:T(8,128)(2,1)S(1)} %shard_map.101), channel_id=1, replica_groups=mesh['zh'=4,'x'=4,'y'=8,'zl'=2,'core'=2] {'zh','y'}, dimensions={0} | all-to-all | bytes 786432 | tf_op jit(solution)/shard_map/all_to_all | solution.py:310
  139.2 0.2 shard_map.102
  139.4 0.0 copy-start.1
  139.4 0.0 copy-start.8
  139.4 0.0 copy-start.10
  139.4 18.4 %all_to_all.27.got_ref = bf16[4,1088,128]{2,1,0:T(8,128)(2,1)S(1)} all-to-all(bf16[4,1088,128]{2,1,0:T(8,128)(2,1)S(1)} %shard_map.102), channel_id=1, replica_groups=mesh['zh'=4,'x'=4,'y'=8,'zl'=2,'core'=2] {'x'}, dimensions={0} | all-to-all | bytes 2228224 | tf_op jit(solution)/shard_map/all_to_all | solution.py:315
  157.8 0.0 copy-done.1
  157.8 0.0 copy-done.8
  157.8 0.0 copy-done.10
  157.8 1.4 shard_map.103
  (2 shorter events, 0.0 us)
Async XLA Ops:
  0.6 1.0 copy-start
  1.7 0.7 copy-start.6
  2.4 0.7 copy-start.7
  3.0 0.7 copy-start.9
  5.7 20.0 %copy-start.4 = (s32[128,8]{0,1:T(8,128)S(1)}, s32[128,8]{0,1:T(8,128)}, u32[]{:S(2)}) copy-start(s32[128,8]{0,1:T(8,128)} %param.12) | copy-start | bytes 12292
  5.7 20.0 %copy-start.5 = (s32[128,8]{0,1:T(8,128)S(1)}, s32[128,8]{0,1:T(8,128)}, u32[]{:S(2)}) copy-start(s32[128,8]{0,1:T(8,128)} %param.13) | copy-start | bytes 12292
  5.7 52.3 %all-to-all-start = ((bf16[128,32,128]{2,1,0:T(8,128)(2,1)}), bf16[128,32,128]{2,1,0:T(8,128)(2,1)S(1)}, u32[]{:S(2)}, u32[]{:S(2)}) async-start(bf16[128,32,128]{2,1,0:T(8,128)(2,1)} %shard_map.94.after_ref), calls=%async_computation | async-start | bytes 2097152 | tf_op jit(solution)/shard_map/all_to_all | solution.py:272
  25.7 14.5 %collective-permute-start.2 = (s32[16,128]{1,0:T(8,128)S(1)}, s32[16,128]{1,0:T(8,128)S(1)}, u32[]{:S(2)}, u32[]{:S(2)}) collective-permute-start(s32[16,128]{1,0:T(8,128)S(1)} %shard_map.95.refs_0_), channel_id=1, source_target_pairs={{0,384},{128,0},{256,128},{384,256},{1,385},{129,1},{257,129},{385... | collective-permute-start | bytes 24584 | tf_op jit(solution)/shard_map/ppermute | solution.py:251
  31.7 14.0 %collective-permute-start.1 = (s32[16,128]{1,0:T(8,128)S(1)}, s32[16,128]{1,0:T(8,128)S(1)}, u32[]{:S(2)}, u32[]{:S(2)}) collective-permute-start(s32[16,128]{1,0:T(8,128)S(1)} %shard_map.95.refs_0_), channel_id=1, source_target_pairs={{0,256},{128,384},{256,0},{384,128},{1,257},{129,385},{257,1},{385... | collective-permute-start | bytes 24584 | tf_op jit(solution)/shard_map/ppermute | solution.py:251
  35.6 10.2 %collective-permute-start = (s32[16,128]{1,0:T(8,128)S(1)}, s32[16,128]{1,0:T(8,128)S(1)}, u32[]{:S(2)}, u32[]{:S(2)}) collective-permute-start(s32[16,128]{1,0:T(8,128)S(1)} %shard_map.95.refs_0_), channel_id=1, source_target_pairs={{0,128},{128,256},{256,384},{384,0},{1,129},{129,257},{257,385},{3... | collective-permute-start | bytes 24584 | tf_op jit(solution)/shard_map/ppermute | solution.py:251
  51.7 11.7 %copy-start.3 = (bf16[128,128]{1,0:T(8,128)(2,1)S(1)}, bf16[128,128]{1,0:T(8,128)(2,1)}, u32[]{:S(2)}) copy-start(bf16[128,128]{1,0:T(8,128)(2,1)} %w_ref.5) | copy-start | bytes 98308
  64.7 0.8 copy-start.2
  65.5 29.9 %all-to-all-start.1 = ((bf16[32,64,128]{2,1,0:T(8,128)(2,1)}), bf16[32,64,128]{2,1,0:T(8,128)(2,1)S(1)}, u32[]{:S(2)}, u32[]{:S(2)}) async-start(bf16[32,64,128]{2,1,0:T(8,128)(2,1)} %copy-done.2), calls=%async_computation.1 | async-start | bytes 1048576 | tf_op jit(solution)/shard_map/all_to_all | solution.py:293
  77.3 9.9 %collective-permute-start.5 = (bf16[128,128]{1,0:T(8,128)(2,1)S(1)}, bf16[128,128]{1,0:T(8,128)(2,1)S(1)}, u32[]{:S(2)}, u32[]{:S(2)}) collective-permute-start(bf16[128,128]{1,0:T(8,128)(2,1)S(1)} %all_gather.3.agg_ref.refs_0_), channel_id=1, source_target_pairs={{0,384},{128,0},{256,128},{384,256},{1,385},{129,1},{257,129},{385... | collective-permute-start | bytes 98312 | tf_op jit(solution)/shard_map/ppermute | solution.py:251
  79.9 9.9 %collective-permute-start.4 = (bf16[128,128]{1,0:T(8,128)(2,1)S(1)}, bf16[128,128]{1,0:T(8,128)(2,1)S(1)}, u32[]{:S(2)}, u32[]{:S(2)}) collective-permute-start(bf16[128,128]{1,0:T(8,128)(2,1)S(1)} %all_gather.3.agg_ref.refs_0_), channel_id=1, source_target_pairs={{0,256},{128,384},{256,0},{384,128},{1,257},{129,385},{257,1},{385... | collective-permute-start | bytes 98312 | tf_op jit(solution)/shard_map/ppermute | solution.py:251
  85.3 7.9 %collective-permute-start.3 = (bf16[128,128]{1,0:T(8,128)(2,1)S(1)}, bf16[128,128]{1,0:T(8,128)(2,1)S(1)}, u32[]{:S(2)}, u32[]{:S(2)}) collective-permute-start(bf16[128,128]{1,0:T(8,128)(2,1)S(1)} %all_gather.3.agg_ref.refs_0_), channel_id=1, source_target_pairs={{0,128},{128,256},{256,384},{384,0},{1,129},{129,257},{257,385},{3... | collective-permute-start | bytes 98312 | tf_op jit(solution)/shard_map/ppermute | solution.py:251
  139.4 18.4 %copy-start.1 = (bf16[1,16,128,128]{3,2,1,0:T(8,128)(2,1)S(1)}, bf16[1,16,128,128]{3,2,1,0:T(8,128)(2,1)}, u32[]{:S(2)}) copy-start(bf16[1,16,128,128]{3,2,1,0:T(8,128)(2,1)} %tiles_ref.3) | copy-start | bytes 1572868
  139.4 18.4 %copy-start.8 = (s32[1,16]{1,0:T(1,128)S(1)}, s32[1,16]{1,0:T(1,128)}, u32[]{:S(2)}) copy-start(s32[1,16]{1,0:T(1,128)} %rows_ref.3) | copy-start | bytes 196
  139.4 18.4 %copy-start.10 = (s32[1,16]{1,0:T(1,128)S(1)}, s32[1,16]{1,0:T(1,128)}, u32[]{:S(2)}) copy-start(s32[1,16]{1,0:T(1,128)} %live_ref.3) | copy-start | bytes 196

commit v5 on v4

--- a/solution.py
+++ b/solution.py
@@ -13,7 +13,10 @@
 B = 128
 F = 128
 W32 = 32
-ROWS = ("zh", "x", "y")
+NEAR = ("x", "yl")
+FAR = ("zh", "yh")
+COLUMN = ("x", "yh", "yl")
+ROWS = ("zh",) + COLUMN
 REP = ("zl", "core")
 PARAMS = pltpu.CompilerParams(vmem_limit_bytes=40 * 1024 * 1024)
 VMEM = pl.BlockSpec(memory_space=pltpu.VMEM)
@@ -51,12 +54,28 @@
     return high, value - high
 
 
-def products_kernel(rows_ref, live_ref, feat_ref, tiles_ref, out_ref, acc):
-    acc[...] = jnp.zeros_like(acc)
-    for s in range(tiles_ref.shape[1]):
-        prod = nt(feat_ref[...], tiles_ref[0, s]) * live_ref[0, s].astype(F32)
-        acc[rows_ref[0, s]] += prod
-    out_ref[...] = acc[...].astype(BF)
+def products_kernel(nx, nh, nl, rows_ref, live_ref, feat_ref, tiles_ref, out_ref, acc):
+    out_ref[...] = jnp.zeros_like(out_ref)
+    slots = tiles_ref.shape[1]
+    places = []
+    for s in range(slots):
+        row = rows_ref[0, s]
+        plane, column = lax.div(row, nx * nh * nl), lax.rem(row, nx * nh * nl)
+        line, place = lax.div(column, nh * nl), lax.rem(column, nh * nl)
+        near = line * nl + lax.rem(place, nl)
+        places.append((near, plane * nh + lax.div(place, nl)))
+        acc[places[s]] = jnp.zeros((W32, B), F32)
+    for s in range(slots):
+        acc[places[s]] += nt(feat_ref[...], tiles_ref[0, s]) * live_ref[0, s].astype(F32)
+    for s in range(slots):
+        out_ref[places[s]] = acc[places[s]].astype(BF)
+
+
+def near_kernel(recv_ref, out_ref):
+    total = recv_ref[0].astype(F32)
+    for r in range(1, recv_ref.shape[0]):
+        total = total + recv_ref[r].astype(F32)
+    out_ref[...] = total.astype(BF)
 
 
 def table_kernel(after_ref, pos_ref, neg_ref, out_ref):
@@ -99,7 +118,7 @@
 
 
 def direct_kernel(xy, place_ref, *refs):
-    tables, (cpos_ref, ctot_ref, want_s, wide_s) = refs[:-4], refs[-4:]
+    tables, (cpos_ref, ctot_ref, want_s, wide_s) = refs[1:-4], refs[-4:]
     part, plane = place_ref[0], place_ref[1]
     slots = tables[0].shape[0]
     pk = slots // 2
@@ -213,14 +232,14 @@
 
 def merge_kernel(q, got_ref, out_ref):
     count = got_ref.shape[0]
-    ny = count // q
+    nh = count // q
     eighth = W32 // q
     blocks = got_ref[:, 0:W32, :].reshape(count * W32, B)
     rows = []
     for z in range(q):
-        total = got_ref[z * ny, W32:, :].astype(F32)
-        for y in range(1, ny):
-            total = total + got_ref[z * ny + y, W32:, :].astype(F32)
+        total = got_ref[z * nh, W32:, :].astype(F32)
+        for h in range(1, nh):
+            total = total + got_ref[z * nh + h, W32:, :].astype(F32)
         rows.append(total[:eighth] + total[eighth:])
     high, low = split(jnp.concatenate(rows, axis=0))
     for d in range(out_ref.shape[0]):
@@ -229,20 +248,21 @@
         out_ref[d, (count + 1) * W32 :, :] = low.astype(BF)
 
 
-def features_kernel(q, nx, ny, rows_ref, live_ref, got_ref, tiles_ref, gft_ref, gw_ref):
+def features_kernel(q, nx, nh, nl, rows_ref, live_ref, got_ref, tiles_ref, gft_ref, gw_ref):
     total = jnp.zeros((W32, B), F32)
     for s in range(tiles_ref.shape[1]):
         row = rows_ref[0, s]
-        plane = lax.div(row, nx * ny)
-        line = lax.rem(lax.div(row, ny), nx)
-        first = pl.multiple_of((plane * ny + lax.rem(row, ny)) * W32, W32)
+        plane, column = lax.div(row, nx * nh * nl), lax.rem(row, nx * nh * nl)
+        line, place = lax.div(column, nh * nl), lax.rem(column, nh * nl)
+        near = line * nl + lax.rem(place, nl)
+        first = pl.multiple_of((plane * nh + lax.div(place, nl)) * W32, W32)
         live = live_ref[0, s].astype(F32)
-        block = got_ref[line, pl.ds(first, W32), :].astype(F32) * live
+        block = got_ref[near, pl.ds(first, W32), :].astype(F32) * live
         total = total + nn(block.astype(BF), tiles_ref[0, s])
     gft_ref[...] = total.astype(BF)
-    first = q * ny * W32
+    first = q * nh * W32
     terms = got_ref[:, first : first + W32, :].astype(F32) + got_ref[:, first + W32 :, :].astype(F32)
-    gw_ref[...] = jnp.sum(terms, axis=0) * (1.0 / math.sqrt(q * nx * ny * B))
+    gw_ref[...] = jnp.sum(terms, axis=0) * (1.0 / math.sqrt(q * nx * nh * nl * B))
 
 
 def ring(value, axis, size):
@@ -253,10 +273,10 @@
 
 
 def on_device(features, weight, tiles, tile_rows, tile_live, pos_partner, neg_partner):
-    q = lax.axis_size("zh")
-    nx, ny = lax.axis_size("x"), lax.axis_size("y")
-    xy = nx * ny
-    place = jnp.stack([lax.axis_index(REP), lax.axis_index("zh"), lax.axis_index(("x", "y"))])
+    q, nx = lax.axis_size("zh"), lax.axis_size("x")
+    nh, nl = lax.axis_size("yh"), lax.axis_size("yl")
+    xy, near, far = nx * nh * nl, nx * nl, q * nh
+    place = jnp.stack([lax.axis_index(REP), lax.axis_index("zh"), lax.axis_index(COLUMN)])
     place = place.astype(jnp.int32)
     shape = jax.ShapeDtypeStruct
     slots = 2 * pos_partner.shape[1]
@@ -264,22 +284,24 @@
     pos_t, neg_t = pos_partner.T, neg_partner.T
 
     sent = call(
-        products_kernel,
+        functools.partial(products_kernel, nx, nh, nl),
         [SMEM, SMEM, VMEM, VMEM],
-        shape((q * xy, W32, B), BF),
-        [pltpu.VMEM((q * xy, W32, B), F32)],
+        shape((near, far, W32, B), BF),
+        [pltpu.VMEM((near, far, W32, B), F32)],
     )(tile_rows, tile_live, features.T, tiles)
-    recv = lax.all_to_all(sent, ROWS, 0, 0, tiled=True)
+    near_recv = lax.all_to_all(sent.reshape(near, far * W32, B), NEAR, 0, 0, tiled=True)
 
     table = call(table_kernel, [ANY, VMEM, VMEM], shape((slots, B), jnp.int32))(sent, pos_t, neg_t)
     tables = ring(table, "zh", q)
+    near_sum = call(near_kernel, [VMEM], shape((far * W32, B), BF))(near_recv)
+    recv = lax.all_to_all(near_sum.reshape(far, W32, B), FAR, 0, 0, tiled=True)
     cpos, ctot = call(
         functools.partial(direct_kernel, xy),
-        [SMEM] + [VMEM] * q,
+        [SMEM, ANY] + [VMEM] * q,
         (shape((groups, q * B, B), BF), shape((groups, q * B, B), BF)),
         [pltpu.VMEM((B, B), F32), pltpu.VMEM((slots, B, B), F32)],
         flops=100000000,
-    )(place, *tables)
+    )(place, near_sum, *tables)
 
     agg_own = call(aggregate_kernel, [ANY, VMEM], shape((W32, B), BF))(cpos, recv)
     agg = lax.all_gather(agg_own, REP, axis=0, tiled=True)
@@ -290,7 +312,7 @@
         (shape((W32, B), BF), shape((xy, W32 + 2 * slots, B), BF)),
         [pltpu.VMEM((F, B), BF), pltpu.VMEM((B, F), BF)],
     )(place, agg, weight, pos_t, neg_t)
-    slab = lax.all_to_all(slab_part, ("x", "y"), 0, 0, tiled=True)
+    slab = lax.all_to_all(slab_part, COLUMN, 0, 0, tiled=True)
     nodes = call(nodes_kernel, [VMEM] * (1 + q), shape((q * B, F), BF))(weight, *aggs)
 
     pieces = call(
@@ -306,16 +328,15 @@
     mine = lax.all_to_all(pieces, ("zh",) + REP, 0, 0, tiled=True)
 
     height = pieces.shape[1]
-    plane_part = call(functools.partial(owner_kernel, q), [VMEM], shape((q * ny, height, B), BF))(mine)
-    lines = lax.all_to_all(plane_part, ("zh", "y"), 0, 0, tiled=True)
-
-    line_part = call(
-        functools.partial(merge_kernel, q), [VMEM], shape((nx, (q * ny + 2) * W32, B), BF)
+    far_part = call(functools.partial(owner_kernel, q), [VMEM], shape((far, height, B), BF))(mine)
+    lines = lax.all_to_all(far_part, FAR, 0, 0, tiled=True)
+    near_part = call(
+        functools.partial(merge_kernel, q), [VMEM], shape((near, (far + 2) * W32, B), BF)
     )(lines)
-    every = lax.all_to_all(line_part, "x", 0, 0, tiled=True)
+    every = lax.all_to_all(near_part, NEAR, 0, 0, tiled=True)
 
     gf_t, grad_weight = call(
-        functools.partial(features_kernel, q, nx, ny),
+        functools.partial(features_kernel, q, nx, nh, nl),
         [SMEM, SMEM, VMEM, VMEM],
         (shape((W32, B), BF), shape((W32, F), F32)),
     )(tile_rows, tile_live, every, tiles)
@@ -342,5 +363,5 @@
 
 def solution(mesh):
     rows = mesh.shape["rows"]
-    parts = mesh.devices.reshape(4, 4, rows // 16, 2, 2)
-    return sharded(Mesh(parts, ("zh", "x", "y", "zl", "core")))
+    parts = mesh.devices.reshape(4, 4, rows // 32, 2, 2, 2)
+    return sharded(Mesh(parts, ROWS + REP))

time: 160 us -> 160 us (level)
  the two profiles are of different devices: /device:TPU:8 before, /device:TPU:16 now
where the time goes in v5:
time: 160 us; the launch traced here: 159 us
  blocking collectives  81.9 us (51%)
  starting transfers between devices  50.7 us (32%)
  Pallas kernels  16.9 us (11%)
  waiting for transfers between devices  6.03 us (4%)
  local copies, waits for them, and re-layouts  3.08 us (2%)
    ppermute x6, starting transfers between devices, ring(): lax.ppermute(value, axis, [(i, (i + d) % size) for i in range(size)])  27.7 us
    all_to_all x1, blocking collectives, on_device(): every = lax.all_to_all(near_part, NEAR, 0, 0, tiled=True)  21.3 us
    all_to_all x1, blocking collectives, on_device(): lax.all_to_all(sent.reshape(near, far * W32, B), NEAR, 0, 0, tiled=True)  20.9 us
    all_to_all x1, blocking collectives, on_device(): lines = lax.all_to_all(far_part, FAR, 0, 0, tiled=True)  19.4 us
    all_to_all x1, blocking collectives, on_device(): mine = lax.all_to_all(pieces, ('zh',) + REP, 0, 0, tiled=True)  15.1 us
    all_to_all x1, starting transfers between devices, on_device(): recv = lax.all_to_all(near_sum.reshape(far, W32, B), FAR, 0, 0, tiled=True)  15 us
    all_to_all x1, starting transfers between devices, on_device(): slab = lax.all_to_all(slab_part, COLUMN, 0, 0, tiled=True)  7.91 us
    ppermute x6, waiting for transfers between devices, ring(): lax.ppermute(value, axis, [(i, (i + d) % size) for i in range(size)])  6.03 us
  transfers between devices with their start and end apart: 8, of which 3 were waited for; matrix products, arithmetic and copies ran while one was open for 0% of the time, Pallas kernels for 4%

profile of v5, /device:TPU:16, one launch (start us, length us, event | category | flops | bytes accessed | tf_op | source)
XLA Modules:
  0.0 159.5 jit_solution(11442506450496829454)
XLA Ops:
  0.6 0.0 copy-start
  0.6 1.0 copy-done
  1.7 0.0 copy-start.5
  1.7 0.7 copy-done.5
  2.4 0.0 copy-start.6
  2.4 0.7 copy-done.6
  3.0 0.0 copy-start.8
  3.0 0.7 copy-done.8
  3.7 1.0 shard_map.94.after_ref
  4.7 20.9 %all_to_all.30.recv_ref = bf16[8,512,128]{2,1,0:T(8,128)(2,1)S(1)} all-to-all(bf16[8,512,128]{2,1,0:T(8,128)(2,1)S(1)} %bitcast.10), channel_id=1, replica_groups=mesh['zh'=4,'x'=4,'yh'=4,'yl'=2,'zl'=2,'core'=2] {'x','yl'}, dimensions={0} | all-to-all | bytes 2097152 | tf_op jit(solution)/shard_map/all_to_all | solution.py:292
  25.6 0.0 copy-start.3
  25.6 0.0 copy-start.4
  25.6 0.8 shard_map.95.refs_0_
  26.4 15.0 %all-to-all-start.1 = ((bf16[16,32,128]{2,1,0:T(8,128)(2,1)}), bf16[16,32,128]{2,1,0:T(8,128)(2,1)S(1)}, u32[]{:S(2)}, u32[]{:S(2)}) async-start(bf16[16,32,128]{2,1,0:T(8,128)(2,1)} %bitcast.7), calls=%async_computation.1 | async-start | bytes 262144 | tf_op jit(solution)/shard_map/all_to_all | solution.py:297
  41.4 0.0 copy-done.3
  41.4 0.0 copy-done.4
  41.5 0.0 copy-start.2
  41.5 4.3 %collective-permute-start = (s32[16,128]{1,0:T(8,128)S(1)}, s32[16,128]{1,0:T(8,128)S(1)}, u32[]{:S(2)}, u32[]{:S(2)}) collective-permute-start(s32[16,128]{1,0:T(8,128)S(1)} %shard_map.96.refs_1_), channel_id=1, source_target_pairs={{0,128},{128,256},{256,384},{384,0},{1,129},{129,257},{257,385},{3... | collective-permute-start | bytes 24584 | tf_op jit(solution)/shard_map/ppermute | solution.py:271
  45.8 5.5 %collective-permute-start.1 = (s32[16,128]{1,0:T(8,128)S(1)}, s32[16,128]{1,0:T(8,128)S(1)}, u32[]{:S(2)}, u32[]{:S(2)}) collective-permute-start(s32[16,128]{1,0:T(8,128)S(1)} %shard_map.96.refs_1_), channel_id=1, source_target_pairs={{0,256},{128,384},{256,0},{384,128},{1,257},{129,385},{257,1},{385... | collective-permute-start | bytes 24584 | tf_op jit(solution)/shard_map/ppermute | solution.py:271
  51.3 5.5 %collective-permute-start.2 = (s32[16,128]{1,0:T(8,128)S(1)}, s32[16,128]{1,0:T(8,128)S(1)}, u32[]{:S(2)}, u32[]{:S(2)}) collective-permute-start(s32[16,128]{1,0:T(8,128)S(1)} %shard_map.96.refs_1_), channel_id=1, source_target_pairs={{0,384},{128,0},{256,128},{384,256},{1,385},{129,1},{257,129},{385... | collective-permute-start | bytes 24584 | tf_op jit(solution)/shard_map/ppermute | solution.py:271
  56.8 0.1 pad_add_fusion.place_ref
  56.8 0.0 collective-permute-done.refs_2_
  56.8 0.0 collective-permute-done.1.refs_3_
  56.8 1.2 collective-permute-done.2.refs_4_
  58.1 6.0 %shard_map.97 = (bf16[8,512,128]{2,1,0:T(8,128)(2,1)S(1)}, bf16[8,512,128]{2,1,0:T(8,128)(2,1)S(1)}) custom-call(s32[3]{0:T(128)S(1)} %pad_add_fusion.place_ref, bf16[512,128]{1,0:T(8,128)(2,1)} %shard_map.95.refs_0_, s32[16,128]{1,0:T(8,128)S(1)} %shard_map.96.refs_1_, s32[16,128]{1,0:T(8,128)S(1)} %collective-permute-done.refs_2_, ...), custom_call_target="tpu_custom_call" | custom-call | flops 100000000 | bytes 1000000 | tf_op jit(solution)/shard_map/pallas_call | solution.py:298
  64.1 0.0 all-to-all-done.1.recv_ref
  64.1 5.2 %all_gather.3.agg_ref.refs_0_ = bf16[128,128]{1,0:T(8,128)(2,1)S(1)} all-gather(bf16[32,128]{1,0:T(8,128)(2,1)S(1)} %shard_map.98), channel_id=1, replica_groups=mesh['zh'=4,'x'=4,'yh'=4,'yl'=2,'zl'=2,'core'=2] {'zl','core'}, dimensions={0}, use_global_device_ids=true | all-gather | bytes 40960 | tf_op jit(solution)/shard_map/all_gather | solution.py:307
  69.3 0.0 copy-done.2
  69.3 1.7 %shard_map.99 = (bf16[32,128]{1,0:T(8,128)(2,1)}, bf16[32,64,128]{2,1,0:T(8,128)(2,1)}) custom-call(s32[3]{0:T(128)S(1)} %pad_add_fusion.place_ref, bf16[128,128]{1,0:T(8,128)(2,1)S(1)} %all_gather.3.agg_ref.refs_0_, bf16[128,128]{1,0:T(8,128)(2,1)S(1)} %copy-done.2, s32[8,128]{1,0:T(8,128)S(1)} %bitcast.12, s32[8,128]{1,0:T(8,128)S(1)} %bitcast.14), custom_call_target="tpu_custom_call" | custom-call | flops 1000000 | bytes 1000000 | tf_op jit(solution)/shard_map/pallas_call | solution.py:309
  71.0 7.9 %all-to-all-start.2 = ((bf16[32,64,128]{2,1,0:T(8,128)(2,1)}), bf16[32,64,128]{2,1,0:T(8,128)(2,1)S(1)}, u32[]{:S(2)}, u32[]{:S(2)}) async-start(bf16[32,64,128]{2,1,0:T(8,128)(2,1)} %get-tuple-element.11), calls=%async_computation.2 | async-start | bytes 1048576 | tf_op jit(solution)/shard_map/all_to_all | solution.py:315
  78.9 3.3 %collective-permute-start.3 = (bf16[128,128]{1,0:T(8,128)(2,1)S(1)}, bf16[128,128]{1,0:T(8,128)(2,1)S(1)}, u32[]{:S(2)}, u32[]{:S(2)}) collective-permute-start(bf16[128,128]{1,0:T(8,128)(2,1)S(1)} %all_gather.3.agg_ref.refs_0_), channel_id=1, source_target_pairs={{0,128},{128,256},{256,384},{384,0},{1,129},{129,257},{257,385},{3... | collective-permute-start | bytes 98312 | tf_op jit(solution)/shard_map/ppermute | solution.py:271
  82.2 7.3 %collective-permute-start.4 = (bf16[128,128]{1,0:T(8,128)(2,1)S(1)}, bf16[128,128]{1,0:T(8,128)(2,1)S(1)}, u32[]{:S(2)}, u32[]{:S(2)}) collective-permute-start(bf16[128,128]{1,0:T(8,128)(2,1)S(1)} %all_gather.3.agg_ref.refs_0_), channel_id=1, source_target_pairs={{0,256},{128,384},{256,0},{384,128},{1,257},{129,385},{257,1},{385... | collective-permute-start | bytes 98312 | tf_op jit(solution)/shard_map/ppermute | solution.py:271
  89.5 1.9 %collective-permute-start.5 = (bf16[128,128]{1,0:T(8,128)(2,1)S(1)}, bf16[128,128]{1,0:T(8,128)(2,1)S(1)}, u32[]{:S(2)}, u32[]{:S(2)}) collective-permute-start(bf16[128,128]{1,0:T(8,128)(2,1)S(1)} %all_gather.3.agg_ref.refs_0_), channel_id=1, source_target_pairs={{0,384},{128,0},{256,128},{384,256},{1,385},{129,1},{257,129},{385... | collective-permute-start | bytes 98312 | tf_op jit(solution)/shard_map/ppermute | solution.py:271
  91.4 0.0 collective-permute-done.3.refs_1_
  91.4 0.5 collective-permute-done.4.refs_2_
  91.9 4.3 %collective-permute-done.5.refs_3_ = bf16[128,128]{1,0:T(8,128)(2,1)S(1)} collective-permute-done((bf16[128,128]{1,0:T(8,128)(2,1)S(1)}, bf16[128,128]{1,0:T(8,128)(2,1)S(1)}, u32[]{:S(2)}, u32[]{:S(2)}) %collective-permute-start.5) | collective-permute-done | bytes 32800 | tf_op jit(solution)/shard_map/ppermute | solution.py:271
  96.2 0.3 shard_map.100.en_ref
  96.5 0.0 all-to-all-done.2.got_ref
  96.5 5.6 %shard_map.101 = bf16[16,48,128]{2,1,0:T(8,128)(2,1)S(1)} custom-call(s32[3]{0:T(128)S(1)} %pad_add_fusion.place_ref, bf16[32,64,128]{2,1,0:T(8,128)(2,1)S(1)} %all-to-all-done.2.got_ref, bf16[512,128]{1,0:T(8,128)(2,1)S(1)} %shard_map.100.en_ref, bf16[128,128]{1,0:T(8,128)(2,1)S(1)} %copy-done.2, ...), custom_call_target="tpu_custom_call" | custom-call | flops 1000000 | bytes 1000000 | tf_op jit(solution)/shard_map/pallas_call | solution.py:318
  102.1 15.1 %all_to_all.31.got_ref = bf16[16,48,128]{2,1,0:T(8,128)(2,1)S(1)} all-to-all(bf16[16,48,128]{2,1,0:T(8,128)(2,1)S(1)} %shard_map.101), channel_id=1, replica_groups=mesh['zh'=4,'x'=4,'yh'=4,'yl'=2,'zl'=2,'core'=2] {'zh','zl','core'}, dimensions={0} | all-to-all | bytes 393216 | tf_op jit(solution)/shard_map/all_to_all | solution.py:328
  117.2 19.4 %all_to_all.32.got_ref = bf16[16,48,128]{2,1,0:T(8,128)(2,1)S(1)} all-to-all(bf16[16,48,128]{2,1,0:T(8,128)(2,1)S(1)} %shard_map.102), channel_id=1, replica_groups=mesh['zh'=4,'x'=4,'yh'=4,'yl'=2,'zl'=2,'core'=2] {'zh','yh'}, dimensions={0} | all-to-all | bytes 393216 | tf_op jit(solution)/shard_map/all_to_all | solution.py:332
  136.6 0.1 shard_map.103
  136.7 0.0 copy-start.1
  136.7 0.0 copy-start.7
  136.7 0.0 copy-start.9
  136.8 21.3 %all_to_all.33.got_ref = bf16[8,576,128]{2,1,0:T(8,128)(2,1)S(1)} all-to-all(bf16[8,576,128]{2,1,0:T(8,128)(2,1)S(1)} %shard_map.103), channel_id=1, replica_groups=mesh['zh'=4,'x'=4,'yh'=4,'yl'=2,'zl'=2,'core'=2] {'x','yl'}, dimensions={0} | all-to-all | bytes 2359296 | tf_op jit(solution)/shard_map/all_to_all | solution.py:336
  158.0 0.0 copy-done.1
  158.0 0.0 copy-done.7
  158.0 0.0 copy-done.9
  158.0 1.4 shard_map.104
  (3 shorter events, 0.1 us)
Async XLA Ops:
  0.6 1.0 copy-start
  1.7 0.7 copy-start.5
  2.4 0.7 copy-start.6
  3.0 0.7 copy-start.8
  25.6 15.8 %copy-start.3 = (s32[128,8]{0,1:T(8,128)S(1)}, s32[128,8]{0,1:T(8,128)}, u32[]{:S(2)}) copy-start(s32[128,8]{0,1:T(8,128)} %param.12) | copy-start | bytes 12292
  25.6 15.8 %copy-start.4 = (s32[128,8]{0,1:T(8,128)S(1)}, s32[128,8]{0,1:T(8,128)}, u32[]{:S(2)}) copy-start(s32[128,8]{0,1:T(8,128)} %param.13) | copy-start | bytes 12292
  26.4 37.6 %all-to-all-start.1 = ((bf16[16,32,128]{2,1,0:T(8,128)(2,1)}), bf16[16,32,128]{2,1,0:T(8,128)(2,1)S(1)}, u32[]{:S(2)}, u32[]{:S(2)}) async-start(bf16[16,32,128]{2,1,0:T(8,128)(2,1)} %bitcast.7), calls=%async_computation.1 | async-start | bytes 262144 | tf_op jit(solution)/shard_map/all_to_all | solution.py:297
  41.5 27.8 %copy-start.2 = (bf16[128,128]{1,0:T(8,128)(2,1)S(1)}, bf16[128,128]{1,0:T(8,128)(2,1)}, u32[]{:S(2)}) copy-start(bf16[128,128]{1,0:T(8,128)(2,1)} %w_ref.5) | copy-start | bytes 98308
  41.5 15.3 %collective-permute-start = (s32[16,128]{1,0:T(8,128)S(1)}, s32[16,128]{1,0:T(8,128)S(1)}, u32[]{:S(2)}, u32[]{:S(2)}) collective-permute-start(s32[16,128]{1,0:T(8,128)S(1)} %shard_map.96.refs_1_), channel_id=1, source_target_pairs={{0,128},{128,256},{256,384},{384,0},{1,129},{129,257},{257,385},{3... | collective-permute-start | bytes 24584 | tf_op jit(solution)/shard_map/ppermute | solution.py:271
  45.8 11.1 %collective-permute-start.1 = (s32[16,128]{1,0:T(8,128)S(1)}, s32[16,128]{1,0:T(8,128)S(1)}, u32[]{:S(2)}, u32[]{:S(2)}) collective-permute-start(s32[16,128]{1,0:T(8,128)S(1)} %shard_map.96.refs_1_), channel_id=1, source_target_pairs={{0,256},{128,384},{256,0},{384,128},{1,257},{129,385},{257,1},{385... | collective-permute-start | bytes 24584 | tf_op jit(solution)/shard_map/ppermute | solution.py:271
  51.3 6.8 %collective-permute-start.2 = (s32[16,128]{1,0:T(8,128)S(1)}, s32[16,128]{1,0:T(8,128)S(1)}, u32[]{:S(2)}, u32[]{:S(2)}) collective-permute-start(s32[16,128]{1,0:T(8,128)S(1)} %shard_map.96.refs_1_), channel_id=1, source_target_pairs={{0,384},{128,0},{256,128},{384,256},{1,385},{129,1},{257,129},{385... | collective-permute-start | bytes 24584 | tf_op jit(solution)/shard_map/ppermute | solution.py:271
  71.0 25.5 %all-to-all-start.2 = ((bf16[32,64,128]{2,1,0:T(8,128)(2,1)}), bf16[32,64,128]{2,1,0:T(8,128)(2,1)S(1)}, u32[]{:S(2)}, u32[]{:S(2)}) async-start(bf16[32,64,128]{2,1,0:T(8,128)(2,1)} %get-tuple-element.11), calls=%async_computation.2 | async-start | bytes 1048576 | tf_op jit(solution)/shard_map/all_to_all | solution.py:315
  78.9 12.5 %collective-permute-start.3 = (bf16[128,128]{1,0:T(8,128)(2,1)S(1)}, bf16[128,128]{1,0:T(8,128)(2,1)S(1)}, u32[]{:S(2)}, u32[]{:S(2)}) collective-permute-start(bf16[128,128]{1,0:T(8,128)(2,1)S(1)} %all_gather.3.agg_ref.refs_0_), channel_id=1, source_target_pairs={{0,128},{128,256},{256,384},{384,0},{1,129},{129,257},{257,385},{3... | collective-permute-start | bytes 98312 | tf_op jit(solution)/shard_map/ppermute | solution.py:271
  82.2 9.7 %collective-permute-start.4 = (bf16[128,128]{1,0:T(8,128)(2,1)S(1)}, bf16[128,128]{1,0:T(8,128)(2,1)S(1)}, u32[]{:S(2)}, u32[]{:S(2)}) collective-permute-start(bf16[128,128]{1,0:T(8,128)(2,1)S(1)} %all_gather.3.agg_ref.refs_0_), channel_id=1, source_target_pairs={{0,256},{128,384},{256,0},{384,128},{1,257},{129,385},{257,1},{385... | collective-permute-start | bytes 98312 | tf_op jit(solution)/shard_map/ppermute | solution.py:271
  89.5 6.7 %collective-permute-start.5 = (bf16[128,128]{1,0:T(8,128)(2,1)S(1)}, bf16[128,128]{1,0:T(8,128)(2,1)S(1)}, u32[]{:S(2)}, u32[]{:S(2)}) collective-permute-start(bf16[128,128]{1,0:T(8,128)(2,1)S(1)} %all_gather.3.agg_ref.refs_0_), channel_id=1, source_target_pairs={{0,384},{128,0},{256,128},{384,256},{1,385},{129,1},{257,129},{385... | collective-permute-start | bytes 98312 | tf_op jit(solution)/shard_map/ppermute | solution.py:271
  136.7 21.3 %copy-start.1 = (bf16[1,16,128,128]{3,2,1,0:T(8,128)(2,1)S(1)}, bf16[1,16,128,128]{3,2,1,0:T(8,128)(2,1)}, u32[]{:S(2)}) copy-start(bf16[1,16,128,128]{3,2,1,0:T(8,128)(2,1)} %tiles_ref.3) | copy-start | bytes 1572868
  136.7 21.3 %copy-start.7 = (s32[1,16]{1,0:T(1,128)S(1)}, s32[1,16]{1,0:T(1,128)}, u32[]{:S(2)}) copy-start(s32[1,16]{1,0:T(1,128)} %rows_ref.3) | copy-start | bytes 196
  136.7 21.3 %copy-start.9 = (s32[1,16]{1,0:T(1,128)S(1)}, s32[1,16]{1,0:T(1,128)}, u32[]{:S(2)}) copy-start(s32[1,16]{1,0:T(1,128)} %live_ref.3) | copy-start | bytes 196

commit v6 on v5

--- a/solution.py
+++ b/solution.py
@@ -21,7 +21,6 @@
 PARAMS = pltpu.CompilerParams(vmem_limit_bytes=40 * 1024 * 1024)
 VMEM = pl.BlockSpec(memory_space=pltpu.VMEM)
 SMEM = pl.BlockSpec(memory_space=pltpu.SMEM)
-ANY = pl.BlockSpec(memory_space=pl.ANY)
 
 
 def tn(a, b):
@@ -71,32 +70,49 @@
         out_ref[places[s]] = acc[places[s]].astype(BF)
 
 
-def near_kernel(recv_ref, out_ref):
+def near_kernel(q, place_ref, recv_ref, pos_ref, neg_ref, out_ref):
+    far = out_ref.shape[0]
+    nh = far // q
     total = recv_ref[0].astype(F32)
     for r in range(1, recv_ref.shape[0]):
         total = total + recv_ref[r].astype(F32)
-    out_ref[...] = total.astype(BF)
-
-
-def table_kernel(after_ref, pos_ref, neg_ref, out_ref):
-    out_ref[...] = jnp.concatenate([pos_ref[...], neg_ref[...]], axis=0)
-
-
-def aggregate_kernel(after_ref, recv_ref, out_ref):
-    total = recv_ref[0].astype(F32)
-    for r in range(1, recv_ref.shape[0]):
-        total = total + recv_ref[r].astype(F32)
-    out_ref[...] = total.astype(BF)
-
-
-def embed_kernel(place_ref, agg_ref, w_ref, pos_ref, neg_ref, embt_ref, send_ref, et_s, e_s):
-    part, column = place_ref[0], place_ref[2]
-    et = tn(w_ref[...], agg_ref[...])
-    et_s[...] = et.astype(BF)
-    e_s[...] = et.T.astype(BF)
-    mine = pl.ds(pl.multiple_of(part * W32, W32), W32)
-    embt_ref[...] = et_s[mine, :]
-    nodes = e_s[mine, :]
+    total = total.astype(BF)
+    ids = jnp.concatenate([pos_ref[...], neg_ref[...]], axis=0)
+    block = lax.shift_right_logical(ids, 7)
+    table = jnp.where(lax.rem(place_ref[0], 2) == 0, block, ids - block * B).astype(F32).astype(BF)
+    for d in range(far):
+        h = d % nh
+        for b in range(q):
+            first = (b * nh + h) * W32
+            out_ref[d, b * W32 : (b + 1) * W32, :] = total[first : first + W32]
+        out_ref[d, q * W32 :, :] = table
+
+
+def aggregate_kernel(q, place_ref, recv_ref, out_ref):
+    far = recv_ref.shape[0]
+    nh = far // q
+    slots = recv_ref.shape[1] - q * W32
+    total = recv_ref[0, 0 : q * W32, :].astype(F32)
+    for r in range(1, far):
+        total = total + recv_ref[r, 0 : q * W32, :].astype(F32)
+    out_ref[0 : q * W32, :] = total.astype(BF)
+    for b in range(q):
+        first = q * W32 + b * slots
+        out_ref[first : first + slots, :] = recv_ref[b * nh + place_ref[3], q * W32 :, :]
+
+
+def embed_kernel(
+    q, place_ref, got_ref, w_ref, pos_ref, neg_ref, nodes_ref, agg_ref, embt_ref, send_ref, et_s
+):
+    part, plane, column = place_ref[0], place_ref[1], place_ref[2]
+    for b in range(q):
+        for p in range(q):
+            agg_ref[b, p * W32 : (p + 1) * W32, :] = got_ref[p, b * W32 : (b + 1) * W32, :]
+        et = tn(w_ref[...], agg_ref[b])
+        et_s[b] = et.astype(BF)
+        nodes_ref[b * B : (b + 1) * B, :] = et.T.astype(BF)
+    embt_ref[...] = et_s[plane, pl.ds(pl.multiple_of(part * W32, W32), W32), :]
+    nodes = nodes_ref[pl.ds(pl.multiple_of(plane * B + part * W32, W32), W32), :]
     ids = jnp.concatenate([pos_ref[...], neg_ref[...]], axis=0)
     block = lax.shift_right_logical(ids, 7)
     table = jnp.concatenate([block, ids - block * B], axis=0).astype(F32)
@@ -111,25 +127,18 @@
         send_ref[d, W32:, :] = partners
 
 
-def nodes_kernel(w_ref, *refs):
-    aggs, out_ref = refs[:-1], refs[-1]
-    for d, agg_ref in enumerate(aggs):
-        out_ref[d * B : (d + 1) * B, :] = tn(w_ref[...], agg_ref[...]).T.astype(BF)
-
-
-def direct_kernel(xy, place_ref, *refs):
-    tables, (cpos_ref, ctot_ref, want_s, wide_s) = refs[1:-4], refs[-4:]
+def direct_kernel(q, xy, slots, place_ref, got_ref, cpos_ref, ctot_ref, want_s, wide_s):
     part, plane = place_ref[0], place_ref[1]
-    slots = tables[0].shape[0]
     pk = slots // 2
     lane = lax.broadcasted_iota(jnp.int32, (B, B), 1).astype(F32)
-    for d, table_ref in enumerate(tables):
-        ids = table_ref[...]
-        block = lax.shift_right_logical(ids, 7)
-        piece = block - plane * xy
-        place = ids - block * B - part * W32
-        inside = (piece >= 0) & (piece < xy) & (place >= 0) & (place < W32)
-        want = jnp.where(inside, piece * W32 + place, -1).astype(F32)
+    first_block = (plane * xy).astype(F32)
+    first_place = (part * W32).astype(F32)
+    for d in range(q):
+        rows = slice(q * W32 + d * slots, q * W32 + (d + 1) * slots)
+        piece = got_ref[0, rows, :].astype(F32) - first_block
+        place = got_ref[1, rows, :].astype(F32) - first_place
+        inside = (piece >= 0.0) & (piece < float(xy)) & (place >= 0.0) & (place < float(W32))
+        want = jnp.where(inside, piece * W32 + place, -1.0)
         want_s[...] = jnp.concatenate([want, jnp.zeros((B - slots, B), F32)], axis=0).T
         for k in range(slots):
             wide_s[k] = jnp.broadcast_to(want_s[:, k : k + 1], (B, B))
@@ -148,10 +157,12 @@
         lax.fori_loop(0, cpos_ref.shape[0], step, 0)
 
 
-def decoder_kernel(q, xy, slots, place_ref, got_ref, en_ref, w_ref, cpos_ref, ctot_ref, *refs):
-    aggs, (out_ref, logit_s, high_s, low_s) = refs[:q], refs[q:]
+def decoder_kernel(
+    q, xy, slots, place_ref, got_ref, en_ref, agg_ref, w_ref, cpos_ref, ctot_ref,
+    out_ref, logit_s, high_s, low_s,
+):
     pk = slots // 2
-    plane, column = place_ref[1], place_ref[2]
+    column = place_ref[2]
     quarters = B // W32
     groups = got_ref.shape[0] // quarters
     tile = 16
@@ -171,7 +182,7 @@
         for j in range(1, quarters):
             table = table + got_ref[g * quarters + j, W32:, :].astype(F32)
         for d in range(q):
-            block = lax.rem(plane - d + q, q) * xy + column
+            block = d * xy + column
             code = jnp.where(table[:slots] == block.astype(F32), table[slots:], -1.0)
             wide = [
                 jnp.broadcast_to(code[k : k + 1], (tile, B)).astype(BF) for k in range(slots)
@@ -204,16 +215,13 @@
     terms = jnp.zeros((F, F), F32)
     for d in range(q):
         rows = slice(d * B, (d + 1) * B)
-        terms = terms + nn(aggs[d][...], high[rows]) + nn(aggs[d][...], low[rows])
+        terms = terms + nn(agg_ref[d], high[rows]) + nn(agg_ref[d], low[rows])
     thigh, tlow = split(terms)
     eighth = W32 // q
-    for d in range(q):
-        z = lax.rem(plane - d + q, q)
-        for p in range(q):
-            cols = grad_agg[p * W32 : (p + 1) * W32, d * B : (d + 1) * B]
-            out_ref[z * q + p, 0:W32, :] = cols.astype(BF)
     for z in range(q):
         for p in range(q):
+            cols = grad_agg[p * W32 : (p + 1) * W32, z * B : (z + 1) * B]
+            out_ref[z * q + p, 0:W32, :] = cols.astype(BF)
             first = p * W32 + z * eighth
             piece = [thigh[first : first + eighth], tlow[first : first + eighth]]
             out_ref[z * q + p, W32:, :] = jnp.concatenate(piece, axis=0).astype(BF)
@@ -265,19 +273,12 @@
     gw_ref[...] = jnp.sum(terms, axis=0) * (1.0 / math.sqrt(q * nx * nh * nl * B))
 
 
-def ring(value, axis, size):
-    out = [value]
-    for d in range(1, size):
-        out.append(lax.ppermute(value, axis, [(i, (i + d) % size) for i in range(size)]))
-    return out
-
-
 def on_device(features, weight, tiles, tile_rows, tile_live, pos_partner, neg_partner):
     q, nx = lax.axis_size("zh"), lax.axis_size("x")
     nh, nl = lax.axis_size("yh"), lax.axis_size("yl")
     xy, near, far = nx * nh * nl, nx * nl, q * nh
-    place = jnp.stack([lax.axis_index(REP), lax.axis_index("zh"), lax.axis_index(COLUMN)])
-    place = place.astype(jnp.int32)
+    axes = (REP, "zh", COLUMN, "yh")
+    place = jnp.stack([lax.axis_index(axis) for axis in axes]).astype(jnp.int32)
     shape = jax.ShapeDtypeStruct
     slots = 2 * pos_partner.shape[1]
     groups = xy * W32 // B
@@ -291,40 +292,47 @@
     )(tile_rows, tile_live, features.T, tiles)
     near_recv = lax.all_to_all(sent.reshape(near, far * W32, B), NEAR, 0, 0, tiled=True)
 
-    table = call(table_kernel, [ANY, VMEM, VMEM], shape((slots, B), jnp.int32))(sent, pos_t, neg_t)
-    tables = ring(table, "zh", q)
-    near_sum = call(near_kernel, [VMEM], shape((far * W32, B), BF))(near_recv)
-    recv = lax.all_to_all(near_sum.reshape(far, W32, B), FAR, 0, 0, tiled=True)
+    far_part = call(
+        functools.partial(near_kernel, q),
+        [SMEM] + [VMEM] * 3,
+        shape((far, q * W32 + slots, B), BF),
+    )(place, near_recv, pos_t, neg_t)
+    recv = lax.all_to_all(far_part, FAR, 0, 0, tiled=True)
+    own = call(
+        functools.partial(aggregate_kernel, q), [SMEM, VMEM], shape((q * (W32 + slots), B), BF)
+    )(place, recv)
+    blocks = lax.all_gather(own, REP, axis=0)
+
+    nodes, agg, emb_t, slab_part = call(
+        functools.partial(embed_kernel, q),
+        [SMEM] + [VMEM] * 4,
+        (
+            shape((q * B, F), BF),
+            shape((q, F, B), BF),
+            shape((W32, B), BF),
+            shape((xy, W32 + 2 * slots, B), BF),
+        ),
+        [pltpu.VMEM((q, F, B), BF)],
+    )(place, blocks, weight, pos_t, neg_t)
+    slab = lax.all_to_all(slab_part, COLUMN, 0, 0, tiled=True)
     cpos, ctot = call(
-        functools.partial(direct_kernel, xy),
-        [SMEM, ANY] + [VMEM] * q,
+        functools.partial(direct_kernel, q, xy, slots),
+        [SMEM, VMEM],
         (shape((groups, q * B, B), BF), shape((groups, q * B, B), BF)),
         [pltpu.VMEM((B, B), F32), pltpu.VMEM((slots, B, B), F32)],
         flops=100000000,
-    )(place, near_sum, *tables)
-
-    agg_own = call(aggregate_kernel, [ANY, VMEM], shape((W32, B), BF))(cpos, recv)
-    agg = lax.all_gather(agg_own, REP, axis=0, tiled=True)
-    aggs = ring(agg, "zh", q)
-    emb_t, slab_part = call(
-        embed_kernel,
-        [SMEM] + [VMEM] * 4,
-        (shape((W32, B), BF), shape((xy, W32 + 2 * slots, B), BF)),
-        [pltpu.VMEM((F, B), BF), pltpu.VMEM((B, F), BF)],
-    )(place, agg, weight, pos_t, neg_t)
-    slab = lax.all_to_all(slab_part, COLUMN, 0, 0, tiled=True)
-    nodes = call(nodes_kernel, [VMEM] * (1 + q), shape((q * B, F), BF))(weight, *aggs)
+    )(place, blocks)
 
     pieces = call(
         functools.partial(decoder_kernel, q, xy, slots),
-        [SMEM] + [VMEM] * (5 + q),
+        [SMEM] + [VMEM] * 6,
         shape((q * q, W32 + 2 * W32 // q, B), BF),
         [
             pltpu.VMEM((groups, q * B, B), F32),
             pltpu.VMEM((groups, q * B, B), BF),
             pltpu.VMEM((groups, q * B, B), BF),
         ],
-    )(place, slab, nodes, weight, cpos, ctot, *aggs)
+    )(place, slab, nodes, agg, weight, cpos, ctot)
     mine = lax.all_to_all(pieces, ("zh",) + REP, 0, 0, tiled=True)
 
     height = pieces.shape[1]

time: 160 us -> 153 us (0.956)
  the two profiles are of different devices: /device:TPU:16 before, /device:TPU:8 now
where the time goes in v6:
time: 153 us
  blocking collectives  90.6 us (59%)
  waiting for transfers between devices  23.1 us (15%)
  Pallas kernels  18.1 us (12%)
  starting transfers between devices  17 us (11%)
  local copies, waits for them, and re-layouts  3.08 us (2%)
    all_to_all x1, blocking collectives, on_device(): recv = lax.all_to_all(far_part, FAR, 0, 0, tiled=True)  35.7 us
    all_to_all x1, blocking collectives, on_device(): every = lax.all_to_all(near_part, NEAR, 0, 0, tiled=True)  19.3 us
    all_to_all x1, blocking collectives, on_device(): lines = lax.all_to_all(far_part, FAR, 0, 0, tiled=True)  16.7 us
    all_to_all x1, blocking collectives, on_device(): mine = lax.all_to_all(pieces, ('zh',) + REP, 0, 0, tiled=True)  13.2 us
    all_to_all x1, waiting for transfers between devices, on_device(): slab = lax.all_to_all(slab_part, COLUMN, 0, 0, tiled=True)  12.2 us
    all_to_all x1, waiting for transfers between devices, on_device(): lax.all_to_all(sent.reshape(near, far * W32, B), NEAR, 0, 0, tiled=True)  10.9 us
    all_to_all x1, starting transfers between devices, on_device(): lax.all_to_all(sent.reshape(near, far * W32, B), NEAR, 0, 0, tiled=True)  9.41 us
    all_to_all x1, starting transfers between devices, on_device(): slab = lax.all_to_all(slab_part, COLUMN, 0, 0, tiled=True)  7.55 us
  transfers between devices with their start and end apart: 2, of which 2 were waited for; matrix products, arithmetic and copies ran while one was open for 0% of the time, Pallas kernels for 4%

profile of v6, /device:TPU:8, one launch (start us, length us, event | category | flops | bytes accessed | tf_op | source)
XLA Modules:
  0.0 152.7 jit_solution(16229932405388621658)
XLA Ops:
  0.6 0.0 copy-start
  0.6 1.0 copy-done
  1.7 0.0 copy-start.5
  1.7 0.7 copy-done.5
  2.4 0.0 copy-start.6
  2.4 0.7 copy-done.6
  3.0 0.0 copy-start.8
  3.0 0.7 copy-done.8
  3.7 2.0 %shard_map.94 = bf16[8,16,32,128]{3,2,1,0:T(8,128)(2,1)} custom-call(s32[1,16]{1,0:T(1,128)S(1)} %copy-done.6, s32[1,16]{1,0:T(1,128)S(1)} %copy-done.8, bf16[32,128]{1,0:T(8,128)(2,1)S(1)} %bitcast.17, bf16[1,16,128,128]{3,2,1,0:T(8,128)(2,1)S(1)} %copy-done), custom_call_target="tpu_custom_call" | custom-call | flops 1000000 | bytes 1000000 | tf_op jit(solution)/shard_map/pallas_call | solution.py:287
  5.7 0.0 copy-start.3
  5.7 0.0 copy-start.4
  5.7 9.4 %all-to-all-start = ((bf16[8,512,128]{2,1,0:T(8,128)(2,1)}), bf16[8,512,128]{2,1,0:T(8,128)(2,1)S(1)}, u32[]{:S(2)}, u32[]{:S(2)}) async-start(bf16[8,512,128]{2,1,0:T(8,128)(2,1)} %bitcast.5), calls=%async_computation | async-start | bytes 2097152 | tf_op jit(solution)/shard_map/all_to_all | solution.py:293
  15.1 0.1 pad_add_fusion.place_ref
  15.2 10.9 %all-to-all-done.recv_ref = bf16[8,512,128]{2,1,0:T(8,128)(2,1)S(1)} async-done(((bf16[8,512,128]{2,1,0:T(8,128)(2,1)}), bf16[8,512,128]{2,1,0:T(8,128)(2,1)S(1)}, u32[]{:S(2)}, u32[]{:S(2)}) %all-to-all-start) | async-done | bytes 1048608 | tf_op jit(solution)/shard_map/all_to_all | solution.py:293
  26.1 0.0 copy-done.3
  26.1 0.0 copy-done.4
  26.1 0.7 shard_map.95
  26.8 0.0 copy-start.2
  26.8 35.7 %all_to_all.30.recv_ref = bf16[16,144,128]{2,1,0:T(8,128)(2,1)S(1)} all-to-all(bf16[16,144,128]{2,1,0:T(8,128)(2,1)S(1)} %shard_map.95), channel_id=1, replica_groups=mesh['zh'=4,'x'=4,'yh'=4,'yl'=2,'zl'=2,'core'=2] {'zh','yh'}, dimensions={0} | all-to-all | bytes 1179648 | tf_op jit(solution)/shard_map/all_to_all | solution.py:300
  62.5 0.6 shard_map.96
  63.1 5.6 %all-gather = bf16[768,128]{1,0:T(8,128)(2,1)S(1)} all-gather(bf16[192,128]{1,0:T(8,128)(2,1)S(1)} %shard_map.96), channel_id=2, replica_groups=mesh['zh'=4,'x'=4,'yh'=4,'yl'=2,'zl'=2,'core'=2] {'zl','core'}, dimensions={0}, use_global_device_ids=true | all-gather | bytes 245760 | tf_op jit(solution)/shard_map/all_gather | solution.py:304
  68.8 0.0 copy-done.2
  68.8 1.7 %shard_map.97 = (bf16[512,128]{1,0:T(8,128)(2,1)S(1)}, bf16[4,128,128]{2,1,0:T(8,128)(2,1)S(1)}, bf16[32,128]{1,0:T(8,128)(2,1)}, bf16[32,64,128]{2,1,0:T(8,128)(2,1)}) custom-call(s32[4]{0:T(128)S(1)} %pad_add_fusion.place_ref, bf16[4,192,128]{2,1,0:T(8,128)(2,1)S(1)} %bitcast.11, bf16[128,128]{1,0:T(8,128)(2,1)S(1)} %copy-done.2, s32[8,128]{1,0:T(8,128)S(1)} %bitcast.14, ...), custom_call_target="tpu_custom_call" | custom-call | flops 1000000 | bytes 1000000 | tf_op jit(solution)/shard_map/pallas_call | solution.py:306
  70.5 7.6 %all-to-all-start.2 = ((bf16[32,64,128]{2,1,0:T(8,128)(2,1)}), bf16[32,64,128]{2,1,0:T(8,128)(2,1)S(1)}, u32[]{:S(2)}, u32[]{:S(2)}) async-start(bf16[32,64,128]{2,1,0:T(8,128)(2,1)} %get-tuple-element.12), calls=%async_computation.2 | async-start | bytes 1048576 | tf_op jit(solution)/shard_map/all_to_all | solution.py:317
  78.0 6.0 %shard_map.98 = (bf16[8,512,128]{2,1,0:T(8,128)(2,1)S(1)}, bf16[8,512,128]{2,1,0:T(8,128)(2,1)S(1)}) custom-call(s32[4]{0:T(128)S(1)} %pad_add_fusion.place_ref, bf16[4,192,128]{2,1,0:T(8,128)(2,1)S(1)} %bitcast.12), custom_call_target="tpu_custom_call" | custom-call | flops 100000000 | bytes 1000000 | tf_op jit(solution)/shard_map/pallas_call | solution.py:318
  84.0 12.2 %all-to-all-done.2.got_ref = bf16[32,64,128]{2,1,0:T(8,128)(2,1)S(1)} async-done(((bf16[32,64,128]{2,1,0:T(8,128)(2,1)}), bf16[32,64,128]{2,1,0:T(8,128)(2,1)S(1)}, u32[]{:S(2)}, u32[]{:S(2)}) %all-to-all-start.2) | async-done | bytes 524320 | tf_op jit(solution)/shard_map/all_to_all | solution.py:317
  96.2 5.6 %shard_map.99 = bf16[16,48,128]{2,1,0:T(8,128)(2,1)S(1)} custom-call(s32[4]{0:T(128)S(1)} %pad_add_fusion.place_ref, bf16[32,64,128]{2,1,0:T(8,128)(2,1)S(1)} %all-to-all-done.2.got_ref, bf16[512,128]{1,0:T(8,128)(2,1)S(1)} %get-tuple-element.13.en_ref, bf16[4,128,128]{2,1,0:T(8,128)(2,1)S(1)} %get-tuple-element.14.agg_ref, bf16[128,128]{1,0:T(8,128)(2,1)S(1)} %copy-done.2, ...), custom_call_target="tpu_custom_call" | custom-call | flops 1000000 | bytes 1000000 | tf_op jit(solution)/shard_map/pallas_call | solution.py:326
  101.8 13.2 %all_to_all.31.got_ref = bf16[16,48,128]{2,1,0:T(8,128)(2,1)S(1)} all-to-all(bf16[16,48,128]{2,1,0:T(8,128)(2,1)S(1)} %shard_map.99), channel_id=1, replica_groups=mesh['zh'=4,'x'=4,'yh'=4,'yl'=2,'zl'=2,'core'=2] {'zh','zl','core'}, dimensions={0} | all-to-all | bytes 393216 | tf_op jit(solution)/shard_map/all_to_all | solution.py:336
  115.0 16.7 %all_to_all.32.got_ref = bf16[16,48,128]{2,1,0:T(8,128)(2,1)S(1)} all-to-all(bf16[16,48,128]{2,1,0:T(8,128)(2,1)S(1)} %shard_map.100), channel_id=1, replica_groups=mesh['zh'=4,'x'=4,'yh'=4,'yl'=2,'zl'=2,'core'=2] {'zh','yh'}, dimensions={0} | all-to-all | bytes 393216 | tf_op jit(solution)/shard_map/all_to_all | solution.py:340
  131.7 0.1 shard_map.101
  131.9 0.0 copy-start.1
  131.9 0.0 copy-start.7
  131.9 0.0 copy-start.9
  131.9 19.3 %all_to_all.33.got_ref = bf16[8,576,128]{2,1,0:T(8,128)(2,1)S(1)} all-to-all(bf16[8,576,128]{2,1,0:T(8,128)(2,1)S(1)} %shard_map.101), channel_id=1, replica_groups=mesh['zh'=4,'x'=4,'yh'=4,'yl'=2,'zl'=2,'core'=2] {'x','yl'}, dimensions={0} | all-to-all | bytes 2359296 | tf_op jit(solution)/shard_map/all_to_all | solution.py:344
  151.2 0.0 copy-done.1
  151.2 0.0 copy-done.7
  151.2 0.0 copy-done.9
  151.2 1.4 shard_map.102
  (1 shorter events, 0.0 us)
Async XLA Ops:
  0.6 1.0 copy-start
  1.7 0.7 copy-start.5
  2.4 0.7 copy-start.6
  3.0 0.7 copy-start.8
  5.7 20.4 %copy-start.3 = (s32[128,8]{0,1:T(8,128)S(1)}, s32[128,8]{0,1:T(8,128)}, u32[]{:S(2)}) copy-start(s32[128,8]{0,1:T(8,128)} %param.12) | copy-start | bytes 12292
  5.7 20.4 %copy-start.4 = (s32[128,8]{0,1:T(8,128)S(1)}, s32[128,8]{0,1:T(8,128)}, u32[]{:S(2)}) copy-start(s32[128,8]{0,1:T(8,128)} %param.13) | copy-start | bytes 12292
  5.7 20.4 %all-to-all-start = ((bf16[8,512,128]{2,1,0:T(8,128)(2,1)}), bf16[8,512,128]{2,1,0:T(8,128)(2,1)S(1)}, u32[]{:S(2)}, u32[]{:S(2)}) async-start(bf16[8,512,128]{2,1,0:T(8,128)(2,1)} %bitcast.5), calls=%async_computation | async-start | bytes 2097152 | tf_op jit(solution)/shard_map/all_to_all | solution.py:293
  26.8 42.0 %copy-start.2 = (bf16[128,128]{1,0:T(8,128)(2,1)S(1)}, bf16[128,128]{1,0:T(8,128)(2,1)}, u32[]{:S(2)}) copy-start(bf16[128,128]{1,0:T(8,128)(2,1)} %w_ref.3) | copy-start | bytes 98308
  70.5 25.7 %all-to-all-start.2 = ((bf16[32,64,128]{2,1,0:T(8,128)(2,1)}), bf16[32,64,128]{2,1,0:T(8,128)(2,1)S(1)}, u32[]{:S(2)}, u32[]{:S(2)}) async-start(bf16[32,64,128]{2,1,0:T(8,128)(2,1)} %get-tuple-element.12), calls=%async_computation.2 | async-start | bytes 1048576 | tf_op jit(solution)/shard_map/all_to_all | solution.py:317
  131.9 19.4 %copy-start.1 = (bf16[1,16,128,128]{3,2,1,0:T(8,128)(2,1)S(1)}, bf16[1,16,128,128]{3,2,1,0:T(8,128)(2,1)}, u32[]{:S(2)}) copy-start(bf16[1,16,128,128]{3,2,1,0:T(8,128)(2,1)} %tiles_ref.3) | copy-start | bytes 1572868
  131.9 19.4 %copy-start.7 = (s32[1,16]{1,0:T(1,128)S(1)}, s32[1,16]{1,0:T(1,128)}, u32[]{:S(2)}) copy-start(s32[1,16]{1,0:T(1,128)} %rows_ref.3) | copy-start | bytes 196
  131.9 19.4 %copy-start.9 = (s32[1,16]{1,0:T(1,128)S(1)}, s32[1,16]{1,0:T(1,128)}, u32[]{:S(2)}) copy-start(s32[1,16]{1,0:T(1,128)} %live_ref.3) | copy-start | bytes 196

commit v7 on v6

--- a/solution.py
+++ b/solution.py
@@ -70,9 +70,14 @@
         out_ref[places[s]] = acc[places[s]].astype(BF)
 
 
-def near_kernel(q, place_ref, recv_ref, pos_ref, neg_ref, out_ref):
-    far = out_ref.shape[0]
-    nh = far // q
+def near_kernel(recv_ref, out_ref):
+    total = recv_ref[0].astype(F32)
+    for r in range(1, recv_ref.shape[0]):
+        total = total + recv_ref[r].astype(F32)
+    out_ref[...] = total.astype(BF)
+
+
+def aggregate_kernel(place_ref, recv_ref, pos_ref, neg_ref, out_ref):
     total = recv_ref[0].astype(F32)
     for r in range(1, recv_ref.shape[0]):
         total = total + recv_ref[r].astype(F32)
@@ -80,25 +85,9 @@
     ids = jnp.concatenate([pos_ref[...], neg_ref[...]], axis=0)
     block = lax.shift_right_logical(ids, 7)
     table = jnp.where(lax.rem(place_ref[0], 2) == 0, block, ids - block * B).astype(F32).astype(BF)
-    for d in range(far):
-        h = d % nh
-        for b in range(q):
-            first = (b * nh + h) * W32
-            out_ref[d, b * W32 : (b + 1) * W32, :] = total[first : first + W32]
-        out_ref[d, q * W32 :, :] = table
-
-
-def aggregate_kernel(q, place_ref, recv_ref, out_ref):
-    far = recv_ref.shape[0]
-    nh = far // q
-    slots = recv_ref.shape[1] - q * W32
-    total = recv_ref[0, 0 : q * W32, :].astype(F32)
-    for r in range(1, far):
-        total = total + recv_ref[r, 0 : q * W32, :].astype(F32)
-    out_ref[0 : q * W32, :] = total.astype(BF)
-    for b in range(q):
-        first = q * W32 + b * slots
-        out_ref[first : first + slots, :] = recv_ref[b * nh + place_ref[3], q * W32 :, :]
+    for d in range(out_ref.shape[0]):
+        out_ref[d, 0:W32, :] = total
+        out_ref[d, W32:, :] = table
 
 
 def embed_kernel(
@@ -107,7 +96,7 @@
     part, plane, column = place_ref[0], place_ref[1], place_ref[2]
     for b in range(q):
         for p in range(q):
-            agg_ref[b, p * W32 : (p + 1) * W32, :] = got_ref[p, b * W32 : (b + 1) * W32, :]
+            agg_ref[b, p * W32 : (p + 1) * W32, :] = got_ref[b * q + p, 0:W32, :]
         et = tn(w_ref[...], agg_ref[b])
         et_s[b] = et.astype(BF)
         nodes_ref[b * B : (b + 1) * B, :] = et.T.astype(BF)
@@ -134,9 +123,8 @@
     first_block = (plane * xy).astype(F32)
     first_place = (part * W32).astype(F32)
     for d in range(q):
-        rows = slice(q * W32 + d * slots, q * W32 + (d + 1) * slots)
-        piece = got_ref[0, rows, :].astype(F32) - first_block
-        place = got_ref[1, rows, :].astype(F32) - first_place
+        piece = got_ref[d * q, W32:, :].astype(F32) - first_block
+        place = got_ref[d * q + 1, W32:, :].astype(F32) - first_place
         inside = (piece >= 0.0) & (piece < float(xy)) & (place >= 0.0) & (place < float(W32))
         want = jnp.where(inside, piece * W32 + place, -1.0)
         want_s[...] = jnp.concatenate([want, jnp.zeros((B - slots, B), F32)], axis=0).T
@@ -249,11 +237,10 @@
         for h in range(1, nh):
             total = total + got_ref[z * nh + h, W32:, :].astype(F32)
         rows.append(total[:eighth] + total[eighth:])
-    high, low = split(jnp.concatenate(rows, axis=0))
+    terms = jnp.concatenate(rows, axis=0).astype(BF)
     for d in range(out_ref.shape[0]):
         out_ref[d, 0 : count * W32, :] = blocks
-        out_ref[d, count * W32 : (count + 1) * W32, :] = high.astype(BF)
-        out_ref[d, (count + 1) * W32 :, :] = low.astype(BF)
+        out_ref[d, count * W32 :, :] = terms
 
 
 def features_kernel(q, nx, nh, nl, rows_ref, live_ref, got_ref, tiles_ref, gft_ref, gw_ref):
@@ -269,7 +256,7 @@
         total = total + nn(block.astype(BF), tiles_ref[0, s])
     gft_ref[...] = total.astype(BF)
     first = q * nh * W32
-    terms = got_ref[:, first : first + W32, :].astype(F32) + got_ref[:, first + W32 :, :].astype(F32)
+    terms = got_ref[:, first:, :].astype(F32)
     gw_ref[...] = jnp.sum(terms, axis=0) * (1.0 / math.sqrt(q * nx * nh * nl * B))
 
 
@@ -277,7 +264,7 @@
     q, nx = lax.axis_size("zh"), lax.axis_size("x")
     nh, nl = lax.axis_size("yh"), lax.axis_size("yl")
     xy, near, far = nx * nh * nl, nx * nl, q * nh
-    axes = (REP, "zh", COLUMN, "yh")
+    axes = (REP, "zh", COLUMN)
     place = jnp.stack([lax.axis_index(axis) for axis in axes]).astype(jnp.int32)
     shape = jax.ShapeDtypeStruct
     slots = 2 * pos_partner.shape[1]
@@ -292,16 +279,12 @@
     )(tile_rows, tile_live, features.T, tiles)
     near_recv = lax.all_to_all(sent.reshape(near, far * W32, B), NEAR, 0, 0, tiled=True)
 
-    far_part = call(
-        functools.partial(near_kernel, q),
-        [SMEM] + [VMEM] * 3,
-        shape((far, q * W32 + slots, B), BF),
-    )(place, near_recv, pos_t, neg_t)
-    recv = lax.all_to_all(far_part, FAR, 0, 0, tiled=True)
+    near_sum = call(near_kernel, [VMEM], shape((far * W32, B), BF))(near_recv)
+    recv = lax.all_to_all(near_sum.reshape(far, W32, B), FAR, 0, 0, tiled=True)
     own = call(
-        functools.partial(aggregate_kernel, q), [SMEM, VMEM], shape((q * (W32 + slots), B), BF)
-    )(place, recv)
-    blocks = lax.all_gather(own, REP, axis=0)
+        aggregate_kernel, [SMEM] + [VMEM] * 3, shape((q * q, W32 + slots, B), BF)
+    )(place, recv, pos_t, neg_t)
+    blocks = lax.all_to_all(own, ("zh",) + REP, 0, 0, tiled=True)
 
     nodes, agg, emb_t, slab_part = call(
         functools.partial(embed_kernel, q),
@@ -339,7 +322,7 @@
     far_part = call(functools.partial(owner_kernel, q), [VMEM], shape((far, height, B), BF))(mine)
     lines = lax.all_to_all(far_part, FAR, 0, 0, tiled=True)
     near_part = call(
-        functools.partial(merge_kernel, q), [VMEM], shape((near, (far + 2) * W32, B), BF)
+        functools.partial(merge_kernel, q), [VMEM], shape((near, (far + 1) * W32, B), BF)
     )(lines)
     every = lax.all_to_all(near_part, NEAR, 0, 0, tiled=True)
 

time: 153 us -> 148 us (0.967)
  blocking collectives: 90.6 us -> 81 us
  starting transfers between devices: 17 us -> 19.5 us
  waiting for transfers between devices: 23.1 us -> 25.4 us
    all_gather x1 -> x0, blocking collectives: 5.61 us -> none  [on_device(): blocks = lax.all_gather(own, REP, axis=0)]
    all_to_all x1, starting transfers between devices: 9.41 us -> 14.8 us  [on_device(): recv = lax.all_to_all(near_sum.reshape(far, W32, B), FAR, 0, 0, tiled=True)]
    all_to_all x1 -> x2, blocking collectives: 35.7 us -> 32.8 us  [the longest x1 20.1 us: on_device(): lax.all_to_all(sent.reshape(near, far * W32, B), NEAR, 0, 0, tiled=True)]
    all_to_all x1, starting transfers between devices: 7.55 us -> 4.75 us  [on_device(): slab = lax.all_to_all(slab_part, COLUMN, 0, 0, tiled=True)]
    all_to_all x1, waiting for transfers between devices: 10.9 us -> 12.7 us  [on_device(): recv = lax.all_to_all(near_sum.reshape(far, W32, B), FAR, 0, 0, tiled=True)]
where the time goes in v7:
time: 148 us; the launch traced here: 147 us
  blocking collectives  81 us (55%)
  waiting for transfers between devices  25.4 us (17%)
  starting transfers between devices  19.5 us (13%)
  Pallas kernels  17.2 us (12%)
  local copies, waits for them, and re-layouts  3.07 us (2%)
    all_to_all x1, blocking collectives, on_device(): lax.all_to_all(sent.reshape(near, far * W32, B), NEAR, 0, 0, tiled=True)  20.1 us
    all_to_all x1, blocking collectives, on_device(): every = lax.all_to_all(near_part, NEAR, 0, 0, tiled=True)  18.9 us
    all_to_all x1, blocking collectives, on_device(): lines = lax.all_to_all(far_part, FAR, 0, 0, tiled=True)  16.8 us
    all_to_all x1, starting transfers between devices, on_device(): recv = lax.all_to_all(near_sum.reshape(far, W32, B), FAR, 0, 0, tiled=True)  14.8 us
    all_to_all x1, waiting for transfers between devices, on_device(): slab = lax.all_to_all(slab_part, COLUMN, 0, 0, tiled=True)  12.8 us
    all_to_all x1, blocking collectives, on_device(): blocks = lax.all_to_all(own, ('zh',) + REP, 0, 0, tiled=True)  12.7 us
    all_to_all x1, waiting for transfers between devices, on_device(): recv = lax.all_to_all(near_sum.reshape(far, W32, B), FAR, 0, 0, tiled=True)  12.7 us
    all_to_all x1, blocking collectives, on_device(): mine = lax.all_to_all(pieces, ('zh',) + REP, 0, 0, tiled=True)  12.5 us
  transfers between devices with their start and end apart: 2, of which 2 were waited for; matrix products, arithmetic and copies ran while one was open for 0% of the time, Pallas kernels for 4%

profile of v7, /device:TPU:8, one launch (start us, length us, event | category | flops | bytes accessed | tf_op | source)
XLA Modules:
  0.0 147.1 jit_solution(16368700225882712508)
XLA Ops:
  0.6 0.0 copy-start
  0.6 1.0 copy-done
  1.7 0.0 copy-start.5
  1.7 0.7 copy-done.5
  2.4 0.0 copy-start.6
  2.4 0.7 copy-done.6
  3.0 0.0 copy-start.8
  3.0 0.7 copy-done.8
  3.7 1.0 shard_map.94
  4.7 20.1 %all_to_all.35.recv_ref = bf16[8,512,128]{2,1,0:T(8,128)(2,1)S(1)} all-to-all(bf16[8,512,128]{2,1,0:T(8,128)(2,1)S(1)} %bitcast.10), channel_id=1, replica_groups=mesh['zh'=4,'x'=4,'yh'=4,'yl'=2,'zl'=2,'core'=2] {'x','yl'}, dimensions={0} | all-to-all | bytes 2097152 | tf_op jit(solution)/shard_map/all_to_all | solution.py:280
  24.8 0.0 copy-start.3
  24.8 0.0 copy-start.4
  24.8 0.0 copy-start.2
  24.8 0.8 shard_map.95
  25.6 14.8 %all-to-all-start.1 = ((bf16[16,32,128]{2,1,0:T(8,128)(2,1)}), bf16[16,32,128]{2,1,0:T(8,128)(2,1)S(1)}, u32[]{:S(2)}, u32[]{:S(2)}) async-start(bf16[16,32,128]{2,1,0:T(8,128)(2,1)} %bitcast.5), calls=%async_computation.1 | async-start | bytes 262144 | tf_op jit(solution)/shard_map/all_to_all | solution.py:283
  40.4 0.1 pad_add_fusion.place_ref
  40.5 12.7 %all-to-all-done.1.recv_ref = bf16[16,32,128]{2,1,0:T(8,128)(2,1)S(1)} async-done(((bf16[16,32,128]{2,1,0:T(8,128)(2,1)}), bf16[16,32,128]{2,1,0:T(8,128)(2,1)S(1)}, u32[]{:S(2)}, u32[]{:S(2)}) %all-to-all-start.1) | async-done | bytes 131104 | tf_op jit(solution)/shard_map/all_to_all | solution.py:283
  53.1 0.0 copy-done.3
  53.1 0.0 copy-done.4
  53.1 0.6 shard_map.96
  53.7 12.7 %all_to_all.36.got_ref = bf16[16,48,128]{2,1,0:T(8,128)(2,1)S(1)} all-to-all(bf16[16,48,128]{2,1,0:T(8,128)(2,1)S(1)} %shard_map.96), channel_id=1, replica_groups=mesh['zh'=4,'x'=4,'yh'=4,'yl'=2,'zl'=2,'core'=2] {'zh','zl','core'}, dimensions={0} | all-to-all | bytes 393216 | tf_op jit(solution)/shard_map/all_to_all | solution.py:287
  66.4 0.0 copy-done.2
  66.4 1.7 %shard_map.97 = (bf16[512,128]{1,0:T(8,128)(2,1)S(1)}, bf16[4,128,128]{2,1,0:T(8,128)(2,1)S(1)}, bf16[32,128]{1,0:T(8,128)(2,1)}, bf16[32,64,128]{2,1,0:T(8,128)(2,1)}) custom-call(s32[3]{0:T(128)S(1)} %pad_add_fusion.place_ref, bf16[16,48,128]{2,1,0:T(8,128)(2,1)S(1)} %all_to_all.36.got_ref, bf16[128,128]{1,0:T(8,128)(2,1)S(1)} %copy-done.2, ...), custom_call_target="tpu_custom_call" | custom-call | flops 1000000 | bytes 1000000 | tf_op jit(solution)/shard_map/pallas_call | solution.py:289
  68.1 4.7 %all-to-all-start.3 = ((bf16[32,64,128]{2,1,0:T(8,128)(2,1)}), bf16[32,64,128]{2,1,0:T(8,128)(2,1)S(1)}, u32[]{:S(2)}, u32[]{:S(2)}) async-start(bf16[32,64,128]{2,1,0:T(8,128)(2,1)} %get-tuple-element.12), calls=%async_computation.3 | async-start | bytes 1048576 | tf_op jit(solution)/shard_map/all_to_all | solution.py:300
  72.9 6.0 %shard_map.98 = (bf16[8,512,128]{2,1,0:T(8,128)(2,1)S(1)}, bf16[8,512,128]{2,1,0:T(8,128)(2,1)S(1)}) custom-call(s32[3]{0:T(128)S(1)} %pad_add_fusion.place_ref, bf16[16,48,128]{2,1,0:T(8,128)(2,1)S(1)} %all_to_all.36.got_ref), custom_call_target="tpu_custom_call" | custom-call | flops 100000000 | bytes 1000000 | tf_op jit(solution)/shard_map/pallas_call | solution.py:301
  78.8 12.8 %all-to-all-done.3.got_ref = bf16[32,64,128]{2,1,0:T(8,128)(2,1)S(1)} async-done(((bf16[32,64,128]{2,1,0:T(8,128)(2,1)}), bf16[32,64,128]{2,1,0:T(8,128)(2,1)S(1)}, u32[]{:S(2)}, u32[]{:S(2)}) %all-to-all-start.3) | async-done | bytes 524320 | tf_op jit(solution)/shard_map/all_to_all | solution.py:300
  91.6 5.6 %shard_map.99 = bf16[16,48,128]{2,1,0:T(8,128)(2,1)S(1)} custom-call(s32[3]{0:T(128)S(1)} %pad_add_fusion.place_ref, bf16[32,64,128]{2,1,0:T(8,128)(2,1)S(1)} %all-to-all-done.3.got_ref, bf16[512,128]{1,0:T(8,128)(2,1)S(1)} %get-tuple-element.13.en_ref, bf16[4,128,128]{2,1,0:T(8,128)(2,1)S(1)} %get-tuple-element.14.agg_ref, bf16[128,128]{1,0:T(8,128)(2,1)S(1)} %copy-done.2, ...), custom_call_target="tpu_custom_call" | custom-call | flops 1000000 | bytes 1000000 | tf_op jit(solution)/shard_map/pallas_call | solution.py:309
  97.2 12.5 %all_to_all.37.got_ref = bf16[16,48,128]{2,1,0:T(8,128)(2,1)S(1)} all-to-all(bf16[16,48,128]{2,1,0:T(8,128)(2,1)S(1)} %shard_map.99), channel_id=1, replica_groups=mesh['zh'=4,'x'=4,'yh'=4,'yl'=2,'zl'=2,'core'=2] {'zh','zl','core'}, dimensions={0} | all-to-all | bytes 393216 | tf_op jit(solution)/shard_map/all_to_all | solution.py:319
  109.8 16.8 %all_to_all.38.got_ref = bf16[16,48,128]{2,1,0:T(8,128)(2,1)S(1)} all-to-all(bf16[16,48,128]{2,1,0:T(8,128)(2,1)S(1)} %shard_map.100), channel_id=1, replica_groups=mesh['zh'=4,'x'=4,'yh'=4,'yl'=2,'zl'=2,'core'=2] {'zh','yh'}, dimensions={0} | all-to-all | bytes 393216 | tf_op jit(solution)/shard_map/all_to_all | solution.py:323
  126.6 0.1 shard_map.101
  126.7 0.0 copy-start.1
  126.7 0.0 copy-start.7
  126.7 0.0 copy-start.9
  126.8 18.9 %all_to_all.39.got_ref = bf16[8,544,128]{2,1,0:T(8,128)(2,1)S(1)} all-to-all(bf16[8,544,128]{2,1,0:T(8,128)(2,1)S(1)} %shard_map.101), channel_id=1, replica_groups=mesh['zh'=4,'x'=4,'yh'=4,'yl'=2,'zl'=2,'core'=2] {'x','yl'}, dimensions={0} | all-to-all | bytes 2228224 | tf_op jit(solution)/shard_map/all_to_all | solution.py:327
  145.6 0.0 copy-done.1
  145.6 0.0 copy-done.7
  145.6 0.0 copy-done.9
  145.6 1.4 shard_map.102
  (1 shorter events, 0.0 us)
Async XLA Ops:
  0.6 1.0 copy-start
  1.7 0.7 copy-start.5
  2.4 0.7 copy-start.6
  3.0 0.7 copy-start.8
  24.8 28.3 %copy-start.3 = (s32[128,8]{0,1:T(8,128)S(1)}, s32[128,8]{0,1:T(8,128)}, u32[]{:S(2)}) copy-start(s32[128,8]{0,1:T(8,128)} %param.12) | copy-start | bytes 12292
  24.8 28.3 %copy-start.4 = (s32[128,8]{0,1:T(8,128)S(1)}, s32[128,8]{0,1:T(8,128)}, u32[]{:S(2)}) copy-start(s32[128,8]{0,1:T(8,128)} %param.13) | copy-start | bytes 12292
  24.8 41.6 %copy-start.2 = (bf16[128,128]{1,0:T(8,128)(2,1)S(1)}, bf16[128,128]{1,0:T(8,128)(2,1)}, u32[]{:S(2)}) copy-start(bf16[128,128]{1,0:T(8,128)(2,1)} %w_ref.3) | copy-start | bytes 98308
  25.6 27.5 %all-to-all-start.1 = ((bf16[16,32,128]{2,1,0:T(8,128)(2,1)}), bf16[16,32,128]{2,1,0:T(8,128)(2,1)S(1)}, u32[]{:S(2)}, u32[]{:S(2)}) async-start(bf16[16,32,128]{2,1,0:T(8,128)(2,1)} %bitcast.5), calls=%async_computation.1 | async-start | bytes 262144 | tf_op jit(solution)/shard_map/all_to_all | solution.py:283
  68.1 23.5 %all-to-all-start.3 = ((bf16[32,64,128]{2,1,0:T(8,128)(2,1)}), bf16[32,64,128]{2,1,0:T(8,128)(2,1)S(1)}, u32[]{:S(2)}, u32[]{:S(2)}) async-start(bf16[32,64,128]{2,1,0:T(8,128)(2,1)} %get-tuple-element.12), calls=%async_computation.3 | async-start | bytes 1048576 | tf_op jit(solution)/shard_map/all_to_all | solution.py:300
  126.7 18.9 %copy-start.1 = (bf16[1,16,128,128]{3,2,1,0:T(8,128)(2,1)S(1)}, bf16[1,16,128,128]{3,2,1,0:T(8,128)(2,1)}, u32[]{:S(2)}) copy-start(bf16[1,16,128,128]{3,2,1,0:T(8,128)(2,1)} %tiles_ref.3) | copy-start | bytes 1572868
  126.7 18.9 %copy-start.7 = (s32[1,16]{1,0:T(1,128)S(1)}, s32[1,16]{1,0:T(1,128)}, u32[]{:S(2)}) copy-start(s32[1,16]{1,0:T(1,128)} %rows_ref.3) | copy-start | bytes 196
  126.7 18.9 %copy-start.9 = (s32[1,16]{1,0:T(1,128)S(1)}, s32[1,16]{1,0:T(1,128)}, u32[]{:S(2)}) copy-start(s32[1,16]{1,0:T(1,128)} %live_ref.3) | copy-start | bytes 196

commit v8 on v7

--- a/solution.py
+++ b/solution.py
@@ -104,13 +104,14 @@
     nodes = nodes_ref[pl.ds(pl.multiple_of(plane * B + part * W32, W32), W32), :]
     ids = jnp.concatenate([pos_ref[...], neg_ref[...]], axis=0)
     block = lax.shift_right_logical(ids, 7)
-    table = jnp.concatenate([block, ids - block * B], axis=0).astype(F32)
-    lane = lax.broadcasted_iota(jnp.int32, table.shape, 1)
+    lane = lax.broadcasted_iota(jnp.int32, ids.shape, 1)
     first = part * W32
-    table = jnp.where((lane >= first) & (lane < first + W32), table, 0.0)
+    mine = (lane >= first) & (lane < first + W32)
+    blocks = jnp.where(mine, block, 0).astype(F32)
+    places = jnp.where(mine, ids - block * B, 0).astype(F32)
     quarters = B // W32
     turn = lax.rem(lax.rem(column, quarters) - part + quarters, quarters) * W32
-    partners = pltpu.roll(table, turn, 1).astype(BF)
+    partners = pltpu.roll(blocks + pltpu.roll(places, B // 2, 1), turn, 1).astype(BF)
     for d in range(send_ref.shape[0]):
         send_ref[d, 0:W32, :] = nodes
         send_ref[d, W32:, :] = partners
@@ -147,7 +148,7 @@
 
 def decoder_kernel(
     q, xy, slots, place_ref, got_ref, en_ref, agg_ref, w_ref, cpos_ref, ctot_ref,
-    out_ref, logit_s, high_s, low_s,
+    out_ref, logit_s, coef_s,
 ):
     pk = slots // 2
     column = place_ref[2]
@@ -162,16 +163,21 @@
     for g in range(groups):
         em = got_ref[g * quarters : (g + 1) * quarters, 0:W32, :].reshape(B, F)
         logit_s[g] = nt(en, em)
+    quarter = lax.div(lax.broadcasted_iota(jnp.int32, (slots, B), 1), W32)
     half = 0.5 / math.sqrt(F)
     one, zero = jnp.ones((tile, B), BF), jnp.zeros((tile, B), BF)
 
     def step(g, carry):
-        table = got_ref[g * quarters, W32:, :].astype(F32)
-        for j in range(1, quarters):
-            table = table + got_ref[g * quarters + j, W32:, :].astype(F32)
+        theirs = jnp.zeros((slots, B), F32)
+        places = jnp.zeros((slots, B), F32)
+        for j in range(quarters):
+            table = got_ref[g * quarters + j, W32:, :].astype(F32)
+            theirs = jnp.where(quarter == j, table, theirs)
+            places = jnp.where(quarter == (j + quarters // 2) % quarters, table, places)
+        places = pltpu.roll(places, B // 2, 1)
         for d in range(q):
             block = d * xy + column
-            code = jnp.where(table[:slots] == block.astype(F32), table[slots:], -1.0)
+            code = jnp.where(theirs == block.astype(F32), places, -1.0)
             wide = [
                 jnp.broadcast_to(code[k : k + 1], (tile, B)).astype(BF) for k in range(slots)
             ]
@@ -187,16 +193,14 @@
             cpos = (cpos_ref[g, rows, :] + jnp.concatenate(both, axis=0)).astype(F32)
             ctot = (ctot_ref[g, rows, :] + jnp.concatenate(ineg, axis=0)).astype(F32)
             sig = 0.5 * jnp.tanh(logit_s[g, rows, :] * half) + 0.5
-            high, low = split(ctot * sig - cpos)
-            high_s[g, rows, :] = high.astype(BF)
-            low_s[g, rows, :] = low.astype(BF)
+            coef_s[g, rows, :] = (ctot * sig - cpos).astype(BF)
         return carry
 
     lax.fori_loop(0, groups, step, 0)
     grad = jnp.zeros((q * B, F), F32)
     for g in range(groups):
         em = got_ref[g * quarters : (g + 1) * quarters, 0:W32, :].reshape(B, F)
-        grad = grad + nn(high_s[g], em) + nn(low_s[g], em)
+        grad = grad + nn(coef_s[g], em)
     high, low = split(grad * (1.0 / pk))
     high, low = high.astype(BF), low.astype(BF)
     grad_agg = nt(w_ref[...], high) + nt(w_ref[...], low)
@@ -244,16 +248,17 @@
 
 
 def features_kernel(q, nx, nh, nl, rows_ref, live_ref, got_ref, tiles_ref, gft_ref, gw_ref):
-    total = jnp.zeros((W32, B), F32)
-    for s in range(tiles_ref.shape[1]):
+    slots = tiles_ref.shape[1]
+    blocks = []
+    for s in range(slots):
         row = rows_ref[0, s]
         plane, column = lax.div(row, nx * nh * nl), lax.rem(row, nx * nh * nl)
         line, place = lax.div(column, nh * nl), lax.rem(column, nh * nl)
         near = line * nl + lax.rem(place, nl)
         first = pl.multiple_of((plane * nh + lax.div(place, nl)) * W32, W32)
         live = live_ref[0, s].astype(F32)
-        block = got_ref[near, pl.ds(first, W32), :].astype(F32) * live
-        total = total + nn(block.astype(BF), tiles_ref[0, s])
+        blocks.append((got_ref[near, pl.ds(first, W32), :].astype(F32) * live).astype(BF))
+    total = nn(jnp.concatenate(blocks, axis=1), tiles_ref[0].reshape(slots * B, B))
     gft_ref[...] = total.astype(BF)
     first = q * nh * W32
     terms = got_ref[:, first:, :].astype(F32)
@@ -293,7 +298,7 @@
             shape((q * B, F), BF),
             shape((q, F, B), BF),
             shape((W32, B), BF),
-            shape((xy, W32 + 2 * slots, B), BF),
+            shape((xy, W32 + slots, B), BF),
         ),
         [pltpu.VMEM((q, F, B), BF)],
     )(place, blocks, weight, pos_t, neg_t)
@@ -312,7 +317,6 @@
         shape((q * q, W32 + 2 * W32 // q, B), BF),
         [
             pltpu.VMEM((groups, q * B, B), F32),
-            pltpu.VMEM((groups, q * B, B), BF),
             pltpu.VMEM((groups, q * B, B), BF),
         ],
     )(place, slab, nodes, agg, weight, cpos, ctot)

time: 148 us -> 144 us (0.973)
  waiting for transfers between devices: 25.4 us -> 22.8 us
    all_to_all x1, waiting for transfers between devices: 12.8 us -> 10.1 us  [on_device(): slab = lax.all_to_all(slab_part, COLUMN, 0, 0, tiled=True)]
where the time goes in v8:
time: 144 us
  blocking collectives  80.7 us (56%)
  waiting for transfers between devices  22.8 us (16%)
  starting transfers between devices  19.5 us (14%)
  Pallas kernels  16.8 us (12%)
  local copies, waits for them, and re-layouts  3.07 us (2%)
    all_to_all x1, blocking collectives, on_device(): lax.all_to_all(sent.reshape(near, far * W32, B), NEAR, 0, 0, tiled=True)  20.1 us
    all_to_all x1, blocking collectives, on_device(): every = lax.all_to_all(near_part, NEAR, 0, 0, tiled=True)  18.7 us
    all_to_all x1, blocking collectives, on_device(): lines = lax.all_to_all(far_part, FAR, 0, 0, tiled=True)  16.8 us
    all_to_all x1, starting transfers between devices, on_device(): recv = lax.all_to_all(near_sum.reshape(far, W32, B), FAR, 0, 0, tiled=True)  14.8 us
    all_to_all x1, blocking collectives, on_device(): blocks = lax.all_to_all(own, ('zh',) + REP, 0, 0, tiled=True)  12.7 us
    all_to_all x1, waiting for transfers between devices, on_device(): recv = lax.all_to_all(near_sum.reshape(far, W32, B), FAR, 0, 0, tiled=True)  12.7 us
    all_to_all x1, blocking collectives, on_device(): mine = lax.all_to_all(pieces, ('zh',) + REP, 0, 0, tiled=True)  12.5 us
    all_to_all x1, waiting for transfers between devices, on_device(): slab = lax.all_to_all(slab_part, COLUMN, 0, 0, tiled=True)  10.1 us
  transfers between devices with their start and end apart: 2, of which 2 were waited for; matrix products, arithmetic and copies ran while one was open for 0% of the time, Pallas kernels for 4%

profile of v8, /device:TPU:8, one launch (start us, length us, event | category | flops | bytes accessed | tf_op | source)
XLA Modules:
  0.0 143.7 jit_solution(7263904410749931824)
XLA Ops:
  0.6 0.0 copy-start
  0.6 1.0 copy-done
  1.7 0.0 copy-start.5
  1.7 0.7 copy-done.5
  2.4 0.0 copy-start.6
  2.4 0.7 copy-done.6
  3.0 0.0 copy-start.8
  3.0 0.7 copy-done.8
  3.7 1.0 shard_map.94
  4.7 20.1 %all_to_all.35.recv_ref = bf16[8,512,128]{2,1,0:T(8,128)(2,1)S(1)} all-to-all(bf16[8,512,128]{2,1,0:T(8,128)(2,1)S(1)} %bitcast.10), channel_id=1, replica_groups=mesh['zh'=4,'x'=4,'yh'=4,'yl'=2,'zl'=2,'core'=2] {'x','yl'}, dimensions={0} | all-to-all | bytes 2097152 | tf_op jit(solution)/shard_map/all_to_all | solution.py:285
  24.8 0.0 copy-start.3
  24.8 0.0 copy-start.4
  24.8 0.0 copy-start.2
  24.8 0.8 shard_map.95
  25.6 14.8 %all-to-all-start.1 = ((bf16[16,32,128]{2,1,0:T(8,128)(2,1)}), bf16[16,32,128]{2,1,0:T(8,128)(2,1)S(1)}, u32[]{:S(2)}, u32[]{:S(2)}) async-start(bf16[16,32,128]{2,1,0:T(8,128)(2,1)} %bitcast.5), calls=%async_computation.1 | async-start | bytes 262144 | tf_op jit(solution)/shard_map/all_to_all | solution.py:288
  40.4 0.1 pad_add_fusion.place_ref
  40.5 12.7 %all-to-all-done.1.recv_ref = bf16[16,32,128]{2,1,0:T(8,128)(2,1)S(1)} async-done(((bf16[16,32,128]{2,1,0:T(8,128)(2,1)}), bf16[16,32,128]{2,1,0:T(8,128)(2,1)S(1)}, u32[]{:S(2)}, u32[]{:S(2)}) %all-to-all-start.1) | async-done | bytes 131104 | tf_op jit(solution)/shard_map/all_to_all | solution.py:288
  53.1 0.0 copy-done.3
  53.1 0.0 copy-done.4
  53.1 0.6 shard_map.96
  53.7 12.7 %all_to_all.36.got_ref = bf16[16,48,128]{2,1,0:T(8,128)(2,1)S(1)} all-to-all(bf16[16,48,128]{2,1,0:T(8,128)(2,1)S(1)} %shard_map.96), channel_id=1, replica_groups=mesh['zh'=4,'x'=4,'yh'=4,'yl'=2,'zl'=2,'core'=2] {'zh','zl','core'}, dimensions={0} | all-to-all | bytes 393216 | tf_op jit(solution)/shard_map/all_to_all | solution.py:292
  66.4 0.0 copy-done.2
  66.4 1.7 %shard_map.97 = (bf16[512,128]{1,0:T(8,128)(2,1)S(1)}, bf16[4,128,128]{2,1,0:T(8,128)(2,1)S(1)}, bf16[32,128]{1,0:T(8,128)(2,1)}, bf16[32,48,128]{2,1,0:T(8,128)(2,1)}) custom-call(s32[3]{0:T(128)S(1)} %pad_add_fusion.place_ref, bf16[16,48,128]{2,1,0:T(8,128)(2,1)S(1)} %all_to_all.36.got_ref, bf16[128,128]{1,0:T(8,128)(2,1)S(1)} %copy-done.2, ...), custom_call_target="tpu_custom_call" | custom-call | flops 1000000 | bytes 1000000 | tf_op jit(solution)/shard_map/pallas_call | solution.py:294
  68.1 4.7 %all-to-all-start.3 = ((bf16[32,48,128]{2,1,0:T(8,128)(2,1)}), bf16[32,48,128]{2,1,0:T(8,128)(2,1)S(1)}, u32[]{:S(2)}, u32[]{:S(2)}) async-start(bf16[32,48,128]{2,1,0:T(8,128)(2,1)} %get-tuple-element.12), calls=%async_computation.3 | async-start | bytes 786432 | tf_op jit(solution)/shard_map/all_to_all | solution.py:305
  72.8 6.0 %shard_map.98 = (bf16[8,512,128]{2,1,0:T(8,128)(2,1)S(1)}, bf16[8,512,128]{2,1,0:T(8,128)(2,1)S(1)}) custom-call(s32[3]{0:T(128)S(1)} %pad_add_fusion.place_ref, bf16[16,48,128]{2,1,0:T(8,128)(2,1)S(1)} %all_to_all.36.got_ref), custom_call_target="tpu_custom_call" | custom-call | flops 100000000 | bytes 1000000 | tf_op jit(solution)/shard_map/pallas_call | solution.py:306
  78.8 10.1 %all-to-all-done.3.got_ref = bf16[32,48,128]{2,1,0:T(8,128)(2,1)S(1)} async-done(((bf16[32,48,128]{2,1,0:T(8,128)(2,1)}), bf16[32,48,128]{2,1,0:T(8,128)(2,1)S(1)}, u32[]{:S(2)}, u32[]{:S(2)}) %all-to-all-start.3) | async-done | bytes 393248 | tf_op jit(solution)/shard_map/all_to_all | solution.py:305
  88.9 5.2 %shard_map.99 = bf16[16,48,128]{2,1,0:T(8,128)(2,1)S(1)} custom-call(s32[3]{0:T(128)S(1)} %pad_add_fusion.place_ref, bf16[32,48,128]{2,1,0:T(8,128)(2,1)S(1)} %all-to-all-done.3.got_ref, bf16[512,128]{1,0:T(8,128)(2,1)S(1)} %get-tuple-element.13.en_ref, bf16[4,128,128]{2,1,0:T(8,128)(2,1)S(1)} %get-tuple-element.14.agg_ref, bf16[128,128]{1,0:T(8,128)(2,1)S(1)} %copy-done.2, ...), custom_call_target="tpu_custom_call" | custom-call | flops 1000000 | bytes 1000000 | tf_op jit(solution)/shard_map/pallas_call | solution.py:314
  94.1 12.5 %all_to_all.37.got_ref = bf16[16,48,128]{2,1,0:T(8,128)(2,1)S(1)} all-to-all(bf16[16,48,128]{2,1,0:T(8,128)(2,1)S(1)} %shard_map.99), channel_id=1, replica_groups=mesh['zh'=4,'x'=4,'yh'=4,'yl'=2,'zl'=2,'core'=2] {'zh','zl','core'}, dimensions={0} | all-to-all | bytes 393216 | tf_op jit(solution)/shard_map/all_to_all | solution.py:323
  106.6 16.8 %all_to_all.38.got_ref = bf16[16,48,128]{2,1,0:T(8,128)(2,1)S(1)} all-to-all(bf16[16,48,128]{2,1,0:T(8,128)(2,1)S(1)} %shard_map.100), channel_id=1, replica_groups=mesh['zh'=4,'x'=4,'yh'=4,'yl'=2,'zl'=2,'core'=2] {'zh','yh'}, dimensions={0} | all-to-all | bytes 393216 | tf_op jit(solution)/shard_map/all_to_all | solution.py:327
  123.4 0.1 shard_map.101
  123.5 0.0 copy-start.1
  123.5 0.0 copy-start.7
  123.5 0.0 copy-start.9
  123.5 18.7 %all_to_all.39.got_ref = bf16[8,544,128]{2,1,0:T(8,128)(2,1)S(1)} all-to-all(bf16[8,544,128]{2,1,0:T(8,128)(2,1)S(1)} %shard_map.101), channel_id=1, replica_groups=mesh['zh'=4,'x'=4,'yh'=4,'yl'=2,'zl'=2,'core'=2] {'x','yl'}, dimensions={0} | all-to-all | bytes 2228224 | tf_op jit(solution)/shard_map/all_to_all | solution.py:331
  142.2 0.0 copy-done.1
  142.2 0.0 copy-done.7
  142.2 0.0 copy-done.9
  142.2 1.4 %shard_map.102 = (bf16[32,128]{1,0:T(8,128)(2,1)}, f32[32,128]{1,0:T(8,128)}) custom-call(s32[1,16]{1,0:T(1,128)S(1)} %copy-done.7, s32[1,16]{1,0:T(1,128)S(1)} %copy-done.9, bf16[8,544,128]{2,1,0:T(8,128)(2,1)S(1)} %all_to_all.39.got_ref, bf16[1,16,128,128]{3,2,1,0:T(8,128)(2,1)S(1)} %copy-done.1), custom_call_target="tpu_custom_call" | custom-call | flops 1000000 | bytes 1000000 | tf_op jit(solution)/shard_map/pallas_call | solution.py:333
  (1 shorter events, 0.0 us)
Async XLA Ops:
  0.6 1.0 copy-start
  1.7 0.7 copy-start.5
  2.4 0.7 copy-start.6
  3.0 0.7 copy-start.8
  24.8 28.3 %copy-start.3 = (s32[128,8]{0,1:T(8,128)S(1)}, s32[128,8]{0,1:T(8,128)}, u32[]{:S(2)}) copy-start(s32[128,8]{0,1:T(8,128)} %param.12) | copy-start | bytes 12292
  24.8 28.3 %copy-start.4 = (s32[128,8]{0,1:T(8,128)S(1)}, s32[128,8]{0,1:T(8,128)}, u32[]{:S(2)}) copy-start(s32[128,8]{0,1:T(8,128)} %param.13) | copy-start | bytes 12292
  24.8 41.6 %copy-start.2 = (bf16[128,128]{1,0:T(8,128)(2,1)S(1)}, bf16[128,128]{1,0:T(8,128)(2,1)}, u32[]{:S(2)}) copy-start(bf16[128,128]{1,0:T(8,128)(2,1)} %w_ref.3) | copy-start | bytes 98308
  25.6 27.5 %all-to-all-start.1 = ((bf16[16,32,128]{2,1,0:T(8,128)(2,1)}), bf16[16,32,128]{2,1,0:T(8,128)(2,1)S(1)}, u32[]{:S(2)}, u32[]{:S(2)}) async-start(bf16[16,32,128]{2,1,0:T(8,128)(2,1)} %bitcast.5), calls=%async_computation.1 | async-start | bytes 262144 | tf_op jit(solution)/shard_map/all_to_all | solution.py:288
  68.1 20.8 %all-to-all-start.3 = ((bf16[32,48,128]{2,1,0:T(8,128)(2,1)}), bf16[32,48,128]{2,1,0:T(8,128)(2,1)S(1)}, u32[]{:S(2)}, u32[]{:S(2)}) async-start(bf16[32,48,128]{2,1,0:T(8,128)(2,1)} %get-tuple-element.12), calls=%async_computation.3 | async-start | bytes 786432 | tf_op jit(solution)/shard_map/all_to_all | solution.py:305
  123.5 18.7 %copy-start.1 = (bf16[1,16,128,128]{3,2,1,0:T(8,128)(2,1)S(1)}, bf16[1,16,128,128]{3,2,1,0:T(8,128)(2,1)}, u32[]{:S(2)}) copy-start(bf16[1,16,128,128]{3,2,1,0:T(8,128)(2,1)} %tiles_ref.3) | copy-start | bytes 1572868
  123.5 18.7 %copy-start.7 = (s32[1,16]{1,0:T(1,128)S(1)}, s32[1,16]{1,0:T(1,128)}, u32[]{:S(2)}) copy-start(s32[1,16]{1,0:T(1,128)} %rows_ref.3) | copy-start | bytes 196
  123.5 18.7 %copy-start.9 = (s32[1,16]{1,0:T(1,128)S(1)}, s32[1,16]{1,0:T(1,128)}, u32[]{:S(2)}) copy-start(s32[1,16]{1,0:T(1,128)} %live_ref.3) | copy-start | bytes 196

commit v9 on v8

--- a/solution.py
+++ b/solution.py
@@ -35,7 +35,7 @@
     return lax.dot_general(a, b, (((1,), (0,)), ((), ())), preferred_element_type=F32)
 
 
-def call(body, in_specs, out_shape, scratch=(), flops=1000000, nbytes=1000000):
+def call(body, in_specs, out_shape, scratch=(), flops=1000000, nbytes=1000000, params=PARAMS):
     multi = isinstance(out_shape, (tuple, list))
     return pl.pallas_call(
         body,
@@ -43,7 +43,7 @@
         in_specs=in_specs,
         out_specs=[VMEM] * len(out_shape) if multi else VMEM,
         scratch_shapes=list(scratch),
-        compiler_params=PARAMS,
+        compiler_params=params,
         cost_estimate=pl.CostEstimate(flops=flops, bytes_accessed=nbytes, transcendentals=0),
     )
 
@@ -281,6 +281,7 @@
         [SMEM, SMEM, VMEM, VMEM],
         shape((near, far, W32, B), BF),
         [pltpu.VMEM((near, far, W32, B), F32)],
+        params=pltpu.CompilerParams(vmem_limit_bytes=60 * 1024 * 1024),
     )(tile_rows, tile_live, features.T, tiles)
     near_recv = lax.all_to_all(sent.reshape(near, far * W32, B), NEAR, 0, 0, tiled=True)
 

time: 144 us -> 143 us (level)
  local copies, waits for them, and re-layouts: 3.07 us -> 0.03 us
  Pallas kernels: 16.8 us -> 18.3 us
    unnamed x20 -> x12, local copies, waits for them, and re-layouts: 3.07 us -> 0.03 us
    pallas_call x1, Pallas kernels: 1 us -> 2.51 us  [on_device(): call(functools.partial(products_kernel, nx, nh, nl), [SMEM, SMEM, VMEM, V...]
where the time goes in v9:
time: 143 us; the launch traced here: 142 us
  blocking collectives  80.9 us (57%)
  waiting for transfers between devices  22.8 us (16%)
  starting transfers between devices  19.5 us (14%)
  Pallas kernels  18.3 us (13%)
    all_to_all x1, blocking collectives, on_device(): lax.all_to_all(sent.reshape(near, far * W32, B), NEAR, 0, 0, tiled=True)  20.3 us
    all_to_all x1, blocking collectives, on_device(): every = lax.all_to_all(near_part, NEAR, 0, 0, tiled=True)  18.7 us
    all_to_all x1, blocking collectives, on_device(): lines = lax.all_to_all(far_part, FAR, 0, 0, tiled=True)  16.8 us
    all_to_all x1, starting transfers between devices, on_device(): recv = lax.all_to_all(near_sum.reshape(far, W32, B), FAR, 0, 0, tiled=True)  14.8 us
    all_to_all x1, blocking collectives, on_device(): blocks = lax.all_to_all(own, ('zh',) + REP, 0, 0, tiled=True)  12.7 us
    all_to_all x1, waiting for transfers between devices, on_device(): recv = lax.all_to_all(near_sum.reshape(far, W32, B), FAR, 0, 0, tiled=True)  12.7 us
    all_to_all x1, blocking collectives, on_device(): mine = lax.all_to_all(pieces, ('zh',) + REP, 0, 0, tiled=True)  12.5 us
    all_to_all x1, waiting for transfers between devices, on_device(): slab = lax.all_to_all(slab_part, COLUMN, 0, 0, tiled=True)  10.1 us
  transfers between devices with their start and end apart: 2, of which 2 were waited for; matrix products, arithmetic and copies ran while one was open for 0% of the time, Pallas kernels for 4%

profile of v9, /device:TPU:8, one launch (start us, length us, event | category | flops | bytes accessed | tf_op | source)
XLA Modules:
  0.0 142.3 jit_solution(7844100152023999815)
XLA Ops:
  0.6 2.5 %shard_map.94 = bf16[8,16,32,128]{3,2,1,0:T(8,128)(2,1)} custom-call(s32[1,16]{1,0:T(1,128)} %rows_ref.3, s32[1,16]{1,0:T(1,128)} %live_ref.3, bf16[32,128]{1,0:T(8,128)(2,1)} %bitcast.15, bf16[1,16,128,128]{3,2,1,0:T(8,128)(2,1)} %tiles_ref.3), custom_call_target="tpu_custom_call" | custom-call | flops 1000000 | bytes 1000000 | tf_op jit(solution)/shard_map/pallas_call | solution.py:279
  3.1 20.3 %all_to_all.35.recv_ref = bf16[8,512,128]{2,1,0:T(8,128)(2,1)S(1)} all-to-all(bf16[8,512,128]{2,1,0:T(8,128)(2,1)} %bitcast.14), channel_id=1, replica_groups=mesh['zh'=4,'x'=4,'yh'=4,'yl'=2,'zl'=2,'core'=2] {'x','yl'}, dimensions={0} | all-to-all | bytes 2097152 | tf_op jit(solution)/shard_map/all_to_all | solution.py:286
  23.4 0.0 copy-start.2
  23.4 0.0 copy-start.3
  23.4 0.0 copy-start.1
  23.4 0.8 shard_map.95
  24.2 14.8 %all-to-all-start.1 = ((bf16[16,32,128]{2,1,0:T(8,128)(2,1)}), bf16[16,32,128]{2,1,0:T(8,128)(2,1)S(1)}, u32[]{:S(2)}, u32[]{:S(2)}) async-start(bf16[16,32,128]{2,1,0:T(8,128)(2,1)} %bitcast.5), calls=%async_computation.1 | async-start | bytes 262144 | tf_op jit(solution)/shard_map/all_to_all | solution.py:289
  39.0 0.1 pad_add_fusion.place_ref
  39.1 12.7 %all-to-all-done.1.recv_ref = bf16[16,32,128]{2,1,0:T(8,128)(2,1)S(1)} async-done(((bf16[16,32,128]{2,1,0:T(8,128)(2,1)}), bf16[16,32,128]{2,1,0:T(8,128)(2,1)S(1)}, u32[]{:S(2)}, u32[]{:S(2)}) %all-to-all-start.1) | async-done | bytes 131104 | tf_op jit(solution)/shard_map/all_to_all | solution.py:289
  51.7 0.0 copy-done.2
  51.8 0.0 copy-done.3
  51.8 0.6 shard_map.96
  52.3 12.7 %all_to_all.36.got_ref = bf16[16,48,128]{2,1,0:T(8,128)(2,1)S(1)} all-to-all(bf16[16,48,128]{2,1,0:T(8,128)(2,1)S(1)} %shard_map.96), channel_id=1, replica_groups=mesh['zh'=4,'x'=4,'yh'=4,'yl'=2,'zl'=2,'core'=2] {'zh','zl','core'}, dimensions={0} | all-to-all | bytes 393216 | tf_op jit(solution)/shard_map/all_to_all | solution.py:293
  65.0 0.0 copy-done.1
  65.0 1.7 %shard_map.97 = (bf16[512,128]{1,0:T(8,128)(2,1)S(1)}, bf16[4,128,128]{2,1,0:T(8,128)(2,1)S(1)}, bf16[32,128]{1,0:T(8,128)(2,1)}, bf16[32,48,128]{2,1,0:T(8,128)(2,1)}) custom-call(s32[3]{0:T(128)S(1)} %pad_add_fusion.place_ref, bf16[16,48,128]{2,1,0:T(8,128)(2,1)S(1)} %all_to_all.36.got_ref, bf16[128,128]{1,0:T(8,128)(2,1)S(1)} %copy-done.1, ...), custom_call_target="tpu_custom_call" | custom-call | flops 1000000 | bytes 1000000 | tf_op jit(solution)/shard_map/pallas_call | solution.py:295
  66.7 4.7 %all-to-all-start.3 = ((bf16[32,48,128]{2,1,0:T(8,128)(2,1)}), bf16[32,48,128]{2,1,0:T(8,128)(2,1)S(1)}, u32[]{:S(2)}, u32[]{:S(2)}) async-start(bf16[32,48,128]{2,1,0:T(8,128)(2,1)} %get-tuple-element.12), calls=%async_computation.3 | async-start | bytes 786432 | tf_op jit(solution)/shard_map/all_to_all | solution.py:306
  71.5 6.0 %shard_map.98 = (bf16[8,512,128]{2,1,0:T(8,128)(2,1)S(1)}, bf16[8,512,128]{2,1,0:T(8,128)(2,1)S(1)}) custom-call(s32[3]{0:T(128)S(1)} %pad_add_fusion.place_ref, bf16[16,48,128]{2,1,0:T(8,128)(2,1)S(1)} %all_to_all.36.got_ref), custom_call_target="tpu_custom_call" | custom-call | flops 100000000 | bytes 1000000 | tf_op jit(solution)/shard_map/pallas_call | solution.py:307
  77.4 10.1 %all-to-all-done.3.got_ref = bf16[32,48,128]{2,1,0:T(8,128)(2,1)S(1)} async-done(((bf16[32,48,128]{2,1,0:T(8,128)(2,1)}), bf16[32,48,128]{2,1,0:T(8,128)(2,1)S(1)}, u32[]{:S(2)}, u32[]{:S(2)}) %all-to-all-start.3) | async-done | bytes 393248 | tf_op jit(solution)/shard_map/all_to_all | solution.py:306
  87.5 5.2 %shard_map.99 = bf16[16,48,128]{2,1,0:T(8,128)(2,1)S(1)} custom-call(s32[3]{0:T(128)S(1)} %pad_add_fusion.place_ref, bf16[32,48,128]{2,1,0:T(8,128)(2,1)S(1)} %all-to-all-done.3.got_ref, bf16[512,128]{1,0:T(8,128)(2,1)S(1)} %get-tuple-element.13.en_ref, bf16[4,128,128]{2,1,0:T(8,128)(2,1)S(1)} %get-tuple-element.14.agg_ref, bf16[128,128]{1,0:T(8,128)(2,1)S(1)} %copy-done.1, ...), custom_call_target="tpu_custom_call" | custom-call | flops 1000000 | bytes 1000000 | tf_op jit(solution)/shard_map/pallas_call | solution.py:315
  92.7 12.5 %all_to_all.37.got_ref = bf16[16,48,128]{2,1,0:T(8,128)(2,1)S(1)} all-to-all(bf16[16,48,128]{2,1,0:T(8,128)(2,1)S(1)} %shard_map.99), channel_id=1, replica_groups=mesh['zh'=4,'x'=4,'yh'=4,'yl'=2,'zl'=2,'core'=2] {'zh','zl','core'}, dimensions={0} | all-to-all | bytes 393216 | tf_op jit(solution)/shard_map/all_to_all | solution.py:324
  105.2 16.8 %all_to_all.38.got_ref = bf16[16,48,128]{2,1,0:T(8,128)(2,1)S(1)} all-to-all(bf16[16,48,128]{2,1,0:T(8,128)(2,1)S(1)} %shard_map.100), channel_id=1, replica_groups=mesh['zh'=4,'x'=4,'yh'=4,'yl'=2,'zl'=2,'core'=2] {'zh','yh'}, dimensions={0} | all-to-all | bytes 393216 | tf_op jit(solution)/shard_map/all_to_all | solution.py:328
  122.0 0.1 shard_map.101
  122.1 0.0 copy-start
  122.1 0.0 copy-start.4
  122.1 0.0 copy-start.5
  122.1 18.7 %all_to_all.39.got_ref = bf16[8,544,128]{2,1,0:T(8,128)(2,1)S(1)} all-to-all(bf16[8,544,128]{2,1,0:T(8,128)(2,1)S(1)} %shard_map.101), channel_id=1, replica_groups=mesh['zh'=4,'x'=4,'yh'=4,'yl'=2,'zl'=2,'core'=2] {'x','yl'}, dimensions={0} | all-to-all | bytes 2228224 | tf_op jit(solution)/shard_map/all_to_all | solution.py:332
  140.8 0.0 copy-done
  140.8 0.0 copy-done.4
  140.8 0.0 copy-done.5
  140.9 1.4 %shard_map.102 = (bf16[32,128]{1,0:T(8,128)(2,1)}, f32[32,128]{1,0:T(8,128)}) custom-call(s32[1,16]{1,0:T(1,128)S(1)} %copy-done.4, s32[1,16]{1,0:T(1,128)S(1)} %copy-done.5, bf16[8,544,128]{2,1,0:T(8,128)(2,1)S(1)} %all_to_all.39.got_ref, bf16[1,16,128,128]{3,2,1,0:T(8,128)(2,1)S(1)} %copy-done), custom_call_target="tpu_custom_call" | custom-call | flops 1000000 | bytes 1000000 | tf_op jit(solution)/shard_map/pallas_call | solution.py:334
  (1 shorter events, 0.0 us)
Async XLA Ops:
  23.4 28.3 %copy-start.2 = (s32[128,8]{0,1:T(8,128)S(1)}, s32[128,8]{0,1:T(8,128)}, u32[]{:S(2)}) copy-start(s32[128,8]{0,1:T(8,128)} %param.12) | copy-start | bytes 12292
  23.4 28.3 %copy-start.3 = (s32[128,8]{0,1:T(8,128)S(1)}, s32[128,8]{0,1:T(8,128)}, u32[]{:S(2)}) copy-start(s32[128,8]{0,1:T(8,128)} %param.13) | copy-start | bytes 12292
  23.4 41.6 %copy-start.1 = (bf16[128,128]{1,0:T(8,128)(2,1)S(1)}, bf16[128,128]{1,0:T(8,128)(2,1)}, u32[]{:S(2)}) copy-start(bf16[128,128]{1,0:T(8,128)(2,1)} %w_ref.3) | copy-start | bytes 98308
  24.2 27.5 %all-to-all-start.1 = ((bf16[16,32,128]{2,1,0:T(8,128)(2,1)}), bf16[16,32,128]{2,1,0:T(8,128)(2,1)S(1)}, u32[]{:S(2)}, u32[]{:S(2)}) async-start(bf16[16,32,128]{2,1,0:T(8,128)(2,1)} %bitcast.5), calls=%async_computation.1 | async-start | bytes 262144 | tf_op jit(solution)/shard_map/all_to_all | solution.py:289
  66.7 20.8 %all-to-all-start.3 = ((bf16[32,48,128]{2,1,0:T(8,128)(2,1)}), bf16[32,48,128]{2,1,0:T(8,128)(2,1)S(1)}, u32[]{:S(2)}, u32[]{:S(2)}) async-start(bf16[32,48,128]{2,1,0:T(8,128)(2,1)} %get-tuple-element.12), calls=%async_computation.3 | async-start | bytes 786432 | tf_op jit(solution)/shard_map/all_to_all | solution.py:306
  122.1 18.7 %copy-start = (bf16[1,16,128,128]{3,2,1,0:T(8,128)(2,1)S(1)}, bf16[1,16,128,128]{3,2,1,0:T(8,128)(2,1)}, u32[]{:S(2)}) copy-start(bf16[1,16,128,128]{3,2,1,0:T(8,128)(2,1)} %tiles_ref.3) | copy-start | bytes 1572868
  122.1 18.7 %copy-start.4 = (s32[1,16]{1,0:T(1,128)S(1)}, s32[1,16]{1,0:T(1,128)}, u32[]{:S(2)}) copy-start(s32[1,16]{1,0:T(1,128)} %rows_ref.3) | copy-start | bytes 196
  122.1 18.7 %copy-start.5 = (s32[1,16]{1,0:T(1,128)S(1)}, s32[1,16]{1,0:T(1,128)}, u32[]{:S(2)}) copy-start(s32[1,16]{1,0:T(1,128)} %live_ref.3) | copy-start | bytes 196

commit v10 on v9

--- a/solution.py
+++ b/solution.py
@@ -201,13 +201,12 @@
     for g in range(groups):
         em = got_ref[g * quarters : (g + 1) * quarters, 0:W32, :].reshape(B, F)
         grad = grad + nn(coef_s[g], em)
-    high, low = split(grad * (1.0 / pk))
-    high, low = high.astype(BF), low.astype(BF)
-    grad_agg = nt(w_ref[...], high) + nt(w_ref[...], low)
+    grad = (grad * (1.0 / pk)).astype(BF)
+    grad_agg = nt(w_ref[...], grad)
     terms = jnp.zeros((F, F), F32)
     for d in range(q):
         rows = slice(d * B, (d + 1) * B)
-        terms = terms + nn(agg_ref[d], high[rows]) + nn(agg_ref[d], low[rows])
+        terms = terms + nn(agg_ref[d], grad[rows])
     thigh, tlow = split(terms)
     eighth = W32 // q
     for z in range(q):

time: 143 us -> 143 us (level)
  no operation moved by 1% of the time
where the time goes in v10:
time: 143 us; the launch traced here: 142 us
  blocking collectives  81.1 us (57%)
  waiting for transfers between devices  22.8 us (16%)
  starting transfers between devices  19.5 us (14%)
  Pallas kernels  18.2 us (13%)
    all_to_all x1, blocking collectives, on_device(): lax.all_to_all(sent.reshape(near, far * W32, B), NEAR, 0, 0, tiled=True)  20.3 us
    all_to_all x1, blocking collectives, on_device(): every = lax.all_to_all(near_part, NEAR, 0, 0, tiled=True)  18.9 us
    all_to_all x1, blocking collectives, on_device(): lines = lax.all_to_all(far_part, FAR, 0, 0, tiled=True)  16.8 us
    all_to_all x1, starting transfers between devices, on_device(): recv = lax.all_to_all(near_sum.reshape(far, W32, B), FAR, 0, 0, tiled=True)  14.8 us
    all_to_all x1, blocking collectives, on_device(): blocks = lax.all_to_all(own, ('zh',) + REP, 0, 0, tiled=True)  12.7 us
    all_to_all x1, waiting for transfers between devices, on_device(): recv = lax.all_to_all(near_sum.reshape(far, W32, B), FAR, 0, 0, tiled=True)  12.7 us
    all_to_all x1, blocking collectives, on_device(): mine = lax.all_to_all(pieces, ('zh',) + REP, 0, 0, tiled=True)  12.5 us
    all_to_all x1, waiting for transfers between devices, on_device(): slab = lax.all_to_all(slab_part, COLUMN, 0, 0, tiled=True)  10.1 us
  transfers between devices with their start and end apart: 2, of which 2 were waited for; matrix products, arithmetic and copies ran while one was open for 0% of the time, Pallas kernels for 4%

profile of v10, /device:TPU:8, one launch (start us, length us, event | category | flops | bytes accessed | tf_op | source)
XLA Modules:
  0.0 142.5 jit_solution(6073246312757117644)
XLA Ops:
  0.6 2.5 %shard_map.94 = bf16[8,16,32,128]{3,2,1,0:T(8,128)(2,1)} custom-call(s32[1,16]{1,0:T(1,128)} %rows_ref.3, s32[1,16]{1,0:T(1,128)} %live_ref.3, bf16[32,128]{1,0:T(8,128)(2,1)} %bitcast.15, bf16[1,16,128,128]{3,2,1,0:T(8,128)(2,1)} %tiles_ref.3), custom_call_target="tpu_custom_call" | custom-call | flops 1000000 | bytes 1000000 | tf_op jit(solution)/shard_map/pallas_call | solution.py:278
  3.1 20.3 %all_to_all.35.recv_ref = bf16[8,512,128]{2,1,0:T(8,128)(2,1)S(1)} all-to-all(bf16[8,512,128]{2,1,0:T(8,128)(2,1)} %bitcast.14), channel_id=1, replica_groups=mesh['zh'=4,'x'=4,'yh'=4,'yl'=2,'zl'=2,'core'=2] {'x','yl'}, dimensions={0} | all-to-all | bytes 2097152 | tf_op jit(solution)/shard_map/all_to_all | solution.py:285
  23.4 0.0 copy-start.2
  23.4 0.0 copy-start.3
  23.4 0.0 copy-start.1
  23.4 0.8 shard_map.95
  24.2 14.8 %all-to-all-start.1 = ((bf16[16,32,128]{2,1,0:T(8,128)(2,1)}), bf16[16,32,128]{2,1,0:T(8,128)(2,1)S(1)}, u32[]{:S(2)}, u32[]{:S(2)}) async-start(bf16[16,32,128]{2,1,0:T(8,128)(2,1)} %bitcast.5), calls=%async_computation.1 | async-start | bytes 262144 | tf_op jit(solution)/shard_map/all_to_all | solution.py:288
  39.0 0.1 pad_add_fusion.place_ref
  39.1 12.7 %all-to-all-done.1.recv_ref = bf16[16,32,128]{2,1,0:T(8,128)(2,1)S(1)} async-done(((bf16[16,32,128]{2,1,0:T(8,128)(2,1)}), bf16[16,32,128]{2,1,0:T(8,128)(2,1)S(1)}, u32[]{:S(2)}, u32[]{:S(2)}) %all-to-all-start.1) | async-done | bytes 131104 | tf_op jit(solution)/shard_map/all_to_all | solution.py:288
  51.7 0.0 copy-done.2
  51.8 0.0 copy-done.3
  51.8 0.6 shard_map.96
  52.3 12.7 %all_to_all.36.got_ref = bf16[16,48,128]{2,1,0:T(8,128)(2,1)S(1)} all-to-all(bf16[16,48,128]{2,1,0:T(8,128)(2,1)S(1)} %shard_map.96), channel_id=1, replica_groups=mesh['zh'=4,'x'=4,'yh'=4,'yl'=2,'zl'=2,'core'=2] {'zh','zl','core'}, dimensions={0} | all-to-all | bytes 393216 | tf_op jit(solution)/shard_map/all_to_all | solution.py:292
  65.0 0.0 copy-done.1
  65.0 1.7 %shard_map.97 = (bf16[512,128]{1,0:T(8,128)(2,1)S(1)}, bf16[4,128,128]{2,1,0:T(8,128)(2,1)S(1)}, bf16[32,128]{1,0:T(8,128)(2,1)}, bf16[32,48,128]{2,1,0:T(8,128)(2,1)}) custom-call(s32[3]{0:T(128)S(1)} %pad_add_fusion.place_ref, bf16[16,48,128]{2,1,0:T(8,128)(2,1)S(1)} %all_to_all.36.got_ref, bf16[128,128]{1,0:T(8,128)(2,1)S(1)} %copy-done.1, ...), custom_call_target="tpu_custom_call" | custom-call | flops 1000000 | bytes 1000000 | tf_op jit(solution)/shard_map/pallas_call | solution.py:294
  66.7 4.7 %all-to-all-start.3 = ((bf16[32,48,128]{2,1,0:T(8,128)(2,1)}), bf16[32,48,128]{2,1,0:T(8,128)(2,1)S(1)}, u32[]{:S(2)}, u32[]{:S(2)}) async-start(bf16[32,48,128]{2,1,0:T(8,128)(2,1)} %get-tuple-element.12), calls=%async_computation.3 | async-start | bytes 786432 | tf_op jit(solution)/shard_map/all_to_all | solution.py:305
  71.5 6.0 %shard_map.98 = (bf16[8,512,128]{2,1,0:T(8,128)(2,1)S(1)}, bf16[8,512,128]{2,1,0:T(8,128)(2,1)S(1)}) custom-call(s32[3]{0:T(128)S(1)} %pad_add_fusion.place_ref, bf16[16,48,128]{2,1,0:T(8,128)(2,1)S(1)} %all_to_all.36.got_ref), custom_call_target="tpu_custom_call" | custom-call | flops 100000000 | bytes 1000000 | tf_op jit(solution)/shard_map/pallas_call | solution.py:306
  77.4 10.1 %all-to-all-done.3.got_ref = bf16[32,48,128]{2,1,0:T(8,128)(2,1)S(1)} async-done(((bf16[32,48,128]{2,1,0:T(8,128)(2,1)}), bf16[32,48,128]{2,1,0:T(8,128)(2,1)S(1)}, u32[]{:S(2)}, u32[]{:S(2)}) %all-to-all-start.3) | async-done | bytes 393248 | tf_op jit(solution)/shard_map/all_to_all | solution.py:305
  87.5 5.1 %shard_map.99 = bf16[16,48,128]{2,1,0:T(8,128)(2,1)S(1)} custom-call(s32[3]{0:T(128)S(1)} %pad_add_fusion.place_ref, bf16[32,48,128]{2,1,0:T(8,128)(2,1)S(1)} %all-to-all-done.3.got_ref, bf16[512,128]{1,0:T(8,128)(2,1)S(1)} %get-tuple-element.13.en_ref, bf16[4,128,128]{2,1,0:T(8,128)(2,1)S(1)} %get-tuple-element.14.agg_ref, bf16[128,128]{1,0:T(8,128)(2,1)S(1)} %copy-done.1, ...), custom_call_target="tpu_custom_call" | custom-call | flops 1000000 | bytes 1000000 | tf_op jit(solution)/shard_map/pallas_call | solution.py:314
  92.6 12.5 %all_to_all.37.got_ref = bf16[16,48,128]{2,1,0:T(8,128)(2,1)S(1)} all-to-all(bf16[16,48,128]{2,1,0:T(8,128)(2,1)S(1)} %shard_map.99), channel_id=1, replica_groups=mesh['zh'=4,'x'=4,'yh'=4,'yl'=2,'zl'=2,'core'=2] {'zh','zl','core'}, dimensions={0} | all-to-all | bytes 393216 | tf_op jit(solution)/shard_map/all_to_all | solution.py:323
  105.1 16.8 %all_to_all.38.got_ref = bf16[16,48,128]{2,1,0:T(8,128)(2,1)S(1)} all-to-all(bf16[16,48,128]{2,1,0:T(8,128)(2,1)S(1)} %shard_map.100), channel_id=1, replica_groups=mesh['zh'=4,'x'=4,'yh'=4,'yl'=2,'zl'=2,'core'=2] {'zh','yh'}, dimensions={0} | all-to-all | bytes 393216 | tf_op jit(solution)/shard_map/all_to_all | solution.py:327
  121.9 0.1 shard_map.101
  122.0 0.0 copy-start
  122.0 0.0 copy-start.4
  122.1 0.0 copy-start.5
  122.1 18.9 %all_to_all.39.got_ref = bf16[8,544,128]{2,1,0:T(8,128)(2,1)S(1)} all-to-all(bf16[8,544,128]{2,1,0:T(8,128)(2,1)S(1)} %shard_map.101), channel_id=1, replica_groups=mesh['zh'=4,'x'=4,'yh'=4,'yl'=2,'zl'=2,'core'=2] {'x','yl'}, dimensions={0} | all-to-all | bytes 2228224 | tf_op jit(solution)/shard_map/all_to_all | solution.py:331
  141.0 0.0 copy-done
  141.0 0.0 copy-done.4
  141.0 0.0 copy-done.5
  141.0 1.4 %shard_map.102 = (bf16[32,128]{1,0:T(8,128)(2,1)}, f32[32,128]{1,0:T(8,128)}) custom-call(s32[1,16]{1,0:T(1,128)S(1)} %copy-done.4, s32[1,16]{1,0:T(1,128)S(1)} %copy-done.5, bf16[8,544,128]{2,1,0:T(8,128)(2,1)S(1)} %all_to_all.39.got_ref, bf16[1,16,128,128]{3,2,1,0:T(8,128)(2,1)S(1)} %copy-done), custom_call_target="tpu_custom_call" | custom-call | flops 1000000 | bytes 1000000 | tf_op jit(solution)/shard_map/pallas_call | solution.py:333
  (1 shorter events, 0.0 us)
Async XLA Ops:
  23.4 28.3 %copy-start.2 = (s32[128,8]{0,1:T(8,128)S(1)}, s32[128,8]{0,1:T(8,128)}, u32[]{:S(2)}) copy-start(s32[128,8]{0,1:T(8,128)} %param.12) | copy-start | bytes 12292
  23.4 28.3 %copy-start.3 = (s32[128,8]{0,1:T(8,128)S(1)}, s32[128,8]{0,1:T(8,128)}, u32[]{:S(2)}) copy-start(s32[128,8]{0,1:T(8,128)} %param.13) | copy-start | bytes 12292
  23.4 41.6 %copy-start.1 = (bf16[128,128]{1,0:T(8,128)(2,1)S(1)}, bf16[128,128]{1,0:T(8,128)(2,1)}, u32[]{:S(2)}) copy-start(bf16[128,128]{1,0:T(8,128)(2,1)} %w_ref.3) | copy-start | bytes 98308
  24.2 27.5 %all-to-all-start.1 = ((bf16[16,32,128]{2,1,0:T(8,128)(2,1)}), bf16[16,32,128]{2,1,0:T(8,128)(2,1)S(1)}, u32[]{:S(2)}, u32[]{:S(2)}) async-start(bf16[16,32,128]{2,1,0:T(8,128)(2,1)} %bitcast.5), calls=%async_computation.1 | async-start | bytes 262144 | tf_op jit(solution)/shard_map/all_to_all | solution.py:288
  66.7 20.8 %all-to-all-start.3 = ((bf16[32,48,128]{2,1,0:T(8,128)(2,1)}), bf16[32,48,128]{2,1,0:T(8,128)(2,1)S(1)}, u32[]{:S(2)}, u32[]{:S(2)}) async-start(bf16[32,48,128]{2,1,0:T(8,128)(2,1)} %get-tuple-element.12), calls=%async_computation.3 | async-start | bytes 786432 | tf_op jit(solution)/shard_map/all_to_all | solution.py:305
  122.0 19.0 %copy-start = (bf16[1,16,128,128]{3,2,1,0:T(8,128)(2,1)S(1)}, bf16[1,16,128,128]{3,2,1,0:T(8,128)(2,1)}, u32[]{:S(2)}) copy-start(bf16[1,16,128,128]{3,2,1,0:T(8,128)(2,1)} %tiles_ref.3) | copy-start | bytes 1572868
  122.0 19.0 %copy-start.4 = (s32[1,16]{1,0:T(1,128)S(1)}, s32[1,16]{1,0:T(1,128)}, u32[]{:S(2)}) copy-start(s32[1,16]{1,0:T(1,128)} %rows_ref.3) | copy-start | bytes 196
  122.1 19.0 %copy-start.5 = (s32[1,16]{1,0:T(1,128)S(1)}, s32[1,16]{1,0:T(1,128)}, u32[]{:S(2)}) copy-start(s32[1,16]{1,0:T(1,128)} %live_ref.3) | copy-start | bytes 196
